TPU v7x, 256 devices: a whole 4x4x8 slice. The times are simulated.
256 devices in a mesh: grp: 4 (over y), blk: 64 (over z, x, core).
Axes of the slice: x: 4, y: 4, z: 8, core: 2. Of those that a mesh axis runs over, the one named last changes fastest.
Arguments:
- coeffs: bfloat16 [2, 2048, 1024], P(None, ('grp', 'blk')), may hold values from -6 to 6
- coupling: int32 [4, 4], replicated, may hold values from -1 to 1, as said below
- one_body: float32 [4, 4, 2, 64, 64], P('grp', None, None, 'blk'), may hold values from -0.125 to 0.125
- target_orb: int32 [131072], P(('grp', 'blk')), may hold values from 0 to 63
- source_orb: int32 [2048], replicated, may hold values from 0 to 63
- excite: int32 [131072, 2048], P(('grp', 'blk')), may hold values from -1 to 1
- live_rows: int32 [256], P(('grp', 'blk')), may hold values from 1 to 512, 98304 in all
Outputs:
- sigma: float32 [2, 131072, 1024], P(None, ('grp', 'blk'))
Inputs may be any that keep to these rules, and one draw needn't show every extreme that they name: `coupling`: Symmetric, with ones on the diagonal and entries of 1 or -1 elsewhere. `live_rows`: some block has all 512 strings live.
All inputs are finite; a program needn't handle non-finite values.
Results may differ from a plain program's by a relative error of at most 0.0029.
Values may be sent and summed in bfloat16 or wider, within the bound.
No kernel may reach another device: no remote copies, remote signals or barrier semaphores. Data moves between devices by JAX's collectives and lax.ppermute only.
A program may use at most 128 MiB of HBM per device.

v0:
```python
import jax
import jax.numpy as jnp
from jax import lax
from jax.sharding import PartitionSpec as P


def on_device(coeffs, coupling, one_body, target_orb, source_orb, excite, live_rows):
    group_count = lax.axis_size("grp")
    block_rows = target_orb.shape[0]
    per_group = source_orb.shape[0] // group_count
    beta_count = coeffs.shape[2]
    group = lax.axis_index("grp")
    tables = lax.all_gather(one_body, "blk", axis=3, tiled=True)[0].astype(jnp.bfloat16)
    orbitals = tables.shape[-1]
    labels = jnp.arange(orbitals, dtype=jnp.int32)
    target_hot = (target_orb[:, None] == labels[None, :]).astype(jnp.bfloat16)
    source_hot = (
        source_orb.reshape(group_count, per_group)[:, :, None] == labels[None, None, :]
    ).astype(jnp.bfloat16)
    rowwise = jnp.einsum(
        "im,gcmn->cgin", target_hot, tables, preferred_element_type=jnp.float32
    ).astype(jnp.bfloat16)
    lookup = jnp.einsum(
        "cgin,gjn->cigj", rowwise, source_hot, preferred_element_type=jnp.float32
    ).astype(jnp.bfloat16)
    couple_row = lax.dynamic_index_in_dim(coupling, group, 0, keepdims=False)
    signs = excite.reshape(block_rows, group_count, per_group) * couple_row[None, :, None]
    plus_mask = (signs == 1)[None]
    minus_mask = (signs == -1)[None]
    zeros_like = jnp.zeros_like(lookup)
    operator = jnp.where(plus_mask, lookup, jnp.where(minus_mask, -lookup, zeros_like))
    slabs = lax.all_gather(
        coeffs.reshape(2, 1, coeffs.shape[1], beta_count), "grp", axis=1, tiled=True
    )
    part = operator
    part = part.reshape(part.shape[0], part.shape[1], -1)
    merged = lax.all_gather(slabs, "blk", axis=2, tiled=True).reshape(2, -1, beta_count)
    real_part = jnp.dot(part[0], merged[0], preferred_element_type=jnp.float32) - jnp.dot(
        part[1], merged[1], preferred_element_type=jnp.float32
    )
    imag_part = jnp.dot(part[0], merged[1], preferred_element_type=jnp.float32) + jnp.dot(
        part[1], merged[0], preferred_element_type=jnp.float32
    )
    real_part, imag_part = (real_part, imag_part)
    live = jnp.arange(block_rows, dtype=jnp.int32) < live_rows[0]
    result = jnp.stack([real_part, imag_part])
    return jnp.where(live[None, :, None], result, jnp.zeros_like(result))


def solution(mesh):
    return jax.shard_map(
        on_device,
        mesh=mesh,
        in_specs=(
            P(None, ("grp", "blk"), None),
            P(),
            P("grp", None, None, "blk", None),
            P(("grp", "blk")),
            P(),
            P(("grp", "blk"), None),
            P(("grp", "blk")),
        ),
        out_specs=P(None, ("grp", "blk"), None),
        check_vma=False,
    )
```

profile of v0, /device:TPU:1, one launch (start us, length us, event | category | flops | bytes accessed | tf_op | source)
XLA Modules:
  0.0 129.6 jit_solution(16559320343730305991)
XLA Ops:
  6.5 0.0 copy-start
  6.5 0.0 all-gather.3.cloned.1.call-start
  6.5 12.4 %all-gather = bf16[2,32,1024]{2,1,0:T(8,128)(2,1)} all-gather(bf16[2,8,1024]{2,1,0:T(8,128)(2,1)} %param.7), channel_id=2, replica_groups=mesh['grp'=4,'blk'=64] {'grp'}, dimensions={1}, use_global_device_ids=true | all-gather | bytes 163840 | tf_op jit(solution)/shard_map/all_gather | solution.py:32
  19.0 0.0 all-gather.3.cloned.1.call-update
  19.0 0.0 copy-start.2
  19.0 0.0 copy-start.1
  19.0 5.3 %copy.26 = s32[512,2048]{0,1:T(8,128)} copy(s32[512,2048]{1,0:T(8,128)} %param.12) | data formatting | bytes 8388608 | tf_op jit(solution)/shard_map/reshape | solution.py:27
  24.4 0.0 copy-done.2
  24.4 0.0 copy-start.4
  24.4 0.0 copy-done.1
  25.1 55.9 %all_gather.9 = bf16[1,4,2,64,64]{4,1,2,0,3:T(4,128)(2,1)S(1)} all-gather(bf16[1,4,2,1,64]{4,1,2,0,3:T(4,128)(2,1)S(1)} %copy.14), channel_id=1, replica_groups=mesh['grp'=4,'blk'=64] {'blk'}, dimensions={3}, use_global_device_ids=true | all-gather | bytes 66560 | tf_op jit(solution)/shard_map/all_gather | solution.py:13
  80.9 0.0 copy-done
  80.9 3.6 %multiply_compare_fusion.1 = (pred[512,4,512]{0,2,1:T(8,128)(4,1)S(1)}, pred[512,4,512]{0,2,1:T(8,128)(4,1)S(1)}) fusion(s32[512,4,512]{0,2,1:T(8,128)} %bitcast.71, s32[4]{0:T(128)S(1)} %dynamic-slice_bitcast_fusion), kind=kLoop, calls=%fused_computation.7 | loop fusion | flops 3145728 | bytes 6291472 | tf_op jit(solution)/shard_map/eq | solution.py:28
  84.6 0.0 copy-done.4
  84.6 4.6 %bitcast_select_fusion = bf16[2,512,4,512]{1,3,0,2:T(8,128)(2,1)} fusion(pred[512,4,512]{0,2,1:T(8,128)(4,1)S(1)} %get-tuple-element.6, pred[512,4,512]{0,2,1:T(8,128)(4,1)S(1)} %get-tuple-element.5, s32[4,512]{1,0:T(4,128)S(1)} %eq.50, bf16[4,2,64,64]{3,0,1,2:T(4,128)(2,1)S(1)} %bitcast.73, s32[512]{0:T(512)S(1)} %copy-done.4), kind=kOutput, calls=%fused_computation.3 | convolution fusion | flops 314998784 | bytes 6367232 | tf_op jit(solution)/shard_map/cgin,gjn->cigj/dot_general | solution.py:23
  89.2 17.7 %all-gather.3.cloned.1.call-done = bf16[2,4,512,1024]{3,2,1,0:T(8,128)(2,1)} async-done(((bf16[2,4,8,1024]{3,2,1,0:T(8,128)(2,1)}), bf16[2,4,512,1024]{3,2,1,0:T(8,128)(2,1)}) %all-gather.3.cloned.1.call-update) | async-done | bytes 8388624 | tf_op jit(solution)/shard_map/all_gather | solution.py:37
  106.9 0.0 copy-start.3
  106.9 0.0 copy-start.5
  106.9 5.3 %fusion.2 = f32[512,1024,1]{1,0,2:T(8,128)S(1)} fusion(bf16[2,4,512,1024]{3,2,1,0:T(8,128)(2,1)} %all-gather.3.cloned.1.call-done, bf16[2,512,4,512]{1,3,0,2:T(8,128)(2,1)} %bitcast_select_fusion), kind=kOutput, calls=%fused_computation.9 | convolution fusion | flops 2147483648 | bytes 8388608 | tf_op jit(solution)/shard_map/dot_general | solution.py:38
  112.2 0.0 copy-done.3
  112.2 1.1 copy-done.5
  113.3 2.4 %fusion.1 = f32[512,1024,1]{1,0,2:T(8,128)S(1)} fusion(bf16[2,4,512,1024]{3,2,1,0:T(8,128)(2,1)S(1)} %copy-done.3, bf16[2,512,4,512]{1,3,0,2:T(8,128)(2,1)S(1)} %copy-done.5), kind=kOutput, calls=%fused_computation.8 | convolution fusion | flops 2147483648 | bytes 8388608 | tf_op jit(solution)/shard_map/dot_general | solution.py:41
  115.6 2.4 %fusion.6 = f32[1,512,1024]{2,1,0:T(8,128)S(1)} fusion(f32[512,1024,1]{1,0,2:T(8,128)S(1)} %fusion.2, bf16[2,4,512,1024]{3,2,1,0:T(8,128)(2,1)S(1)} %copy-done.3, bf16[2,512,4,512]{1,3,0,2:T(8,128)(2,1)S(1)} %copy-done.5), kind=kOutput, calls=%fused_computation.17 | convolution fusion | flops 2148007936 | bytes 10485760 | tf_op jit(solution)/shard_map/dot_general | solution.py:38
  118.0 2.4 %fusion.5 = f32[1,512,1024]{2,1,0:T(8,128)S(1)} fusion(f32[512,1024,1]{1,0,2:T(8,128)S(1)} %fusion.1, bf16[2,4,512,1024]{3,2,1,0:T(8,128)(2,1)S(1)} %copy-done.3, bf16[2,512,4,512]{1,3,0,2:T(8,128)(2,1)S(1)} %copy-done.5), kind=kOutput, calls=%fused_computation.15 | convolution fusion | flops 2148007936 | bytes 10485760 | tf_op jit(solution)/shard_map/dot_general | solution.py:41
  120.4 2.4 %maximum_select_fusion = f32[2,512,1024]{2,1,0:T(8,128)} fusion(f32[1,512,1024]{2,1,0:T(8,128)S(1)} %fusion.5, f32[1,512,1024]{2,1,0:T(8,128)S(1)} %fusion.6, pred[512]{0:T(512)(128)(4,1)S(1)} %iota_compare_fusion.2), kind=kLoop, calls=%fused_computation.2 | loop fusion | flops 2097152 | bytes 8389120 | tf_op jit(solution)/shard_map/jit(_where)/select_n | solution.py:47
  (4 shorter events, 0.0 us)
Async XLA Ops:
  6.5 74.4 %copy-start = (s32[4,4]{1,0:T(4,128)S(1)}, s32[4,4]{1,0:T(4,128)}, u32[]{:S(2)}) copy-start(s32[4,4]{1,0:T(4,128)} %param.8) | copy-start | bytes 196
  6.5 100.3 %all-gather.3.cloned.1.call-start = ((), (), s32[]{:S(2)}) async-start(), calls=%async_computation | async-start | bytes 8519680 | tf_op jit(solution)/shard_map/all_gather | solution.py:37
  19.0 5.4 %copy-start.2 = (f32[1,4,2,1,64]{4,3,2,1,0:T(1,128)S(1)}, f32[1,4,2,1,64]{4,3,2,1,0:T(1,128)}, u32[]{:S(2)}) copy-start(f32[1,4,2,1,64]{4,3,2,1,0:T(1,128)} %param.9) | copy-start | bytes 6148
  19.0 5.4 %copy-start.1 = (s32[2048]{0:T(1024)S(1)}, s32[2048]{0:T(1024)}, u32[]{:S(2)}) copy-start(s32[2048]{0:T(1024)} %param.11) | copy-start | bytes 24580
  24.4 60.2 %copy-start.4 = (s32[512]{0:T(512)S(1)}, s32[512]{0:T(512)}, u32[]{:S(2)}) copy-start(s32[512]{0:T(512)} %param.10) | copy-start | bytes 6148
  106.9 5.3 %copy-start.3 = (bf16[2,4,512,1024]{3,2,1,0:T(8,128)(2,1)S(1)}, bf16[2,4,512,1024]{3,2,1,0:T(8,128)(2,1)}, u32[]{:S(2)}) copy-start(bf16[2,4,512,1024]{3,2,1,0:T(8,128)(2,1)} %all-gather.3.cloned.1.call-done) | copy-start | bytes 25165828
  106.9 6.4 %copy-start.5 = (bf16[2,512,4,512]{1,3,0,2:T(8,128)(2,1)S(1)}, bf16[2,512,4,512]{1,3,0,2:T(8,128)(2,1)}, u32[]{:S(2)}) copy-start(bf16[2,512,4,512]{1,3,0,2:T(8,128)(2,1)} %bitcast_select_fusion) | copy-start | bytes 12582916
Sparse Core Ops, SparseCore 0:
  19.1 87.7 all-gather.2
where the time goes:
time: 130 us
  blocking collectives  68.3 us (53%)
  waiting for transfers between devices  17.7 us (14%)
  matrix products  17 us (13%)
  between operations  14.1 us (11%)
  local copies, waits for them, and re-layouts  6.48 us (5%)
  other arithmetic  5.97 us (5%)
    all_gather x1, blocking collectives, on_device(): lax.all_gather(one_body, 'blk', axis=3, tiled=True)[0].astype(jnp.bfloat16)  55.9 us
    all_gather x1, waiting for transfers between devices, on_device(): lax.all_gather(slabs, 'blk', axis=2, tiled=True).reshape(2, -1, beta_count)  17.7 us
    all_gather x1, blocking collectives, on_device(): lax.all_gather(coeffs.reshape(2, 1, coeffs.shape[1], beta_count), 'grp',...  12.4 us
    reshape x1, local copies, waits for them, and re-layouts, on_device(): excite.reshape(block_rows, group_count, per_group)  5.35 us
    dot_general x1, matrix products, on_device(): jnp.dot(part[0], merged[0], preferred_element_type=jnp.float32)  5.31 us
    dot_general x1, matrix products, on_device(): jnp.einsum('cgin,gjn->cigj', rowwise, source_hot, preferred_element_type=...  4.59 us
    eq x1, other arithmetic, on_device(): plus_mask = (signs == 1)[None]  3.6 us
  transfers between devices with their start and end apart: 1, of which 1 were waited for; matrix products, arithmetic and copies ran while one was open for 10% of the time, Pallas kernels for 0%

commit v1 on v0

v1 whole, which is shorter than its diff:
```python
import functools

import jax
import jax.numpy as jnp
import numpy as np
from jax import lax
from jax.experimental import pallas as pl
from jax.experimental.pallas import tpu as pltpu

NY, NZ, NX = 4, 8, 4
AXES = ("grp", "blk")
STAGES = (
    ((0, 0, 4),),
    ((2, 0, 1), (0, 0, 2), (2, 0, -1)),
    ((0, 1, 1), (0, 2, 0), (0, -1, 1)),
    ((1, 0, 0), (-1, 0, 0), (0, 0, 1)),
)
HERE = ((0, 0, 0),)
SWAP = [(i, i ^ 1) for i in range(NY * NZ * NX * 2)]
MIB = 1 << 20


def mirrored(o):
    return (o[1], o[0], -o[2])


def index(x, y, z, c):
    return ((y % NY * NZ + z % NZ) * NX + x % NX) * 2 + c


def route(offset):
    pairs = []
    for y in range(NY):
        for z in range(NZ):
            for x in range(NX):
                for c in range(2):
                    dx, dy, dz = mirrored(offset) if c else offset
                    pairs.append((index(x + dx, y + dy, z + dz, c), index(x, y, z, c)))
    return pairs


def fetch(block, stage):
    return [lax.ppermute(block, AXES, route(o)) for o in STAGES[stage]]


def swap(block):
    return lax.ppermute(block, AXES, SWAP)


def chunk_offsets(last, half):
    second = HERE + STAGES[2]
    out = []
    for o2 in second[2 * half : 2 * half + 2]:
        for o1 in HERE + STAGES[1]:
            for o0 in HERE + STAGES[0]:
                out.append([sum(t) for t in zip(last, o2, o1, o0)])
    return out


def order_constants():
    lasts = HERE + STAGES[3]
    chunks = [(lasts[0], h, s) for s in (0, 1) for h in (0, 1)]
    for h in (0, 1):
        chunks += [(o, h, s) for s in (0, 1) for o in lasts[1:]]
    table = np.zeros((2, 5, len(chunks) * 128), np.int32)
    for core in (0, 1):
        at = 0
        for last, half, sibling in chunks:
            owner = core ^ sibling
            for o in chunk_offsets(last, half):
                dx, dy, dz = mirrored(o) if owner else o
                table[core, :, at : at + 8] = np.array([[dx], [dy], [dz], [owner], [0]])
                table[core, 4, at : at + 8] = np.arange(8)
                at += 8
    return table


ORDER = order_constants()


def operator_kernel(order_ref, aux_ref, target_ref, table_ref, excite_ref, out_ref, signs, rows):
    @pl.when(pl.program_id(0) == 0)
    def _():
        signs[:512, :] = excite_ref[...].astype(jnp.float32).astype(jnp.bfloat16)
        signs[512:, :] = aux_ref[...].astype(jnp.bfloat16)
        labels = lax.broadcasted_iota(jnp.int32, (64, 512), 0)
        hot = (labels == target_ref[...]).astype(jnp.float32).astype(jnp.bfloat16)
        rows[...] = lax.dot_general(
            hot, table_ref[...], (((0,), (0,)), ((), ())), preferred_element_type=jnp.float32
        ).astype(jnp.bfloat16)

    width = order_ref.shape[1]
    place = lax.broadcasted_iota(jnp.int32, (2048, width), 0)
    move = (place == order_ref[...]).astype(jnp.float32).astype(jnp.bfloat16)
    moved = jnp.dot(signs[...], move, preferred_element_type=jnp.float32)
    label = moved[512:513, :].astype(jnp.int32)
    couple = moved[513:514, :]
    lines = lax.broadcasted_iota(jnp.int32, (256, width), 0)
    hot = jnp.where(lines == label, couple, 0.0).astype(jnp.bfloat16)
    sign = moved[:512, :]
    for part in range(2):
        look = jnp.dot(rows[:, part * 256 : part * 256 + 256], hot, preferred_element_type=jnp.float32)
        value = (look * sign).astype(jnp.bfloat16)
        for piece in range(width // 128):
            at = piece * 256 + part * 128
            out_ref[:, at : at + 128] = value[:, piece * 128 : piece * 128 + 128]


def build_operator(order, aux, target, table, excite, width=256):
    columns = order.shape[1]
    return pl.pallas_call(
        operator_kernel,
        grid=(columns // width,),
        in_specs=[
            pl.BlockSpec((1, width), lambda i: (0, i)),
            pl.BlockSpec((16, 2048), lambda i: (0, 0)),
            pl.BlockSpec((1, 512), lambda i: (0, 0)),
            pl.BlockSpec((64, 512), lambda i: (0, 0)),
            pl.BlockSpec((512, 2048), lambda i: (0, 0)),
        ],
        out_specs=pl.BlockSpec((512, 2 * width), lambda i: (0, i)),
        out_shape=jax.ShapeDtypeStruct((512, 2 * columns), jnp.bfloat16),
        scratch_shapes=[pltpu.VMEM((528, 2048), jnp.bfloat16), pltpu.VMEM((512, 512), jnp.bfloat16)],
        compiler_params=pltpu.CompilerParams(vmem_limit_bytes=32 * MIB),
        cost_estimate=pl.CostEstimate(
            flops=2 * 512 * columns * 2560, bytes_accessed=4 * MIB + 2048 * columns, transcendentals=0
        ),
    )(order, aux, target, table, excite)


def product_kernel(first, last, count, *refs):
    live_ref, left_ref = refs[:2]
    chunks = refs[2 : 2 + count]
    total_ref = None if first else refs[2 + count]
    out_ref = refs[-1]

    def run(signs):
        acc = jnp.zeros((512, out_ref.shape[2]), jnp.float32) if first else total_ref[0]
        for k, chunk in enumerate(chunks):
            for half, (part, negative) in enumerate(signs):
                right = chunk[part]
                if negative:
                    right = -right
                at = k * 256 + half * 128
                acc = acc + jnp.dot(left_ref[:, at : at + 128], right, preferred_element_type=jnp.float32)
        if last:
            line = lax.broadcasted_iota(jnp.int32, acc.shape, 0)
            acc = jnp.where(line < live_ref[0], acc, 0.0)
        out_ref[0] = acc

    @pl.when(pl.program_id(0) == 0)
    def _():
        run(((0, False), (1, True)))

    @pl.when(pl.program_id(0) == 1)
    def _():
        run(((1, False), (0, False)))


def product(live, left, chunks, total, last, width=512):
    count = len(chunks)
    first = total is None
    block = pl.BlockSpec((1, 512, width), lambda p, n: (p, 0, n))
    return pl.pallas_call(
        functools.partial(product_kernel, first, last, count),
        grid=(2, 1024 // width),
        in_specs=[
            pl.BlockSpec(memory_space=pltpu.SMEM),
            pl.BlockSpec((512, 256 * count), lambda p, n: (0, 0)),
        ]
        + [pl.BlockSpec((2, 128, width), lambda p, n: (0, 0, n))] * count
        + ([] if first else [block]),
        out_specs=block,
        out_shape=jax.ShapeDtypeStruct((2, 512, 1024), jnp.float32),
        input_output_aliases={} if first else {2 + count: 0},
        compiler_params=pltpu.CompilerParams(vmem_limit_bytes=32 * MIB),
        cost_estimate=pl.CostEstimate(
            flops=2 * 512 * 1024 * 512 * count, bytes_accessed=(12 + count) * MIB, transcendentals=0
        ),
    )(live, left, *chunks, *([] if first else [total]))


def on_device(coeffs, coupling, one_body, target_orb, source_orb, excite, live_rows):
    grp, blk = lax.axis_index("grp"), lax.axis_index("blk")
    y, z, x, core = grp, blk // 8, blk // 2 % 4, blk % 2

    slab = jnp.concatenate([coeffs] + fetch(coeffs, 0), 1)

    row = one_body[0, :, :, 0, :].astype(jnp.bfloat16).transpose(1, 0, 2).reshape(1, 4, 128)
    table = lax.all_to_all(jnp.broadcast_to(row, (64, 4, 128)), "blk", 0, 0, tiled=True).reshape(64, 512)

    dx, dy, dz, owner, place = jnp.where(core == 0, ORDER[0], ORDER[1])
    order = ((((y + dy) % NY * NZ + (z + dz) % NZ) * NX + (x + dx) % NX) * 2 + owner) * 8 + place
    order = order[None, :]
    group = jnp.arange(2048, dtype=jnp.int32) // 512
    label = group * 64 + source_orb
    couple = jnp.repeat(lax.dynamic_index_in_dim(coupling, grp, 0, keepdims=False), 512)
    aux = jnp.concatenate([label[None], couple[None], jnp.zeros((14, 2048), jnp.int32)]).astype(jnp.float32)
    target = target_orb[None, :]
    build = functools.partial(build_operator, aux=aux, target=target, table=table, excite=excite)
    left0, left1, left2 = build(order[:, :512]), build(order[:, 512:1280]), build(order[:, 1280:])

    slab = jnp.concatenate([slab] + fetch(slab, 1), 1)
    near = fetch(slab, 2)
    halves = [jnp.concatenate([slab, near[0]], 1), jnp.concatenate(near[1:], 1)]
    total = product(live_rows, left0, halves + [swap(h) for h in halves], None, False)
    for half, left, last in ((halves[0], left1, False), (halves[1], left2, True)):
        got = fetch(half, 3)
        total = product(live_rows, left, got + [swap(g) for g in got], total, last)
    return total


def solution(mesh):
    from jax.sharding import PartitionSpec as P

    return jax.shard_map(
        on_device,
        mesh=mesh,
        in_specs=(
            P(None, ("grp", "blk"), None),
            P(),
            P("grp", None, None, "blk", None),
            P(("grp", "blk")),
            P(),
            P(("grp", "blk"), None),
            P(("grp", "blk")),
        ),
        out_specs=P(None, ("grp", "blk"), None),
        check_vma=False,
    )
```

time: 130 us -> 109 us (0.84)
  blocking collectives: 68.3 us -> 0 us
  starting transfers between devices: 0.01 us -> 43.6 us
  Pallas kernels: 0 us -> 39.7 us
  matrix products: 17 us -> 0 us
  between operations: 14.1 us -> 0.88 us
  waiting for transfers between devices: 17.7 us -> 10.4 us
  local copies, waits for them, and re-layouts: 6.48 us -> 11.5 us
  other arithmetic: 5.97 us -> 2.44 us
    all_gather x2 -> x0, blocking collectives: 68.3 us -> none  [the longest x1 55.9 us: on_device(): lax.all_gather(one_body, 'blk', axis=3, tiled=True)[0].astype(jnp.bfloat16)]
    pallas_call x0 -> x6, Pallas kernels: none -> 39.7 us  [the longest x3 26.8 us: product(): pl.pallas_call(functools.partial(product_kernel, first, last, count), gri...]
    ppermute x0 -> x21, starting transfers between devices: none -> 36.4 us  [the longest x13 32.1 us: fetch(): return [lax.ppermute(block, AXES, route(o)) for o in STAGES[stage]]]
    all_gather x1 -> x0, waiting for transfers between devices: 17.7 us -> none  [on_device(): lax.all_gather(slabs, 'blk', axis=2, tiled=True).reshape(2, -1, beta_count)]
    dot_general x5 -> x0, matrix products: 17 us -> none  [the longest x1 5.31 us: on_device(): jnp.dot(part[0], merged[0], preferred_element_type=jnp.float32)]
    ppermute x0 -> x21, waiting for transfers between devices: none -> 10.4 us  [the longest x13 10.4 us: fetch(): return [lax.ppermute(block, AXES, route(o)) for o in STAGES[stage]]]
    unnamed x13 -> x26, local copies, waits for them, and re-layouts: 1.11 us -> 9.24 us
    all_to_all x0 -> x1, starting transfers between devices: none -> 7.17 us  [on_device(): lax.all_to_all(jnp.broadcast_to(row, (64, 4, 128)), 'blk', 0, 0, tiled=True)]
  transfers between devices with their start and end apart: 1 -> 22, of which waited for: 1 -> 6; matrix products, arithmetic and copies ran while one was open for 10% -> 9% of each run, Pallas kernels for 0% -> 28%
where the time goes in v1:
time: 109 us
  starting transfers between devices  43.6 us (40%)
  Pallas kernels  39.7 us (36%)
  local copies, waits for them, and re-layouts  11.5 us (11%)
  waiting for transfers between devices  10.4 us (10%)
  other arithmetic  2.44 us (2%)
    ppermute x13, starting transfers between devices, fetch(): return [lax.ppermute(block, AXES, route(o)) for o in STAGES[stage]]  32.1 us
    pallas_call x3, Pallas kernels, product(): pl.pallas_call(functools.partial(product_kernel, first, last, count), gri...  26.8 us
    pallas_call x3, Pallas kernels, build_operator(): pl.pallas_call(operator_kernel, grid=(columns // width,), in_specs=[pl.Bl...  12.9 us
    ppermute x13, waiting for transfers between devices, fetch(): return [lax.ppermute(block, AXES, route(o)) for o in STAGES[stage]]  10.4 us
    unnamed x26, local copies, waits for them, and re-layouts  9.24 us
    all_to_all x1, starting transfers between devices, on_device(): lax.all_to_all(jnp.broadcast_to(row, (64, 4, 128)), 'blk', 0, 0, tiled=True)  7.17 us
    ppermute x8, starting transfers between devices, swap(): return lax.ppermute(block, AXES, SWAP)  4.36 us
  transfers between devices with their start and end apart: 22, of which 6 were waited for; matrix products, arithmetic and copies ran while one was open for 9% of the time, Pallas kernels for 28%

profile of v1, /device:TPU:1, one launch (start us, length us, event | category | flops | bytes accessed | tf_op | source)
XLA Modules:
  0.0 108.6 jit_solution(514121746634502027)
XLA Ops:
  0.0 7.7 %collective-permute-start = (bf16[2,8,1024]{2,1,0:T(8,128)(2,1)}, bf16[2,8,1024]{2,1,0:T(8,128)(2,1)S(1)}, u32[]{:S(2)}, u32[]{:S(2)}) collective-permute-start(bf16[2,8,1024]{2,1,0:T(8,128)(2,1)} %param.9), channel_id=1, source_target_pairs={{32,0},{33,1},{34,2},{35,3},{36,4},{37,5},{38,6},{39,7},{40,8},{41... | collective-permute-start | bytes 98312 | tf_op jit(solution)/shard_map/ppermute | solution.py:43
  7.7 0.7 convert_element_type.10
  8.4 0.1 broadcast_in_dim.24
  8.5 0.6 broadcast_in_dim.25
  9.2 7.2 %all-to-all-start = ((bf16[64,4,128]{2,1,0:T(4,128)(2,1)}), bf16[64,4,128]{2,1,0:T(4,128)(2,1)S(1)}, u32[]{:S(2)}, u32[]{:S(2)}) async-start(bf16[64,4,128]{2,1,0:T(4,128)(2,1)} %broadcast_in_dim.25), calls=%async_computation | async-start | bytes 131072 | tf_op jit(solution)/shard_map/all_to_all | solution.py:190
  16.4 1.4 %constant_dynamic-update-slice_fusion.14 = (bf16[2,128,1024]{2,1,0:T(8,128)(2,1)}, bf16[2,16,1024]{2,1,0:T(8,128)(2,1)S(1)}, bf16[2,64,1024]{2,1,0:T(8,128)(2,1)S(1)}) fusion(bf16[2,8,1024]{2,1,0:T(8,128)(2,1)} %param.9), kind=kLoop, calls=%fused_computation.22 | loop fusion | bytes 131072
  17.7 0.0 collective-permute-done
  17.7 0.6 constant_dynamic-update-slice_fusion.13
  18.4 4.0 %collective-permute-start.1 = (bf16[2,16,1024]{2,1,0:T(8,128)(2,1)S(1)}, bf16[2,16,1024]{2,1,0:T(8,128)(2,1)S(1)}, u32[]{:S(2)}, u32[]{:S(2)}) collective-permute-start(bf16[2,16,1024]{2,1,0:T(8,128)(2,1)S(1)} %get-tuple-element.13), channel_id=1, source_target_pairs={{12,0},{185,1},{14,2},{187,3},{8,4},{189,5},{10,6},{191,7},{20,8},... | collective-permute-start | bytes 196616 | tf_op jit(solution)/shard_map/ppermute | solution.py:43
  22.4 0.9 broadcast_select_fusion
  23.3 2.2 %collective-permute-start.2 = (bf16[2,16,1024]{2,1,0:T(8,128)(2,1)S(1)}, bf16[2,16,1024]{2,1,0:T(8,128)(2,1)S(1)}, u32[]{:S(2)}, u32[]{:S(2)}) collective-permute-start(bf16[2,16,1024]{2,1,0:T(8,128)(2,1)S(1)} %get-tuple-element.13), channel_id=1, source_target_pairs={{16,0},{49,1},{18,2},{51,3},{20,4},{53,5},{22,6},{55,7},{24,8},{57... | collective-permute-start | bytes 196616 | tf_op jit(solution)/shard_map/ppermute | solution.py:43
  25.5 1.2 %collective-permute-start.3 = (bf16[2,16,1024]{2,1,0:T(8,128)(2,1)S(1)}, bf16[2,16,1024]{2,1,0:T(8,128)(2,1)S(1)}, u32[]{:S(2)}, u32[]{:S(2)}) collective-permute-start(bf16[2,16,1024]{2,1,0:T(8,128)(2,1)S(1)} %get-tuple-element.13), channel_id=1, source_target_pairs={{60,0},{137,1},{62,2},{139,3},{56,4},{141,5},{58,6},{143,7},{4,8},... | collective-permute-start | bytes 196616 | tf_op jit(solution)/shard_map/ppermute | solution.py:43
  26.7 0.0 collective-permute-done.1
  26.7 0.7 constant_dynamic-update-slice_fusion.12
  27.4 1.9 %collective-permute-done.2 = bf16[2,16,1024]{2,1,0:T(8,128)(2,1)S(1)} collective-permute-done((bf16[2,16,1024]{2,1,0:T(8,128)(2,1)S(1)}, bf16[2,16,1024]{2,1,0:T(8,128)(2,1)S(1)}, u32[]{:S(2)}, u32[]{:S(2)}) %collective-permute-start.2) | collective-permute-done | bytes 65568 | tf_op jit(solution)/shard_map/ppermute | solution.py:43
  29.3 0.6 constant_dynamic-update-slice_fusion.11
  29.9 1.1 collective-permute-done.3
  31.0 0.6 constant_dynamic-update-slice_fusion.10
  31.6 4.6 %collective-permute-start.12 = (bf16[2,64,1024]{2,1,0:T(8,128)(2,1)S(1)}, bf16[2,64,1024]{2,1,0:T(8,128)(2,1)S(1)}, u32[]{:S(2)}, u32[]{:S(2)}) collective-permute-start(bf16[2,64,1024]{2,1,0:T(8,128)(2,1)S(1)} %get-tuple-element.6), channel_id=1, source_target_pairs={{72,0},{59,1},{74,2},{61,3},{76,4},{63,5},{78,6},{57,7},{80,8},{3,... | collective-permute-start | bytes 786440 | tf_op jit(solution)/shard_map/ppermute | solution.py:43
  36.2 0.1 slice_add_fusion
  36.4 0.6 collective-permute-start.4
  37.0 0.7 fusion.3
  37.7 0.6 collective-permute-start.5
  38.4 2.0 %collective-permute-done.12 = bf16[2,64,1024]{2,1,0:T(8,128)(2,1)S(1)} collective-permute-done((bf16[2,64,1024]{2,1,0:T(8,128)(2,1)S(1)}, bf16[2,64,1024]{2,1,0:T(8,128)(2,1)S(1)}, u32[]{:S(2)}, u32[]{:S(2)}) %collective-permute-start.12) | collective-permute-done | bytes 262176 | tf_op jit(solution)/shard_map/ppermute | solution.py:43
  40.4 0.7 constant_dynamic-update-slice_fusion.9.refs_2_
  41.1 3.1 %collective-permute-start.19 = (bf16[2,128,1024]{2,1,0:T(8,128)(2,1)}, bf16[2,128,1024]{2,1,0:T(8,128)(2,1)S(1)}, u32[]{:S(2)}, u32[]{:S(2)}) collective-permute-start(bf16[2,128,1024]{2,1,0:T(8,128)(2,1)} %constant_dynamic-update-slice_fusion.9.refs_2_), channel_id=1, source_target_pairs={{0,1},{1,0},{2,3},{3,2},{4,5},{5,4},{6,7},{7,6},{8,9},{9,8},{10,11... | collective-permute-start | bytes 1572872 | tf_op jit(solution)/shard_map/ppermute | solution.py:47
  44.1 5.5 %collective-permute-start.13 = (bf16[2,128,1024]{2,1,0:T(8,128)(2,1)}, bf16[2,128,1024]{2,1,0:T(8,128)(2,1)S(1)}, u32[]{:S(2)}, u32[]{:S(2)}) collective-permute-start(bf16[2,128,1024]{2,1,0:T(8,128)(2,1)} %constant_dynamic-update-slice_fusion.9.refs_2_), channel_id=1, source_target_pairs={{2,0},{65,1},{4,2},{67,3},{6,4},{69,5},{0,6},{71,7},{10,8},{73,9},... | collective-permute-start | bytes 1572872 | tf_op jit(solution)/shard_map/ppermute | solution.py:43
  49.6 0.0 collective-permute-start.14
  49.6 0.0 collective-permute-done.4
  49.6 0.7 constant_dynamic-update-slice_fusion.8
  50.4 0.0 collective-permute-done.5
  50.4 0.7 constant_dynamic-update-slice_fusion.7.refs_3_
  51.1 0.0 collective-permute-start.20
  51.1 0.1 broadcast_bitcast_fusion
  51.2 0.1 pad.2.clone
  51.9 2.2 %collective-permute-start.15 = (bf16[2,128,1024]{2,1,0:T(8,128)(2,1)}, bf16[2,128,1024]{2,1,0:T(8,128)(2,1)S(1)}, u32[]{:S(2)}, u32[]{:S(2)}) collective-permute-start(bf16[2,128,1024]{2,1,0:T(8,128)(2,1)} %constant_dynamic-update-slice_fusion.9.refs_2_), channel_id=1, source_target_pairs={{8,0},{57,1},{10,2},{59,3},{12,4},{61,5},{14,6},{63,7},{16,8},{1,9... | collective-permute-start | bytes 1572872 | tf_op jit(solution)/shard_map/ppermute | solution.py:43
  54.1 0.8 copy-done.4
  54.9 0.0 collective-permute-start.7
  54.9 0.1 add_convert_fusion.aux_ref
  55.0 0.0 collective-permute-done.20.refs_5_
  55.0 0.8 copy-done.6
  55.8 0.0 collective-permute-start.8
  55.8 0.3 collective-permute-done.13.refs_2_
  56.1 3.3 %collective-permute-start.6 = (bf16[2,128,1024]{2,1,0:T(8,128)(2,1)}, bf16[2,128,1024]{2,1,0:T(8,128)(2,1)S(1)}, u32[]{:S(2)}, u32[]{:S(2)}) collective-permute-start(bf16[2,128,1024]{2,1,0:T(8,128)(2,1)} %constant_dynamic-update-slice_fusion.7.refs_3_), channel_id=1, source_target_pairs={{2,0},{65,1},{4,2},{67,3},{6,4},{69,5},{0,6},{71,7},{10,8},{73,9},... | collective-permute-start | bytes 1572872 | tf_op jit(solution)/shard_map/ppermute | solution.py:43
  59.4 0.0 collective-permute-start.16
  59.4 2.3 %collective-permute-done.15.refs_4_ = bf16[2,128,1024]{2,1,0:T(8,128)(2,1)S(1)} collective-permute-done((bf16[2,128,1024]{2,1,0:T(8,128)(2,1)}, bf16[2,128,1024]{2,1,0:T(8,128)(2,1)S(1)}, u32[]{:S(2)}, u32[]{:S(2)}) %collective-permute-start.15) | collective-permute-done | bytes 524320 | tf_op jit(solution)/shard_map/ppermute | solution.py:43
  61.7 0.2 collective-permute-start.17
  61.9 2.8 %collective-permute-done.7.refs_3_ = bf16[2,128,1024]{2,1,0:T(8,128)(2,1)S(1)} collective-permute-done((bf16[2,128,1024]{2,1,0:T(8,128)(2,1)}, bf16[2,128,1024]{2,1,0:T(8,128)(2,1)S(1)}, u32[]{:S(2)}, u32[]{:S(2)}) %collective-permute-start.7) | collective-permute-done | bytes 524320 | tf_op jit(solution)/shard_map/ppermute | solution.py:43
  64.7 0.2 collective-permute-start.18
  65.0 2.2 %copy-done.1 = s32[512,2048]{1,0:T(8,128)S(1)} copy-done((s32[512,2048]{1,0:T(8,128)S(1)}, s32[512,2048]{1,0:T(8,128)}, u32[]{:S(2)}) %copy-start.1) | copy-done | bytes 4194328
  67.1 0.7 copy-done.3
  67.8 4.7 %shard_map.92.refs_1_ = bf16[512,1536]{1,0:T(8,128)(2,1)S(1)} custom-call(s32[1,768]{1,0:T(1,128)S(1)} %get-tuple-element.17.order_ref, f32[16,2048]{1,0:T(8,128)S(1)} %add_convert_fusion.aux_ref, s32[1,512]{1,0:T(1,128)S(1)} %bitcast.20, bf16[64,512]{1,0:T(8,128)(2,1)S(1)} %bitcast.17, s32[512,2048]{1,0:T(8,128)S(1)} %copy-done.1), custom_call_target="tpu_custom_call" | custom-call | flops 2013265920 | bytes 5767168 | tf_op jit(solution)/shard_map/pallas_call | solution.py:111
  72.6 4.8 %shard_map.91.refs_1_ = bf16[512,1536]{1,0:T(8,128)(2,1)S(1)} custom-call(s32[1,768]{1,0:T(1,128)S(1)} %get-tuple-element.18.order_ref, f32[16,2048]{1,0:T(8,128)S(1)} %add_convert_fusion.aux_ref, s32[1,512]{1,0:T(1,128)S(1)} %bitcast.21, bf16[64,512]{1,0:T(8,128)(2,1)S(1)} %bitcast.18, s32[512,2048]{1,0:T(8,128)S(1)} %copy-done.2), custom_call_target="tpu_custom_call" | custom-call | flops 2013265920 | bytes 5767168 | tf_op jit(solution)/shard_map/pallas_call | solution.py:111
  77.3 0.0 copy-start.5
  77.4 0.4 collective-permute-start.10
  77.7 0.0 collective-permute-done.6.refs_2_
  77.7 0.2 collective-permute-start.11
  78.0 0.0 collective-permute-done.16.refs_5_
  78.0 0.3 collective-permute-start.9
  78.3 3.4 %shard_map.93.refs_1_ = bf16[512,1024]{1,0:T(8,128)(2,1)S(1)} custom-call(s32[1,512]{1,0:T(1,128)S(1)} %slice.14.order_ref, f32[16,2048]{1,0:T(8,128)S(1)} %add_convert_fusion.aux_ref, s32[1,512]{1,0:T(1,128)S(1)} %bitcast.22, bf16[64,512]{1,0:T(8,128)(2,1)S(1)} %bitcast.19, s32[512,2048]{1,0:T(8,128)S(1)} %copy-done.2), custom_call_target="tpu_custom_call" | custom-call | flops 1342177280 | bytes 5242880 | tf_op jit(solution)/shard_map/pallas_call | solution.py:111
  81.7 7.2 %shard_map.94.refs_8_ = f32[2,512,1024]{2,1,0:T(8,128)} custom-call(s32[1]{0:T(128)S(6)} %copy.33.refs_0_, bf16[512,1024]{1,0:T(8,128)(2,1)S(1)} %shard_map.93.refs_1_, bf16[2,128,1024]{2,1,0:T(8,128)(2,1)} %constant_dynamic-update-slice_fusion.9.refs_2_, bf16[2,128,1024]{2,1,0:T(8,128)(2,1)} %constant_dynamic-update-slice_fusion.7.refs_3_, ...), custom_call_target="tpu_custom_call" | custom-call | flops 2147483648 | bytes 16777216 | tf_op jit(solution)/shard_map/pallas_call | solution.py:164
  89.0 9.8 %shard_map.95.refs_8_ = f32[2,512,1024]{2,1,0:T(8,128)} custom-call(s32[1]{0:T(128)S(6)} %copy.33.refs_0_, bf16[512,1536]{1,0:T(8,128)(2,1)S(1)} %shard_map.92.refs_1_, bf16[2,128,1024]{2,1,0:T(8,128)(2,1)S(1)} %collective-permute-done.13.refs_2_, bf16[2,128,1024]{2,1,0:T(8,128)(2,1)S(1)} %collective-permute-done.14.refs_3_, ...), custom_call_target="tpu_custom_call", output_to_operand_aliasing={{}: (8, {})} | custom-call | flops 3221225472 | bytes 18874368 | tf_op jit(solution)/shard_map/pallas_call | solution.py:164
  98.8 0.0 collective-permute-done.9.refs_5_
  98.8 9.8 %shard_map.96 = f32[2,512,1024]{2,1,0:T(8,128)} custom-call(s32[1]{0:T(128)S(6)} %copy.33.refs_0_, bf16[512,1536]{1,0:T(8,128)(2,1)S(1)} %shard_map.91.refs_1_, bf16[2,128,1024]{2,1,0:T(8,128)(2,1)S(1)} %collective-permute-done.6.refs_2_, bf16[2,128,1024]{2,1,0:T(8,128)(2,1)S(1)} %collective-permute-done.7.refs_3_, ...), custom_call_target="tpu_custom_call", output_to_operand_aliasing={{}: (8, {})} | custom-call | flops 3221225472 | bytes 18874368 | tf_op jit(solution)/shard_map/pallas_call | solution.py:164
  (27 shorter events, 0.1 us)
Async XLA Ops:
  0.0 44.1 %copy-start = (s32[4,4]{1,0:T(4,128)S(1)}, s32[4,4]{1,0:T(4,128)}, u32[]{:S(2)}) copy-start(s32[4,4]{1,0:T(4,128)} %param.10) | copy-start | bytes 196
  0.0 17.7 %collective-permute-start = (bf16[2,8,1024]{2,1,0:T(8,128)(2,1)}, bf16[2,8,1024]{2,1,0:T(8,128)(2,1)S(1)}, u32[]{:S(2)}, u32[]{:S(2)}) collective-permute-start(bf16[2,8,1024]{2,1,0:T(8,128)(2,1)} %param.9), channel_id=1, source_target_pairs={{32,0},{33,1},{34,2},{35,3},{36,4},{37,5},{38,6},{39,7},{40,8},{41... | collective-permute-start | bytes 98312 | tf_op jit(solution)/shard_map/ppermute | solution.py:43
  9.2 50.2 %all-to-all-start = ((bf16[64,4,128]{2,1,0:T(4,128)(2,1)}), bf16[64,4,128]{2,1,0:T(4,128)(2,1)S(1)}, u32[]{:S(2)}, u32[]{:S(2)}) async-start(bf16[64,4,128]{2,1,0:T(4,128)(2,1)} %broadcast_in_dim.25), calls=%async_computation | async-start | bytes 131072 | tf_op jit(solution)/shard_map/all_to_all | solution.py:190
  18.4 8.3 %collective-permute-start.1 = (bf16[2,16,1024]{2,1,0:T(8,128)(2,1)S(1)}, bf16[2,16,1024]{2,1,0:T(8,128)(2,1)S(1)}, u32[]{:S(2)}, u32[]{:S(2)}) collective-permute-start(bf16[2,16,1024]{2,1,0:T(8,128)(2,1)S(1)} %get-tuple-element.13), channel_id=1, source_target_pairs={{12,0},{185,1},{14,2},{187,3},{8,4},{189,5},{10,6},{191,7},{20,8},... | collective-permute-start | bytes 196616 | tf_op jit(solution)/shard_map/ppermute | solution.py:43
  23.3 6.0 %collective-permute-start.2 = (bf16[2,16,1024]{2,1,0:T(8,128)(2,1)S(1)}, bf16[2,16,1024]{2,1,0:T(8,128)(2,1)S(1)}, u32[]{:S(2)}, u32[]{:S(2)}) collective-permute-start(bf16[2,16,1024]{2,1,0:T(8,128)(2,1)S(1)} %get-tuple-element.13), channel_id=1, source_target_pairs={{16,0},{49,1},{18,2},{51,3},{20,4},{53,5},{22,6},{55,7},{24,8},{57... | collective-permute-start | bytes 196616 | tf_op jit(solution)/shard_map/ppermute | solution.py:43
  25.5 5.5 %collective-permute-start.3 = (bf16[2,16,1024]{2,1,0:T(8,128)(2,1)S(1)}, bf16[2,16,1024]{2,1,0:T(8,128)(2,1)S(1)}, u32[]{:S(2)}, u32[]{:S(2)}) collective-permute-start(bf16[2,16,1024]{2,1,0:T(8,128)(2,1)S(1)} %get-tuple-element.13), channel_id=1, source_target_pairs={{60,0},{137,1},{62,2},{139,3},{56,4},{141,5},{58,6},{143,7},{4,8},... | collective-permute-start | bytes 196616 | tf_op jit(solution)/shard_map/ppermute | solution.py:43
  31.6 8.7 %collective-permute-start.12 = (bf16[2,64,1024]{2,1,0:T(8,128)(2,1)S(1)}, bf16[2,64,1024]{2,1,0:T(8,128)(2,1)S(1)}, u32[]{:S(2)}, u32[]{:S(2)}) collective-permute-start(bf16[2,64,1024]{2,1,0:T(8,128)(2,1)S(1)} %get-tuple-element.6), channel_id=1, source_target_pairs={{72,0},{59,1},{74,2},{61,3},{76,4},{63,5},{78,6},{57,7},{80,8},{3,... | collective-permute-start | bytes 786440 | tf_op jit(solution)/shard_map/ppermute | solution.py:43
  36.4 13.3 %collective-permute-start.4 = (bf16[2,64,1024]{2,1,0:T(8,128)(2,1)S(1)}, bf16[2,64,1024]{2,1,0:T(8,128)(2,1)S(1)}, u32[]{:S(2)}, u32[]{:S(2)}) collective-permute-start(bf16[2,64,1024]{2,1,0:T(8,128)(2,1)S(1)} %get-tuple-element.6), channel_id=1, source_target_pairs={{128,0},{5,1},{130,2},{7,3},{132,4},{1,5},{134,6},{3,7},{136,8},{1... | collective-permute-start | bytes 786440 | tf_op jit(solution)/shard_map/ppermute | solution.py:43
  37.7 12.7 %collective-permute-start.5 = (bf16[2,64,1024]{2,1,0:T(8,128)(2,1)S(1)}, bf16[2,64,1024]{2,1,0:T(8,128)(2,1)S(1)}, u32[]{:S(2)}, u32[]{:S(2)}) collective-permute-start(bf16[2,64,1024]{2,1,0:T(8,128)(2,1)S(1)} %get-tuple-element.6), channel_id=1, source_target_pairs={{200,0},{63,1},{202,2},{57,3},{204,4},{59,5},{206,6},{61,7},{208,8... | collective-permute-start | bytes 786440 | tf_op jit(solution)/shard_map/ppermute | solution.py:43
  41.1 13.0 %collective-permute-start.19 = (bf16[2,128,1024]{2,1,0:T(8,128)(2,1)}, bf16[2,128,1024]{2,1,0:T(8,128)(2,1)S(1)}, u32[]{:S(2)}, u32[]{:S(2)}) collective-permute-start(bf16[2,128,1024]{2,1,0:T(8,128)(2,1)} %constant_dynamic-update-slice_fusion.9.refs_2_), channel_id=1, source_target_pairs={{0,1},{1,0},{2,3},{3,2},{4,5},{5,4},{6,7},{7,6},{8,9},{9,8},{10,11... | collective-permute-start | bytes 1572872 | tf_op jit(solution)/shard_map/ppermute | solution.py:47
  44.1 11.9 %collective-permute-start.13 = (bf16[2,128,1024]{2,1,0:T(8,128)(2,1)}, bf16[2,128,1024]{2,1,0:T(8,128)(2,1)S(1)}, u32[]{:S(2)}, u32[]{:S(2)}) collective-permute-start(bf16[2,128,1024]{2,1,0:T(8,128)(2,1)} %constant_dynamic-update-slice_fusion.9.refs_2_), channel_id=1, source_target_pairs={{2,0},{65,1},{4,2},{67,3},{6,4},{69,5},{0,6},{71,7},{10,8},{73,9},... | collective-permute-start | bytes 1572872 | tf_op jit(solution)/shard_map/ppermute | solution.py:43
  49.6 9.8 %collective-permute-start.14 = (bf16[2,128,1024]{2,1,0:T(8,128)(2,1)}, bf16[2,128,1024]{2,1,0:T(8,128)(2,1)S(1)}, u32[]{:S(2)}, u32[]{:S(2)}) collective-permute-start(bf16[2,128,1024]{2,1,0:T(8,128)(2,1)} %constant_dynamic-update-slice_fusion.9.refs_2_), channel_id=1, source_target_pairs={{6,0},{193,1},{0,2},{195,3},{2,4},{197,5},{4,6},{199,7},{14,8},{20... | collective-permute-start | bytes 1572872 | tf_op jit(solution)/shard_map/ppermute | solution.py:43
  51.1 3.9 %collective-permute-start.20 = (bf16[2,128,1024]{2,1,0:T(8,128)(2,1)}, bf16[2,128,1024]{2,1,0:T(8,128)(2,1)S(1)}, u32[]{:S(2)}, u32[]{:S(2)}) collective-permute-start(bf16[2,128,1024]{2,1,0:T(8,128)(2,1)} %constant_dynamic-update-slice_fusion.7.refs_3_), channel_id=1, source_target_pairs={{0,1},{1,0},{2,3},{3,2},{4,5},{5,4},{6,7},{7,6},{8,9},{9,8},{10,11... | collective-permute-start | bytes 1572872 | tf_op jit(solution)/shard_map/ppermute | solution.py:47
  51.9 9.8 %collective-permute-start.15 = (bf16[2,128,1024]{2,1,0:T(8,128)(2,1)}, bf16[2,128,1024]{2,1,0:T(8,128)(2,1)S(1)}, u32[]{:S(2)}, u32[]{:S(2)}) collective-permute-start(bf16[2,128,1024]{2,1,0:T(8,128)(2,1)} %constant_dynamic-update-slice_fusion.9.refs_2_), channel_id=1, source_target_pairs={{8,0},{57,1},{10,2},{59,3},{12,4},{61,5},{14,6},{63,7},{16,8},{1,9... | collective-permute-start | bytes 1572872 | tf_op jit(solution)/shard_map/ppermute | solution.py:43
  54.1 0.8 copy-start.4
  54.9 9.8 %collective-permute-start.7 = (bf16[2,128,1024]{2,1,0:T(8,128)(2,1)}, bf16[2,128,1024]{2,1,0:T(8,128)(2,1)S(1)}, u32[]{:S(2)}, u32[]{:S(2)}) collective-permute-start(bf16[2,128,1024]{2,1,0:T(8,128)(2,1)} %constant_dynamic-update-slice_fusion.7.refs_3_), channel_id=1, source_target_pairs={{6,0},{193,1},{0,2},{195,3},{2,4},{197,5},{4,6},{199,7},{14,8},{20... | collective-permute-start | bytes 1572872 | tf_op jit(solution)/shard_map/ppermute | solution.py:43
  55.0 0.8 copy-start.6
  55.8 21.6 %collective-permute-start.8 = (bf16[2,128,1024]{2,1,0:T(8,128)(2,1)}, bf16[2,128,1024]{2,1,0:T(8,128)(2,1)S(1)}, u32[]{:S(2)}, u32[]{:S(2)}) collective-permute-start(bf16[2,128,1024]{2,1,0:T(8,128)(2,1)} %constant_dynamic-update-slice_fusion.7.refs_3_), channel_id=1, source_target_pairs={{8,0},{57,1},{10,2},{59,3},{12,4},{61,5},{14,6},{63,7},{16,8},{1,9... | collective-permute-start | bytes 1572872 | tf_op jit(solution)/shard_map/ppermute | solution.py:43
  56.1 21.6 %collective-permute-start.6 = (bf16[2,128,1024]{2,1,0:T(8,128)(2,1)}, bf16[2,128,1024]{2,1,0:T(8,128)(2,1)S(1)}, u32[]{:S(2)}, u32[]{:S(2)}) collective-permute-start(bf16[2,128,1024]{2,1,0:T(8,128)(2,1)} %constant_dynamic-update-slice_fusion.7.refs_3_), channel_id=1, source_target_pairs={{2,0},{65,1},{4,2},{67,3},{6,4},{69,5},{0,6},{71,7},{10,8},{73,9},... | collective-permute-start | bytes 1572872 | tf_op jit(solution)/shard_map/ppermute | solution.py:43
  59.4 18.6 %collective-permute-start.16 = (bf16[2,128,1024]{2,1,0:T(8,128)(2,1)S(1)}, bf16[2,128,1024]{2,1,0:T(8,128)(2,1)}, u32[]{:S(2)}, u32[]{:S(2)}) collective-permute-start(bf16[2,128,1024]{2,1,0:T(8,128)(2,1)S(1)} %collective-permute-done.13.refs_2_), channel_id=1, source_target_pairs={{0,1},{1,0},{2,3},{3,2},{4,5},{5,4},{6,7},{7,6},{8,9},{9,8},{10,11... | collective-permute-start | bytes 1572872 | tf_op jit(solution)/shard_map/ppermute | solution.py:47
  61.7 27.2 %collective-permute-start.17 = (bf16[2,128,1024]{2,1,0:T(8,128)(2,1)S(1)}, bf16[2,128,1024]{2,1,0:T(8,128)(2,1)S(1)}, u32[]{:S(2)}, u32[]{:S(2)}) collective-permute-start(bf16[2,128,1024]{2,1,0:T(8,128)(2,1)S(1)} %collective-permute-done.14.refs_3_), channel_id=1, source_target_pairs={{0,1},{1,0},{2,3},{3,2},{4,5},{5,4},{6,7},{7,6},{8,9},{9,8},{10,11... | collective-permute-start | bytes 1572872 | tf_op jit(solution)/shard_map/ppermute | solution.py:47
  64.7 24.3 %collective-permute-start.18 = (bf16[2,128,1024]{2,1,0:T(8,128)(2,1)S(1)}, bf16[2,128,1024]{2,1,0:T(8,128)(2,1)S(1)}, u32[]{:S(2)}, u32[]{:S(2)}) collective-permute-start(bf16[2,128,1024]{2,1,0:T(8,128)(2,1)S(1)} %collective-permute-done.15.refs_4_), channel_id=1, source_target_pairs={{0,1},{1,0},{2,3},{3,2},{4,5},{5,4},{6,7},{7,6},{8,9},{9,8},{10,11... | collective-permute-start | bytes 1572872 | tf_op jit(solution)/shard_map/ppermute | solution.py:47
  65.0 2.2 %copy-start.1 = (s32[512,2048]{1,0:T(8,128)S(1)}, s32[512,2048]{1,0:T(8,128)}, u32[]{:S(2)}) copy-start(s32[512,2048]{1,0:T(8,128)} %excite_ref.5) | copy-start | bytes 12582916
  67.1 0.7 copy-start.3
  67.8 4.7 %copy-start.2 = (s32[512,2048]{1,0:T(8,128)S(1)}, s32[512,2048]{1,0:T(8,128)}, u32[]{:S(2)}) copy-start(s32[512,2048]{1,0:T(8,128)} %excite_ref.5) | copy-start | bytes 12582916
  77.3 4.4 %copy-start.5 = (bf16[2,128,1024]{2,1,0:T(8,128)(2,1)S(1)}, bf16[2,128,1024]{2,1,0:T(8,128)(2,1)}, u32[]{:S(2)}) copy-start(bf16[2,128,1024]{2,1,0:T(8,128)(2,1)} %copy-done.4) | copy-start | bytes 1572868
  77.3 4.4 %copy-start.7 = (bf16[2,128,1024]{2,1,0:T(8,128)(2,1)S(1)}, bf16[2,128,1024]{2,1,0:T(8,128)(2,1)}, u32[]{:S(2)}) copy-start(bf16[2,128,1024]{2,1,0:T(8,128)(2,1)} %copy-done.6) | copy-start | bytes 1572868
  77.4 21.4 %collective-permute-start.10 = (bf16[2,128,1024]{2,1,0:T(8,128)(2,1)S(1)}, bf16[2,128,1024]{2,1,0:T(8,128)(2,1)S(1)}, u32[]{:S(2)}, u32[]{:S(2)}) collective-permute-start(bf16[2,128,1024]{2,1,0:T(8,128)(2,1)S(1)} %collective-permute-done.7.refs_3_), channel_id=1, source_target_pairs={{0,1},{1,0},{2,3},{3,2},{4,5},{5,4},{6,7},{7,6},{8,9},{9,8},{10,11... | collective-permute-start | bytes 1572872 | tf_op jit(solution)/shard_map/ppermute | solution.py:47
  77.7 21.0 %collective-permute-start.11 = (bf16[2,128,1024]{2,1,0:T(8,128)(2,1)S(1)}, bf16[2,128,1024]{2,1,0:T(8,128)(2,1)S(1)}, u32[]{:S(2)}, u32[]{:S(2)}) collective-permute-start(bf16[2,128,1024]{2,1,0:T(8,128)(2,1)S(1)} %collective-permute-done.8.refs_4_), channel_id=1, source_target_pairs={{0,1},{1,0},{2,3},{3,2},{4,5},{5,4},{6,7},{7,6},{8,9},{9,8},{10,11... | collective-permute-start | bytes 1572872 | tf_op jit(solution)/shard_map/ppermute | solution.py:47
  78.0 20.8 %collective-permute-start.9 = (bf16[2,128,1024]{2,1,0:T(8,128)(2,1)S(1)}, bf16[2,128,1024]{2,1,0:T(8,128)(2,1)S(1)}, u32[]{:S(2)}, u32[]{:S(2)}) collective-permute-start(bf16[2,128,1024]{2,1,0:T(8,128)(2,1)S(1)} %collective-permute-done.6.refs_2_), channel_id=1, source_target_pairs={{0,1},{1,0},{2,3},{3,2},{4,5},{5,4},{6,7},{7,6},{8,9},{9,8},{10,11... | collective-permute-start | bytes 1572872 | tf_op jit(solution)/shard_map/ppermute | solution.py:47

commit v2 on v0

v2 whole, which is shorter than its diff:
```python
import functools

import jax
import jax.numpy as jnp
import numpy as np
from jax import lax
from jax.experimental import pallas as pl
from jax.experimental.pallas import tpu as pltpu

NY, NZ, NX = 4, 8, 4
AXES = ("grp", "blk")
STAGES = (
    ((0, 0, 4),),
    ((2, 0, 1), (0, 0, 2), (2, 0, -1)),
    ((0, 1, 1), (0, 2, 0), (0, -1, 1)),
    ((1, 0, 0), (-1, 0, 0), (0, 0, 1)),
)
HERE = ((0, 0, 0),)
SWAP = [(i, i ^ 1) for i in range(NY * NZ * NX * 2)]
MIB = 1 << 20


def mirrored(o):
    return (o[1], o[0], -o[2])


def index(x, y, z, c):
    return ((y % NY * NZ + z % NZ) * NX + x % NX) * 2 + c


def route(offset):
    pairs = []
    for y in range(NY):
        for z in range(NZ):
            for x in range(NX):
                for c in range(2):
                    dx, dy, dz = mirrored(offset) if c else offset
                    pairs.append((index(x + dx, y + dy, z + dz, c), index(x, y, z, c)))
    return pairs


def fetch(block, stage):
    return [lax.ppermute(block, AXES, route(o)) for o in STAGES[stage]]


def swap(block):
    return lax.ppermute(block, AXES, SWAP)


def half_offsets(last, half):
    second = HERE + STAGES[2]
    out = []
    for o2 in second[2 * half : 2 * half + 2]:
        for o1 in HERE + STAGES[1]:
            for o0 in HERE + STAGES[0]:
                out.append([sum(t) for t in zip(last, o2, o1, o0)])
    return out


def order_constants():
    lasts = HERE + STAGES[3]
    own = [(lasts[0], 0), (lasts[0], 1)] + [(o, h) for h in (0, 1) for o in lasts[1:]]
    table = np.zeros((2, 4, 8, 1, 256), np.int32)
    for core in (0, 1):
        for pair in range(8):
            sibling, first = divmod(pair, 4)
            offsets = []
            for last, half in own[2 * first : 2 * first + 2]:
                offsets += half_offsets(last, half)
            offsets = [mirrored(o) if core ^ sibling else o for o in offsets]
            table[core, :3, pair, 0] = np.repeat(np.array(offsets), 8, 0).T
            table[core, 3, pair, 0] = np.tile(np.arange(8), 32)
    return table


ORDER = order_constants()
VMEM = pl.BlockSpec(memory_space=pltpu.VMEM)
SMEM = pl.BlockSpec(memory_space=pltpu.SMEM)
ANY = pl.BlockSpec(memory_space=pl.ANY)
TOKEN = jax.ShapeDtypeStruct((8, 128), jnp.float32)


def near(x):
    return pltpu.with_memory_space_constraint(x, pltpu.VMEM)


def split_kernel(coupling_ref, source_ref, excite_ref, out_ref, token_ref, tiles, sems):
    token_ref[...] = jnp.zeros_like(token_ref)
    copies = []
    for tile in range(8):
        part = excite_ref.at[:, tile * 256 : tile * 256 + 256]
        copies.append(pltpu.make_async_copy(part, tiles.at[tile], sems.at[tile]))
        copies[-1].start()
    lane = lax.broadcasted_iota(jnp.int32, (256, 256), 0)
    goal = lax.broadcasted_iota(jnp.int32, (256, 256), 1)
    source = goal % 128 // 8 * 16 + goal // 128 * 8 + goal % 8
    move = (lane == source).astype(jnp.float32).astype(jnp.bfloat16)
    line = lax.broadcasted_iota(jnp.int32, (16, 256), 0)
    for tile in range(8):
        couple = coupling_ref[lax.axis_index("grp"), tile // 2]
        label = source_ref[:, tile * 256 : tile * 256 + 256] + tile // 2 * 64
        extra = jnp.where(line == 0, label, jnp.where(line == 1, couple, 0))
        copies[tile].wait()
        both = jnp.concatenate([tiles[tile], extra], 0).astype(jnp.float32).astype(jnp.bfloat16)
        moved = jnp.dot(both, move, preferred_element_type=jnp.float32).astype(jnp.bfloat16)
        out_ref[0, :, tile * 128 : tile * 128 + 128] = moved[:, :128]
        out_ref[1, :, tile * 128 : tile * 128 + 128] = moved[:, 128:]


def split_cores(coupling, source, excite):
    return pl.pallas_call(
        split_kernel,
        in_specs=[SMEM, VMEM, ANY],
        out_specs=[VMEM] * 2,
        out_shape=[pltpu.VMEM((2, 528, 1024), jnp.bfloat16), TOKEN],
        scratch_shapes=[pltpu.VMEM((8, 512, 256), jnp.int32), pltpu.SemaphoreType.DMA((8,))],
        compiler_params=pltpu.CompilerParams(vmem_limit_bytes=16 * MIB),
        cost_estimate=pl.CostEstimate(flops=2 * 528 * 2048 * 256, bytes_accessed=7 * MIB, transcendentals=0),
    )(coupling, source, pltpu.with_memory_space_constraint(excite, pltpu.HBM))


def arrange_kernel(order_ref, signs_ref, out_ref, token_ref):
    token_ref[...] = jnp.zeros_like(token_ref)
    blk, core = lax.axis_index("blk"), lax.axis_index("blk") % 2
    y, z, x = lax.axis_index("grp"), blk // 8, blk // 2 % 4

    @pl.loop(0, 8)
    def _(pair):
        dx, dy, dz, place = (jnp.where(core == 0, order_ref[0, i, pair], order_ref[1, i, pair]) for i in range(4))
        chip = (((y + dy) & 3) * NZ + ((z + dz) & 7)) * NX + ((x + dx) & 3)
        line = lax.broadcasted_iota(jnp.int32, (1024, 256), 0)
        move = (line == chip * 8 + place).astype(jnp.float32).astype(jnp.bfloat16)
        owner = jnp.where(pair < 4, core, 1 - core)
        moved = jnp.dot(signs_ref[owner], move, preferred_element_type=jnp.float32)
        out_ref[pair] = moved.astype(jnp.bfloat16)


def arrange(order, signs):
    return pl.pallas_call(
        arrange_kernel,
        in_specs=[VMEM] * 2,
        out_specs=[VMEM] * 2,
        out_shape=[pltpu.VMEM((8, 528, 256), jnp.bfloat16), TOKEN],
        compiler_params=pltpu.CompilerParams(vmem_limit_bytes=16 * MIB),
        cost_estimate=pl.CostEstimate(flops=2 * 528 * 2048 * 1024, bytes_accessed=4 * MIB, transcendentals=0),
    )(order, near(signs))


def lookup_kernel(target_ref, table_ref, signs_ref, out_ref, rows):
    labels = lax.broadcasted_iota(jnp.int32, (64, 512), 0)
    hot = (labels == target_ref[...]).astype(jnp.float32).astype(jnp.bfloat16)
    for part in range(2):
        table = jnp.concatenate([table_ref[:, 2 * h + part, :64] for h in range(4)], 1).astype(jnp.bfloat16)
        row = lax.dot_general(hot, table, (((0,), (0,)), ((), ())), preferred_element_type=jnp.float32)
        rows[part * 512 : part * 512 + 512, :] = row.astype(jnp.bfloat16)

    @pl.loop(0, 8)
    def _(pair):
        lines = lax.broadcasted_iota(jnp.int32, (256, 256), 0)
        extra = signs_ref[pair, 512:528, :].astype(jnp.float32)
        label = extra[0:1, :].astype(jnp.int32)
        pick = jnp.where(lines == label, extra[1:2, :], 0.0).astype(jnp.bfloat16)
        look = jnp.dot(rows[...], pick, preferred_element_type=jnp.float32)
        sign = signs_ref[pair, 0:512, :].astype(jnp.float32)
        for part in range(2):
            value = (look[part * 512 : part * 512 + 512] * sign).astype(jnp.bfloat16)
            for chunk in range(2):
                at = pl.multiple_of(pair * 512 + chunk * 256 + part * 128, 128)
                out_ref[:, pl.ds(at, 128)] = value[:, chunk * 128 : chunk * 128 + 128]


def lookup(target, table, signs):
    return pl.pallas_call(
        lookup_kernel,
        in_specs=[VMEM] * 3,
        out_specs=VMEM,
        out_shape=pltpu.VMEM((512, 4096), jnp.bfloat16),
        scratch_shapes=[pltpu.VMEM((1024, 256), jnp.bfloat16)],
        compiler_params=pltpu.CompilerParams(vmem_limit_bytes=16 * MIB),
        cost_estimate=pl.CostEstimate(flops=10**6, bytes_accessed=MIB, transcendentals=0),
    )(target, near(table), near(signs))


def join_kernel(groups, *refs):
    for group, out_ref in zip(groups, refs[len(refs) - len(groups) :]):
        pieces = [refs[k] for k in group]
        if pieces[0].shape[1] % 16:
            out_ref[...] = jnp.concatenate([piece[...] for piece in pieces], 1)
            continue
        at = 0
        for piece in pieces:
            out_ref[:, at : at + piece.shape[1], :] = piece[...]
            at += piece.shape[1]


def join(pieces, groups, after=()):
    shapes = [(2, sum(pieces[k].shape[1] for k in group), 1024) for group in groups]
    return pl.pallas_call(
        functools.partial(join_kernel, groups),
        in_specs=[VMEM] * len(pieces) + [ANY] * len(after),
        out_specs=[VMEM] * len(groups),
        out_shape=[pltpu.VMEM(shape, jnp.bfloat16) for shape in shapes],
        compiler_params=pltpu.CompilerParams(vmem_limit_bytes=8 * MIB),
        cost_estimate=pl.CostEstimate(flops=0, bytes_accessed=MIB, transcendentals=0),
    )(*[near(p) for p in pieces], *after)


def product_kernel(first, last, starts, count, width, *refs):
    live_ref, left_ref = refs[:2]
    blocks = refs[2 : 2 + count]
    total_ref = None if first else refs[2 + count]
    out_ref, right = refs[-2 - (not last)], refs[-1]
    pieces = [(block, row) for block in blocks for row in range(0, block.shape[1], 128)]
    if not last:
        refs[-2][...] = jnp.zeros_like(refs[-2])

    def columns(n):
        at = pl.ds(pl.multiple_of(n * width, width), width)
        for part in range(2):
            for k, (block, row) in enumerate(pieces):
                right[k * 256 : k * 256 + 128, :] = block[part, row : row + 128, at]
                other = block[1 - part, row : row + 128, at]
                right[k * 256 + 128 : k * 256 + 256, :] = other if part else -other
            acc = None if first else total_ref[part, :, at]
            row = 0
            for start, deep in starts:
                left = left_ref[:, start : start + deep]
                more = jnp.dot(left, right[row : row + deep, :], preferred_element_type=jnp.float32)
                acc = more if acc is None else acc + more
                row += deep
            if last:
                line = lax.broadcasted_iota(jnp.int32, acc.shape, 0)
                out_ref[part] = jnp.where(line < live_ref[0], acc, 0.0)
            else:
                out_ref[part, :, at] = acc

    if last:
        columns(pl.program_id(0))
    else:
        pl.loop(0, 1024 // width)(columns)


def product(live, left, starts, blocks, total, last, flops=10**6, width=512):
    count = len(blocks)
    first = total is None
    arrays = [near(a) for a in [left, *blocks] + ([] if first else [total])]
    shape = (2, 512, 1024)
    if last:
        out = dict(
            grid=(1024 // width,),
            out_specs=pl.BlockSpec((2, 512, width), lambda n: (0, 0, n)),
            out_shape=jax.ShapeDtypeStruct(shape, jnp.float32),
        )
    else:
        out = dict(
            out_specs=[VMEM] * 2,
            out_shape=[pltpu.VMEM(shape, jnp.float32), TOKEN],
        )
        if not first:
            out["input_output_aliases"] = {2 + count: 0}
    deep = sum(2 * b.shape[1] for b in blocks)
    return pl.pallas_call(
        functools.partial(product_kernel, first, last, starts, count, width),
        in_specs=[SMEM] + [VMEM] * len(arrays),
        scratch_shapes=[pltpu.VMEM((deep, width), jnp.bfloat16)],
        compiler_params=pltpu.CompilerParams(vmem_limit_bytes=16 * MIB),
        cost_estimate=pl.CostEstimate(flops=flops, bytes_accessed=MIB, transcendentals=0),
        **out,
    )(live, *arrays)


def spread_kernel(row_ref, after_ref, out_ref):
    del after_ref
    row = row_ref[...]
    row = jnp.concatenate([row, jnp.zeros_like(row)], 1)
    out_ref[...] = jnp.broadcast_to(row[None], out_ref.shape)


def spread(row, after):
    return pl.pallas_call(
        spread_kernel,
        in_specs=[VMEM] * 2,
        out_specs=VMEM,
        out_shape=jax.ShapeDtypeStruct((64, 8, 128), jnp.float32),
        cost_estimate=pl.CostEstimate(flops=10**6, bytes_accessed=MIB, transcendentals=0),
    )(row, near(after))


def on_device(coeffs, coupling, one_body, target_orb, source_orb, excite, live_rows):
    signs, token = split_cores(coupling, source_orb[None, :], excite)
    slab = join([coeffs] + fetch(coeffs, 0), [(0, 1)], [token])[0]

    table = lax.all_to_all(spread(one_body.reshape(8, 64), slab), "blk", 0, 0, tiled=True)

    slab = join([slab] + fetch(slab, 1), [(0, 1, 2, 3)], [table])[0]
    arranged, token = arrange(ORDER, signs)
    halves = list(join([slab] + fetch(slab, 2), [(0, 1), (2, 3)], [token]))
    left = lookup(target_orb[None, :], table, arranged)

    got = [fetch(half, 3) for half in halves]
    own = halves + [swap(half) for half in halves]
    total, token = product(live_rows, left, ((0, 512), (2048, 512)), own, None, False)
    first = join(got[0], [(0, 1, 2)], [token])[0]
    their_first = swap(first)
    total, token = product(live_rows, left, ((512, 768),), [first], total, False)
    second = join(got[1], [(0, 1, 2)], [token])[0]
    their_second = swap(second)
    total, _ = product(live_rows, left, ((2560, 768), (1280, 768)), [their_first, second], total, False)
    return product(live_rows, left, ((3328, 768),), [their_second], total, True)


def solution(mesh):
    from jax.sharding import PartitionSpec as P

    return jax.shard_map(
        on_device,
        mesh=mesh,
        in_specs=(
            P(None, ("grp", "blk"), None),
            P(),
            P("grp", None, None, "blk", None),
            P(("grp", "blk")),
            P(),
            P(("grp", "blk"), None),
            P(("grp", "blk")),
        ),
        out_specs=P(None, ("grp", "blk"), None),
        check_vma=False,
    )
```

time: 130 us -> 80.7 us (0.62)
  blocking collectives: 68.3 us -> 0 us
  starting transfers between devices: 0.01 us -> 38.6 us
  Pallas kernels: 0 us -> 24.9 us
  matrix products: 17 us -> 0 us
  between operations: 14.1 us -> 0.81 us
  other arithmetic: 5.97 us -> 0 us
  local copies, waits for them, and re-layouts: 6.48 us -> 1.39 us
  waiting for transfers between devices: 17.7 us -> 14.7 us
    all_gather x2 -> x0, blocking collectives: 68.3 us -> none  [the longest x1 55.9 us: on_device(): lax.all_gather(one_body, 'blk', axis=3, tiled=True)[0].astype(jnp.bfloat16)]
    ppermute x0 -> x17, starting transfers between devices: none -> 30.7 us  [the longest x13 26.1 us: fetch(): return [lax.ppermute(block, AXES, route(o)) for o in STAGES[stage]]]
    pallas_call x0 -> x13, Pallas kernels: none -> 24.9 us  [the longest x4 11.9 us: product(): pl.pallas_call(functools.partial(product_kernel, first, last, starts, cou...]
    all_gather x1 -> x0, waiting for transfers between devices: 17.7 us -> none  [on_device(): lax.all_gather(slabs, 'blk', axis=2, tiled=True).reshape(2, -1, beta_count)]
    dot_general x5 -> x0, matrix products: 17 us -> none  [the longest x1 5.31 us: on_device(): jnp.dot(part[0], merged[0], preferred_element_type=jnp.float32)]
    ppermute x0 -> x17, waiting for transfers between devices: none -> 14.1 us  [the longest x13 13.6 us: fetch(): return [lax.ppermute(block, AXES, route(o)) for o in STAGES[stage]]]
    all_to_all x0 -> x1, starting transfers between devices: none -> 7.89 us  [on_device(): lax.all_to_all(spread(one_body.reshape(8, 64), slab), 'blk', 0, 0, tiled=...]
    reshape x1 -> x0, local copies, waits for them, and re-layouts: 5.35 us -> none  [on_device(): excite.reshape(block_rows, group_count, per_group)]
  transfers between devices with their start and end apart: 1 -> 18, of which waited for: 1 -> 5; matrix products, arithmetic and copies ran while one was open for 10% -> 0% of each run, Pallas kernels for 0% -> 25%
where the time goes in v2:
time: 80.7 us; the launch traced here: 80.5 us
  starting transfers between devices  38.6 us (48%)
  Pallas kernels  24.9 us (31%)
  waiting for transfers between devices  14.7 us (18%)
  local copies, waits for them, and re-layouts  1.39 us (2%)
  between operations  0.81 us (1%)
    ppermute x13, starting transfers between devices, fetch(): return [lax.ppermute(block, AXES, route(o)) for o in STAGES[stage]]  26.1 us
    ppermute x13, waiting for transfers between devices, fetch(): return [lax.ppermute(block, AXES, route(o)) for o in STAGES[stage]]  13.6 us
    pallas_call x4, Pallas kernels, product(): pl.pallas_call(functools.partial(product_kernel, first, last, starts, cou...  11.9 us
    all_to_all x1, starting transfers between devices, on_device(): lax.all_to_all(spread(one_body.reshape(8, 64), slab), 'blk', 0, 0, tiled=...  7.89 us
    ppermute x4, starting transfers between devices, swap(): return lax.ppermute(block, AXES, SWAP)  4.62 us
    pallas_call x1, Pallas kernels, split_cores(): pl.pallas_call(split_kernel, in_specs=[SMEM, VMEM, ANY], out_specs=[VMEM]...  3.98 us
    pallas_call x1, Pallas kernels, arrange(): pl.pallas_call(arrange_kernel, in_specs=[VMEM] * 2, out_specs=[VMEM] * 2,...  3.7 us
    pallas_call x1, Pallas kernels, lookup(): pl.pallas_call(lookup_kernel, in_specs=[VMEM] * 3, out_specs=VMEM, out_sh...  3.69 us
  transfers between devices with their start and end apart: 18, of which 5 were waited for; matrix products, arithmetic and copies ran while one was open for 0% of the time, Pallas kernels for 25%

profile of v2, /device:TPU:1, one launch (start us, length us, event | category | flops | bytes accessed | tf_op | source)
XLA Modules:
  0.0 80.5 jit_solution(144518571363821020)
XLA Ops:
  0.0 0.0 copy-start
  0.0 7.7 %collective-permute-start = (bf16[2,8,1024]{2,1,0:T(8,128)(2,1)}, bf16[2,8,1024]{2,1,0:T(8,128)(2,1)S(1)}, u32[]{:S(2)}, u32[]{:S(2)}) collective-permute-start(bf16[2,8,1024]{2,1,0:T(8,128)(2,1)} %refs_0_.5), channel_id=1, source_target_pairs={{32,0},{33,1},{34,2},{35,3},{36,4},{37,5},{38,6},{39,7},{40,8},{41... | collective-permute-start | bytes 98312 | tf_op jit(solution)/shard_map/ppermute | solution.py:43
  7.7 0.0 copy-start.1
  7.7 0.7 copy-done.1
  8.4 0.0 copy-start.2
  8.4 0.7 copy-done.2
  9.1 0.0 copy-start.4
  9.1 4.0 %shard_map.82 = (bf16[2,528,1024]{2,1,0:T(8,128)(2,1)S(1)}, f32[8,128]{1,0:T(8,128)S(1)}) custom-call(s32[4,4]{1,0:T(4,128)S(1)} %copy-done.2, s32[1,2048]{1,0:T(1,128)S(1)} %bitcast.3, s32[512,2048]{1,0:T(8,128)} %excite_ref.1), custom_call_target="tpu_custom_call" | custom-call | flops 553648128 | bytes 7340032 | tf_op jit(solution)/shard_map/pallas_call | solution.py:111
  13.1 0.0 collective-permute-done.refs_1_
  13.1 0.0 copy-done
  13.1 1.4 %shard_map.84 = f32[64,8,128]{2,1,0:T(8,128)} custom-call(f32[8,64]{1,0:T(8,128)} %bitcast.5, bf16[2,16,1024]{2,1,0:T(8,128)(2,1)S(1)} %shard_map.83.after_ref.refs_0_), custom_call_target="tpu_custom_call" | custom-call | flops 1000000 | bytes 1048576 | tf_op jit(solution)/shard_map/pallas_call | solution.py:280
  14.6 7.9 %all-to-all-start = ((f32[64,8,128]{2,1,0:T(8,128)}), f32[64,8,128]{2,1,0:T(8,128)S(1)}, u32[]{:S(2)}, u32[]{:S(2)}) async-start(f32[64,8,128]{2,1,0:T(8,128)} %shard_map.84), calls=%async_computation | async-start | bytes 524288 | tf_op jit(solution)/shard_map/all_to_all | solution.py:293
  22.5 4.1 %collective-permute-start.1 = (bf16[2,16,1024]{2,1,0:T(8,128)(2,1)S(1)}, bf16[2,16,1024]{2,1,0:T(8,128)(2,1)S(1)}, u32[]{:S(2)}, u32[]{:S(2)}) collective-permute-start(bf16[2,16,1024]{2,1,0:T(8,128)(2,1)S(1)} %shard_map.83.after_ref.refs_0_), channel_id=1, source_target_pairs={{12,0},{185,1},{14,2},{187,3},{8,4},{189,5},{10,6},{191,7},{20,8},... | collective-permute-start | bytes 196616 | tf_op jit(solution)/shard_map/ppermute | solution.py:43
  26.6 2.1 %collective-permute-start.2 = (bf16[2,16,1024]{2,1,0:T(8,128)(2,1)S(1)}, bf16[2,16,1024]{2,1,0:T(8,128)(2,1)S(1)}, u32[]{:S(2)}, u32[]{:S(2)}) collective-permute-start(bf16[2,16,1024]{2,1,0:T(8,128)(2,1)S(1)} %shard_map.83.after_ref.refs_0_), channel_id=1, source_target_pairs={{16,0},{49,1},{18,2},{51,3},{20,4},{53,5},{22,6},{55,7},{24,8},{57... | collective-permute-start | bytes 196616 | tf_op jit(solution)/shard_map/ppermute | solution.py:43
  28.7 1.2 %collective-permute-start.3 = (bf16[2,16,1024]{2,1,0:T(8,128)(2,1)S(1)}, bf16[2,16,1024]{2,1,0:T(8,128)(2,1)S(1)}, u32[]{:S(2)}, u32[]{:S(2)}) collective-permute-start(bf16[2,16,1024]{2,1,0:T(8,128)(2,1)S(1)} %shard_map.83.after_ref.refs_0_), channel_id=1, source_target_pairs={{60,0},{137,1},{62,2},{139,3},{56,4},{141,5},{58,6},{143,7},{4,8},... | collective-permute-start | bytes 196616 | tf_op jit(solution)/shard_map/ppermute | solution.py:43
  29.9 5.0 %collective-permute-done.1.refs_1_ = bf16[2,16,1024]{2,1,0:T(8,128)(2,1)S(1)} collective-permute-done((bf16[2,16,1024]{2,1,0:T(8,128)(2,1)S(1)}, bf16[2,16,1024]{2,1,0:T(8,128)(2,1)S(1)}, u32[]{:S(2)}, u32[]{:S(2)}) %collective-permute-start.1) | collective-permute-done | bytes 65568 | tf_op jit(solution)/shard_map/ppermute | solution.py:43
  34.9 0.0 collective-permute-done.2.refs_2_
  34.9 0.0 collective-permute-done.3.refs_3_
  34.9 0.7 all-to-all-done.table_ref.refs_4_
  35.6 3.4 %collective-permute-start.4 = (bf16[2,64,1024]{2,1,0:T(8,128)(2,1)S(1)}, bf16[2,64,1024]{2,1,0:T(8,128)(2,1)S(1)}, u32[]{:S(2)}, u32[]{:S(2)}) collective-permute-start(bf16[2,64,1024]{2,1,0:T(8,128)(2,1)S(1)} %shard_map.87.refs_0_), channel_id=1, source_target_pairs={{72,0},{59,1},{74,2},{61,3},{76,4},{63,5},{78,6},{57,7},{80,8},{3,... | collective-permute-start | bytes 786440 | tf_op jit(solution)/shard_map/ppermute | solution.py:43
  39.1 0.8 collective-permute-start.5
  39.9 0.7 collective-permute-start.6
  40.5 0.0 copy-done.4
  40.5 0.0 copy-start.3
  40.5 3.7 %shard_map.85 = (bf16[8,528,256]{2,1,0:T(8,128)(2,1)S(1)}, f32[8,128]{1,0:T(8,128)S(1)}) custom-call(s32[2,4,8,1,256]{4,3,2,1,0:T(1,128)S(1)} %copy-done.4, bf16[2,528,1024]{2,1,0:T(8,128)(2,1)S(1)} %get-tuple-element.17.signs_ref), custom_call_target="tpu_custom_call" | custom-call | flops 2214592512 | bytes 4194304 | tf_op jit(solution)/shard_map/pallas_call | solution.py:139
  44.2 0.0 collective-permute-done.4.refs_1_
  44.3 4.7 %collective-permute-done.5.refs_2_ = bf16[2,64,1024]{2,1,0:T(8,128)(2,1)S(1)} collective-permute-done((bf16[2,64,1024]{2,1,0:T(8,128)(2,1)S(1)}, bf16[2,64,1024]{2,1,0:T(8,128)(2,1)S(1)}, u32[]{:S(2)}, u32[]{:S(2)}) %collective-permute-start.5) | collective-permute-done | bytes 262176 | tf_op jit(solution)/shard_map/ppermute | solution.py:43
  48.9 0.0 collective-permute-done.6.refs_3_
  48.9 0.1 shard_map.88
  49.0 3.8 %collective-permute-start.13 = (bf16[2,128,1024]{2,1,0:T(8,128)(2,1)S(1)}, bf16[2,128,1024]{2,1,0:T(8,128)(2,1)S(1)}, u32[]{:S(2)}, u32[]{:S(2)}) collective-permute-start(bf16[2,128,1024]{2,1,0:T(8,128)(2,1)S(1)} %get-tuple-element.21.refs_2_), channel_id=1, source_target_pairs={{0,1},{1,0},{2,3},{3,2},{4,5},{5,4},{6,7},{7,6},{8,9},{9,8},{10,11... | collective-permute-start | bytes 1572872 | tf_op jit(solution)/shard_map/ppermute | solution.py:47
  52.8 0.1 collective-permute-start.14
  52.9 0.1 collective-permute-start.10
  53.0 1.4 %collective-permute-start.11 = (bf16[2,128,1024]{2,1,0:T(8,128)(2,1)S(1)}, bf16[2,128,1024]{2,1,0:T(8,128)(2,1)S(1)}, u32[]{:S(2)}, u32[]{:S(2)}) collective-permute-start(bf16[2,128,1024]{2,1,0:T(8,128)(2,1)S(1)} %get-tuple-element.21.refs_2_), channel_id=1, source_target_pairs={{6,0},{193,1},{0,2},{195,3},{2,4},{197,5},{4,6},{199,7},{14,8},{20... | collective-permute-start | bytes 1572872 | tf_op jit(solution)/shard_map/ppermute | solution.py:43
  54.4 1.5 %collective-permute-start.12 = (bf16[2,128,1024]{2,1,0:T(8,128)(2,1)S(1)}, bf16[2,128,1024]{2,1,0:T(8,128)(2,1)S(1)}, u32[]{:S(2)}, u32[]{:S(2)}) collective-permute-start(bf16[2,128,1024]{2,1,0:T(8,128)(2,1)S(1)} %get-tuple-element.21.refs_2_), channel_id=1, source_target_pairs={{8,0},{57,1},{10,2},{59,3},{12,4},{61,5},{14,6},{63,7},{16,8},{1,9... | collective-permute-start | bytes 1572872 | tf_op jit(solution)/shard_map/ppermute | solution.py:43
  55.9 0.0 collective-permute-done.13.refs_4_
  55.9 1.2 %collective-permute-start.7 = (bf16[2,128,1024]{2,1,0:T(8,128)(2,1)S(1)}, bf16[2,128,1024]{2,1,0:T(8,128)(2,1)S(1)}, u32[]{:S(2)}, u32[]{:S(2)}) collective-permute-start(bf16[2,128,1024]{2,1,0:T(8,128)(2,1)S(1)} %get-tuple-element.20.refs_3_), channel_id=1, source_target_pairs={{2,0},{65,1},{4,2},{67,3},{6,4},{69,5},{0,6},{71,7},{10,8},{73,9},... | collective-permute-start | bytes 1572872 | tf_op jit(solution)/shard_map/ppermute | solution.py:43
  57.1 0.0 collective-permute-done.14.refs_5_
  57.2 0.3 collective-permute-start.8
  57.4 3.9 %collective-permute-done.10.refs_0_ = bf16[2,128,1024]{2,1,0:T(8,128)(2,1)S(1)} collective-permute-done((bf16[2,128,1024]{2,1,0:T(8,128)(2,1)S(1)}, bf16[2,128,1024]{2,1,0:T(8,128)(2,1)S(1)}, u32[]{:S(2)}, u32[]{:S(2)}) %collective-permute-start.10) | collective-permute-done | bytes 524320 | tf_op jit(solution)/shard_map/ppermute | solution.py:43
  61.3 1.5 %collective-permute-start.9 = (bf16[2,128,1024]{2,1,0:T(8,128)(2,1)S(1)}, bf16[2,128,1024]{2,1,0:T(8,128)(2,1)S(1)}, u32[]{:S(2)}, u32[]{:S(2)}) collective-permute-start(bf16[2,128,1024]{2,1,0:T(8,128)(2,1)S(1)} %get-tuple-element.20.refs_3_), channel_id=1, source_target_pairs={{8,0},{57,1},{10,2},{59,3},{12,4},{61,5},{14,6},{63,7},{16,8},{1,9... | collective-permute-start | bytes 1572872 | tf_op jit(solution)/shard_map/ppermute | solution.py:43
  63.4 0.0 copy-done.3
  63.5 3.7 %shard_map.86.refs_1_ = bf16[512,4096]{1,0:T(8,128)(2,1)S(1)} custom-call(s32[1,512]{1,0:T(1,128)S(1)} %bitcast.4, f32[64,8,128]{2,1,0:T(8,128)S(1)} %all-to-all-done.table_ref.refs_4_, bf16[8,528,256]{2,1,0:T(8,128)(2,1)S(1)} %get-tuple-element.18.signs_ref), custom_call_target="tpu_custom_call" | custom-call | flops 1000000 | bytes 1048576 | tf_op jit(solution)/shard_map/pallas_call | solution.py:173
  67.2 2.5 %shard_map.89 = (f32[2,512,1024]{2,1,0:T(8,128)S(1)}, f32[8,128]{1,0:T(8,128)S(1)}) custom-call(s32[1]{0:T(128)S(6)} %copy.13.refs_0_, bf16[512,4096]{1,0:T(8,128)(2,1)S(1)} %shard_map.86.refs_1_, bf16[2,128,1024]{2,1,0:T(8,128)(2,1)S(1)} %get-tuple-element.21.refs_2_, bf16[2,128,1024]{2,1,0:T(8,128)(2,1)S(1)} %get-tuple-element.20.refs_3_, ...), custom_call_target="tpu_custom_call" | custom-call | flops 1000000 | bytes 1048576 | tf_op jit(solution)/shard_map/pallas_call | solution.py:262
  69.7 0.0 collective-permute-done.11.refs_1_
  69.7 0.0 collective-permute-done.12.refs_2_
  69.7 0.1 shard_map.90.refs_2_
  69.8 0.2 collective-permute-start.16
  70.0 2.2 %shard_map.91 = (f32[2,512,1024]{2,1,0:T(8,128)S(1)}, f32[8,128]{1,0:T(8,128)S(1)}) custom-call(s32[1]{0:T(128)S(6)} %copy.13.refs_0_, bf16[512,4096]{1,0:T(8,128)(2,1)S(1)} %shard_map.86.refs_1_, bf16[2,384,1024]{2,1,0:T(8,128)(2,1)S(1)} %shard_map.90.refs_2_, f32[2,512,1024]{2,1,0:T(8,128)S(1)} %get-tuple-element.23.refs_3_), custom_call_target="tpu_custom_call", output_to_operand_aliasing={{0}: (3, {})} | custom-call | flops 1000000 | bytes 1048576 | tf_op jit(solution)/shard_map/pallas_call | solution.py:262
  72.2 0.0 collective-permute-done.7.refs_0_
  72.2 0.0 collective-permute-done.8.refs_1_
  72.2 0.0 collective-permute-done.9.refs_2_
  72.2 0.1 shard_map.92.refs_3_
  72.3 0.5 collective-permute-start.15
  72.8 0.5 collective-permute-done.16.refs_2_
  73.3 3.8 %shard_map.93 = (f32[2,512,1024]{2,1,0:T(8,128)S(1)}, f32[8,128]{1,0:T(8,128)}) custom-call(s32[1]{0:T(128)S(6)} %copy.13.refs_0_, bf16[512,4096]{1,0:T(8,128)(2,1)S(1)} %shard_map.86.refs_1_, bf16[2,384,1024]{2,1,0:T(8,128)(2,1)S(1)} %collective-permute-done.16.refs_2_, ...), custom_call_target="tpu_custom_call", output_to_operand_aliasing={{0}: (4, {})} | custom-call | flops 1000000 | bytes 1048576 | tf_op jit(solution)/shard_map/pallas_call | solution.py:262
  77.1 0.0 collective-permute-done.15.refs_2_
  77.1 3.3 %shard_map.94 = f32[2,512,1024]{2,1,0:T(8,128)} custom-call(s32[1]{0:T(128)S(6)} %copy.13.refs_0_, bf16[512,4096]{1,0:T(8,128)(2,1)S(1)} %shard_map.86.refs_1_, bf16[2,384,1024]{2,1,0:T(8,128)(2,1)S(1)} %collective-permute-done.15.refs_2_, f32[2,512,1024]{2,1,0:T(8,128)S(1)} %get-tuple-element.26.refs_3_), custom_call_target="tpu_custom_call" | custom-call | flops 1000000 | bytes 1048576 | tf_op jit(solution)/shard_map/pallas_call | solution.py:262
  (2 shorter events, 0.0 us)
Async XLA Ops:
  0.0 13.1 %copy-start = (bf16[2,8,1024]{2,1,0:T(8,128)(2,1)S(1)}, bf16[2,8,1024]{2,1,0:T(8,128)(2,1)}, u32[]{:S(2)}) copy-start(bf16[2,8,1024]{2,1,0:T(8,128)(2,1)} %refs_0_.5) | copy-start | bytes 98308
  0.0 13.1 %collective-permute-start = (bf16[2,8,1024]{2,1,0:T(8,128)(2,1)}, bf16[2,8,1024]{2,1,0:T(8,128)(2,1)S(1)}, u32[]{:S(2)}, u32[]{:S(2)}) collective-permute-start(bf16[2,8,1024]{2,1,0:T(8,128)(2,1)} %refs_0_.5), channel_id=1, source_target_pairs={{32,0},{33,1},{34,2},{35,3},{36,4},{37,5},{38,6},{39,7},{40,8},{41... | collective-permute-start | bytes 98312 | tf_op jit(solution)/shard_map/ppermute | solution.py:43
  7.7 0.7 copy-start.1
  8.4 0.7 copy-start.2
  9.1 31.4 %copy-start.4 = (s32[2,4,8,1,256]{4,3,2,1,0:T(1,128)S(1)}, s32[2,4,8,1,256]{4,3,2,1,0:T(1,128)}, u32[]{:S(2)}) copy-start(s32[2,4,8,1,256]{4,3,2,1,0:T(1,128)} %constant.2.clone.order_ref) | copy-start | bytes 196612
  14.6 21.1 %all-to-all-start = ((f32[64,8,128]{2,1,0:T(8,128)}), f32[64,8,128]{2,1,0:T(8,128)S(1)}, u32[]{:S(2)}, u32[]{:S(2)}) async-start(f32[64,8,128]{2,1,0:T(8,128)} %shard_map.84), calls=%async_computation | async-start | bytes 524288 | tf_op jit(solution)/shard_map/all_to_all | solution.py:293
  22.5 12.5 %collective-permute-start.1 = (bf16[2,16,1024]{2,1,0:T(8,128)(2,1)S(1)}, bf16[2,16,1024]{2,1,0:T(8,128)(2,1)S(1)}, u32[]{:S(2)}, u32[]{:S(2)}) collective-permute-start(bf16[2,16,1024]{2,1,0:T(8,128)(2,1)S(1)} %shard_map.83.after_ref.refs_0_), channel_id=1, source_target_pairs={{12,0},{185,1},{14,2},{187,3},{8,4},{189,5},{10,6},{191,7},{20,8},... | collective-permute-start | bytes 196616 | tf_op jit(solution)/shard_map/ppermute | solution.py:43
  26.6 8.4 %collective-permute-start.2 = (bf16[2,16,1024]{2,1,0:T(8,128)(2,1)S(1)}, bf16[2,16,1024]{2,1,0:T(8,128)(2,1)S(1)}, u32[]{:S(2)}, u32[]{:S(2)}) collective-permute-start(bf16[2,16,1024]{2,1,0:T(8,128)(2,1)S(1)} %shard_map.83.after_ref.refs_0_), channel_id=1, source_target_pairs={{16,0},{49,1},{18,2},{51,3},{20,4},{53,5},{22,6},{55,7},{24,8},{57... | collective-permute-start | bytes 196616 | tf_op jit(solution)/shard_map/ppermute | solution.py:43
  28.7 6.3 %collective-permute-start.3 = (bf16[2,16,1024]{2,1,0:T(8,128)(2,1)S(1)}, bf16[2,16,1024]{2,1,0:T(8,128)(2,1)S(1)}, u32[]{:S(2)}, u32[]{:S(2)}) collective-permute-start(bf16[2,16,1024]{2,1,0:T(8,128)(2,1)S(1)} %shard_map.83.after_ref.refs_0_), channel_id=1, source_target_pairs={{60,0},{137,1},{62,2},{139,3},{56,4},{141,5},{58,6},{143,7},{4,8},... | collective-permute-start | bytes 196616 | tf_op jit(solution)/shard_map/ppermute | solution.py:43
  35.6 8.6 %collective-permute-start.4 = (bf16[2,64,1024]{2,1,0:T(8,128)(2,1)S(1)}, bf16[2,64,1024]{2,1,0:T(8,128)(2,1)S(1)}, u32[]{:S(2)}, u32[]{:S(2)}) collective-permute-start(bf16[2,64,1024]{2,1,0:T(8,128)(2,1)S(1)} %shard_map.87.refs_0_), channel_id=1, source_target_pairs={{72,0},{59,1},{74,2},{61,3},{76,4},{63,5},{78,6},{57,7},{80,8},{3,... | collective-permute-start | bytes 786440 | tf_op jit(solution)/shard_map/ppermute | solution.py:43
  39.1 9.8 %collective-permute-start.5 = (bf16[2,64,1024]{2,1,0:T(8,128)(2,1)S(1)}, bf16[2,64,1024]{2,1,0:T(8,128)(2,1)S(1)}, u32[]{:S(2)}, u32[]{:S(2)}) collective-permute-start(bf16[2,64,1024]{2,1,0:T(8,128)(2,1)S(1)} %shard_map.87.refs_0_), channel_id=1, source_target_pairs={{128,0},{5,1},{130,2},{7,3},{132,4},{1,5},{134,6},{3,7},{136,8},{1... | collective-permute-start | bytes 786440 | tf_op jit(solution)/shard_map/ppermute | solution.py:43
  39.9 9.0 %collective-permute-start.6 = (bf16[2,64,1024]{2,1,0:T(8,128)(2,1)S(1)}, bf16[2,64,1024]{2,1,0:T(8,128)(2,1)S(1)}, u32[]{:S(2)}, u32[]{:S(2)}) collective-permute-start(bf16[2,64,1024]{2,1,0:T(8,128)(2,1)S(1)} %shard_map.87.refs_0_), channel_id=1, source_target_pairs={{200,0},{63,1},{202,2},{57,3},{204,4},{59,5},{206,6},{61,7},{208,8... | collective-permute-start | bytes 786440 | tf_op jit(solution)/shard_map/ppermute | solution.py:43
  40.5 22.9 %copy-start.3 = (s32[512]{0:T(512)S(1)}, s32[512]{0:T(512)}, u32[]{:S(2)}) copy-start(s32[512]{0:T(512)} %param.11) | copy-start | bytes 6148
  49.0 6.9 %collective-permute-start.13 = (bf16[2,128,1024]{2,1,0:T(8,128)(2,1)S(1)}, bf16[2,128,1024]{2,1,0:T(8,128)(2,1)S(1)}, u32[]{:S(2)}, u32[]{:S(2)}) collective-permute-start(bf16[2,128,1024]{2,1,0:T(8,128)(2,1)S(1)} %get-tuple-element.21.refs_2_), channel_id=1, source_target_pairs={{0,1},{1,0},{2,3},{3,2},{4,5},{5,4},{6,7},{7,6},{8,9},{9,8},{10,11... | collective-permute-start | bytes 1572872 | tf_op jit(solution)/shard_map/ppermute | solution.py:47
  52.8 4.3 %collective-permute-start.14 = (bf16[2,128,1024]{2,1,0:T(8,128)(2,1)S(1)}, bf16[2,128,1024]{2,1,0:T(8,128)(2,1)S(1)}, u32[]{:S(2)}, u32[]{:S(2)}) collective-permute-start(bf16[2,128,1024]{2,1,0:T(8,128)(2,1)S(1)} %get-tuple-element.20.refs_3_), channel_id=1, source_target_pairs={{0,1},{1,0},{2,3},{3,2},{4,5},{5,4},{6,7},{7,6},{8,9},{9,8},{10,11... | collective-permute-start | bytes 1572872 | tf_op jit(solution)/shard_map/ppermute | solution.py:47
  52.9 8.3 %collective-permute-start.10 = (bf16[2,128,1024]{2,1,0:T(8,128)(2,1)S(1)}, bf16[2,128,1024]{2,1,0:T(8,128)(2,1)S(1)}, u32[]{:S(2)}, u32[]{:S(2)}) collective-permute-start(bf16[2,128,1024]{2,1,0:T(8,128)(2,1)S(1)} %get-tuple-element.21.refs_2_), channel_id=1, source_target_pairs={{2,0},{65,1},{4,2},{67,3},{6,4},{69,5},{0,6},{71,7},{10,8},{73,9},... | collective-permute-start | bytes 1572872 | tf_op jit(solution)/shard_map/ppermute | solution.py:43
  53.0 16.7 %collective-permute-start.11 = (bf16[2,128,1024]{2,1,0:T(8,128)(2,1)S(1)}, bf16[2,128,1024]{2,1,0:T(8,128)(2,1)S(1)}, u32[]{:S(2)}, u32[]{:S(2)}) collective-permute-start(bf16[2,128,1024]{2,1,0:T(8,128)(2,1)S(1)} %get-tuple-element.21.refs_2_), channel_id=1, source_target_pairs={{6,0},{193,1},{0,2},{195,3},{2,4},{197,5},{4,6},{199,7},{14,8},{20... | collective-permute-start | bytes 1572872 | tf_op jit(solution)/shard_map/ppermute | solution.py:43
  54.4 15.3 %collective-permute-start.12 = (bf16[2,128,1024]{2,1,0:T(8,128)(2,1)S(1)}, bf16[2,128,1024]{2,1,0:T(8,128)(2,1)S(1)}, u32[]{:S(2)}, u32[]{:S(2)}) collective-permute-start(bf16[2,128,1024]{2,1,0:T(8,128)(2,1)S(1)} %get-tuple-element.21.refs_2_), channel_id=1, source_target_pairs={{8,0},{57,1},{10,2},{59,3},{12,4},{61,5},{14,6},{63,7},{16,8},{1,9... | collective-permute-start | bytes 1572872 | tf_op jit(solution)/shard_map/ppermute | solution.py:43
  55.9 16.2 %collective-permute-start.7 = (bf16[2,128,1024]{2,1,0:T(8,128)(2,1)S(1)}, bf16[2,128,1024]{2,1,0:T(8,128)(2,1)S(1)}, u32[]{:S(2)}, u32[]{:S(2)}) collective-permute-start(bf16[2,128,1024]{2,1,0:T(8,128)(2,1)S(1)} %get-tuple-element.20.refs_3_), channel_id=1, source_target_pairs={{2,0},{65,1},{4,2},{67,3},{6,4},{69,5},{0,6},{71,7},{10,8},{73,9},... | collective-permute-start | bytes 1572872 | tf_op jit(solution)/shard_map/ppermute | solution.py:43
  57.2 15.0 %collective-permute-start.8 = (bf16[2,128,1024]{2,1,0:T(8,128)(2,1)S(1)}, bf16[2,128,1024]{2,1,0:T(8,128)(2,1)S(1)}, u32[]{:S(2)}, u32[]{:S(2)}) collective-permute-start(bf16[2,128,1024]{2,1,0:T(8,128)(2,1)S(1)} %get-tuple-element.20.refs_3_), channel_id=1, source_target_pairs={{6,0},{193,1},{0,2},{195,3},{2,4},{197,5},{4,6},{199,7},{14,8},{20... | collective-permute-start | bytes 1572872 | tf_op jit(solution)/shard_map/ppermute | solution.py:43
  61.3 10.9 %collective-permute-start.9 = (bf16[2,128,1024]{2,1,0:T(8,128)(2,1)S(1)}, bf16[2,128,1024]{2,1,0:T(8,128)(2,1)S(1)}, u32[]{:S(2)}, u32[]{:S(2)}) collective-permute-start(bf16[2,128,1024]{2,1,0:T(8,128)(2,1)S(1)} %get-tuple-element.20.refs_3_), channel_id=1, source_target_pairs={{8,0},{57,1},{10,2},{59,3},{12,4},{61,5},{14,6},{63,7},{16,8},{1,9... | collective-permute-start | bytes 1572872 | tf_op jit(solution)/shard_map/ppermute | solution.py:43
  69.8 3.5 %collective-permute-start.16 = (bf16[2,384,1024]{2,1,0:T(8,128)(2,1)S(1)}, bf16[2,384,1024]{2,1,0:T(8,128)(2,1)S(1)}, u32[]{:S(2)}, u32[]{:S(2)}) collective-permute-start(bf16[2,384,1024]{2,1,0:T(8,128)(2,1)S(1)} %shard_map.90.refs_2_), channel_id=1, source_target_pairs={{0,1},{1,0},{2,3},{3,2},{4,5},{5,4},{6,7},{7,6},{8,9},{9,8},{10,11... | collective-permute-start | bytes 4718600 | tf_op jit(solution)/shard_map/ppermute | solution.py:47
  72.3 4.8 %collective-permute-start.15 = (bf16[2,384,1024]{2,1,0:T(8,128)(2,1)S(1)}, bf16[2,384,1024]{2,1,0:T(8,128)(2,1)S(1)}, u32[]{:S(2)}, u32[]{:S(2)}) collective-permute-start(bf16[2,384,1024]{2,1,0:T(8,128)(2,1)S(1)} %shard_map.92.refs_3_), channel_id=1, source_target_pairs={{0,1},{1,0},{2,3},{3,2},{4,5},{5,4},{6,7},{7,6},{8,9},{9,8},{10,11... | collective-permute-start | bytes 4718600 | tf_op jit(solution)/shard_map/ppermute | solution.py:47

commit v3 on v2

--- a/solution.py
+++ b/solution.py
@@ -84,8 +84,14 @@
     return pltpu.with_memory_space_constraint(x, pltpu.VMEM)
 
 
-def split_kernel(coupling_ref, source_ref, excite_ref, out_ref, token_ref, tiles, sems):
+def split_kernel(coupling_ref, source_ref, excite_ref, out_ref, token_ref, tiles, labels, couples, sems):
     token_ref[...] = jnp.zeros_like(token_ref)
+    small = [
+        pltpu.make_async_copy(coupling_ref, couples, sems.at[8]),
+        pltpu.make_async_copy(source_ref, labels, sems.at[9]),
+    ]
+    for copy in small:
+        copy.start()
     copies = []
     for tile in range(8):
         part = excite_ref.at[:, tile * 256 : tile * 256 + 256]
@@ -96,9 +102,11 @@
     source = goal % 128 // 8 * 16 + goal // 128 * 8 + goal % 8
     move = (lane == source).astype(jnp.float32).astype(jnp.bfloat16)
     line = lax.broadcasted_iota(jnp.int32, (16, 256), 0)
+    for copy in small:
+        copy.wait()
     for tile in range(8):
-        couple = coupling_ref[lax.axis_index("grp"), tile // 2]
-        label = source_ref[:, tile * 256 : tile * 256 + 256] + tile // 2 * 64
+        couple = couples[lax.axis_index("grp"), tile // 2]
+        label = labels[:, tile * 256 : tile * 256 + 256] + tile // 2 * 64
         extra = jnp.where(line == 0, label, jnp.where(line == 1, couple, 0))
         copies[tile].wait()
         both = jnp.concatenate([tiles[tile], extra], 0).astype(jnp.float32).astype(jnp.bfloat16)
@@ -110,13 +118,18 @@
 def split_cores(coupling, source, excite):
     return pl.pallas_call(
         split_kernel,
-        in_specs=[SMEM, VMEM, ANY],
+        in_specs=[ANY] * 3,
         out_specs=[VMEM] * 2,
         out_shape=[pltpu.VMEM((2, 528, 1024), jnp.bfloat16), TOKEN],
-        scratch_shapes=[pltpu.VMEM((8, 512, 256), jnp.int32), pltpu.SemaphoreType.DMA((8,))],
+        scratch_shapes=[
+            pltpu.VMEM((8, 512, 256), jnp.int32),
+            pltpu.VMEM((1, 2048), jnp.int32),
+            pltpu.SMEM((4, 4), jnp.int32),
+            pltpu.SemaphoreType.DMA((10,)),
+        ],
         compiler_params=pltpu.CompilerParams(vmem_limit_bytes=16 * MIB),
         cost_estimate=pl.CostEstimate(flops=2 * 528 * 2048 * 256, bytes_accessed=7 * MIB, transcendentals=0),
-    )(coupling, source, pltpu.with_memory_space_constraint(excite, pltpu.HBM))
+    )(*[pltpu.with_memory_space_constraint(a, pltpu.HBM) for a in (coupling, source, excite)])
 
 
 def arrange_kernel(order_ref, signs_ref, out_ref, token_ref):
@@ -146,11 +159,32 @@
     )(order, near(signs))
 
 
-def lookup_kernel(target_ref, table_ref, signs_ref, out_ref, rows):
-    labels = lax.broadcasted_iota(jnp.int32, (64, 512), 0)
-    hot = (labels == target_ref[...]).astype(jnp.float32).astype(jnp.bfloat16)
+def table_labels(shape):
+    blk = lax.axis_index("blk")
+    core, z, x = blk % 2, blk // 8, blk // 2 % 4
+    row = lax.broadcasted_iota(jnp.int32, shape, 0)
+    along, owner, chip = row >> 4, (row >> 3) & 1, row & 7
+    side = 1 + 2 * core
+    dx = jnp.where(along == 1, side, jnp.where(along == 2, 4 - side, jnp.where(along == 3, 2, 0)))
+    second, first = chip >> 1, chip & 1
+    dx = dx + 2 * (second & 1)
+    dz = 4 * first + jnp.where(second == 3, 7, second)
+    return ((z + dz) & 7) * 8 + ((x + dx) & 3) * 2 + owner
+
+
+def lookup_kernel(target_ref, signs_ref, after_ref, *refs):
+    del after_ref
+    tables, (out_ref, token_ref, rows) = refs[:4], refs[4:]
+    token_ref[...] = jnp.zeros_like(token_ref)
+    hot = (table_labels((64, 512)) == target_ref[...]).astype(jnp.float32).astype(jnp.bfloat16)
+    entries = [ref[...].reshape(8, 8, 128) for ref in tables]
     for part in range(2):
-        table = jnp.concatenate([table_ref[:, 2 * h + part, :64] for h in range(4)], 1).astype(jnp.bfloat16)
+        lines = [
+            jnp.concatenate([entry[:, 2 * h + part, core * 64 : core * 64 + 64] for h in range(4)], 1)
+            for entry in entries
+            for core in range(2)
+        ]
+        table = jnp.concatenate(lines, 0).astype(jnp.bfloat16)
         row = lax.dot_general(hot, table, (((0,), (0,)), ((), ())), preferred_element_type=jnp.float32)
         rows[part * 512 : part * 512 + 512, :] = row.astype(jnp.bfloat16)
 
@@ -169,16 +203,16 @@
                 out_ref[:, pl.ds(at, 128)] = value[:, chunk * 128 : chunk * 128 + 128]
 
 
-def lookup(target, table, signs):
+def lookup(target, tables, signs, after):
     return pl.pallas_call(
         lookup_kernel,
-        in_specs=[VMEM] * 3,
-        out_specs=VMEM,
-        out_shape=pltpu.VMEM((512, 4096), jnp.bfloat16),
+        in_specs=[VMEM] * 7,
+        out_specs=[VMEM] * 2,
+        out_shape=[pltpu.VMEM((512, 4096), jnp.bfloat16), TOKEN],
         scratch_shapes=[pltpu.VMEM((1024, 256), jnp.bfloat16)],
         compiler_params=pltpu.CompilerParams(vmem_limit_bytes=16 * MIB),
         cost_estimate=pl.CostEstimate(flops=10**6, bytes_accessed=MIB, transcendentals=0),
-    )(target, near(table), near(signs))
+    )(target, *[near(a) for a in (signs, after, *tables)])
 
 
 def join_kernel(groups, *refs):
@@ -194,15 +228,31 @@
 
 
 def join(pieces, groups, after=()):
-    shapes = [(2, sum(pieces[k].shape[1] for k in group), 1024) for group in groups]
+    shapes = [(2, sum(pieces[k].shape[1] for k in group), pieces[0].shape[2]) for group in groups]
     return pl.pallas_call(
         functools.partial(join_kernel, groups),
-        in_specs=[VMEM] * len(pieces) + [ANY] * len(after),
+        in_specs=[VMEM] * (len(pieces) + len(after)),
         out_specs=[VMEM] * len(groups),
         out_shape=[pltpu.VMEM(shape, jnp.bfloat16) for shape in shapes],
-        compiler_params=pltpu.CompilerParams(vmem_limit_bytes=8 * MIB),
+        compiler_params=pltpu.CompilerParams(vmem_limit_bytes=4 * MIB),
         cost_estimate=pl.CostEstimate(flops=0, bytes_accessed=MIB, transcendentals=0),
     )(*[near(p) for p in pieces], *after)
+
+
+def relay_kernel(block_ref, after_ref, out_ref):
+    del block_ref, after_ref, out_ref
+
+
+def relay(block, after):
+    return pl.pallas_call(
+        relay_kernel,
+        in_specs=[VMEM] * 2,
+        out_specs=VMEM,
+        out_shape=pltpu.VMEM(block.shape, block.dtype),
+        input_output_aliases={0: 0},
+        compiler_params=pltpu.CompilerParams(vmem_limit_bytes=2 * MIB),
+        cost_estimate=pl.CostEstimate(flops=0, bytes_accessed=0, transcendentals=0),
+    )(near(block), after)
 
 
 def product_kernel(first, last, starts, count, width, *refs):
@@ -269,35 +319,95 @@
     )(live, *arrays)
 
 
-def spread_kernel(row_ref, after_ref, out_ref):
-    del after_ref
-    row = row_ref[...]
-    row = jnp.concatenate([row, jnp.zeros_like(row)], 1)
-    out_ref[...] = jnp.broadcast_to(row[None], out_ref.shape)
-
-
-def spread(row, after):
-    return pl.pallas_call(
-        spread_kernel,
+def along_x(first, second):
+    pairs = []
+    for y in range(NY):
+        for z in range(NZ):
+            for x in range(NX):
+                for c, step in enumerate((first, second)):
+                    pairs.append((index(x + step, y, z, c), index(x, y, z, c)))
+    return pairs
+
+
+def choose(mine, theirs):
+    return jnp.where(lax.axis_index("blk") % 2 == 0, mine, theirs)
+
+
+def pack_kernel(coeffs_ref, mine_ref, theirs_ref, out_ref):
+    mine, theirs = mine_ref[...], theirs_ref[...]
+    entries = jnp.concatenate([choose(mine, theirs), choose(theirs, mine)], 1).astype(jnp.bfloat16)
+    out_ref[:, :, :1024] = coeffs_ref[...]
+    out_ref[0, :, 1024:] = entries
+    out_ref[1, :, 1024:] = jnp.zeros_like(entries)
+
+
+def pack(coeffs, mine, theirs):
+    return pl.pallas_call(
+        pack_kernel,
+        in_specs=[VMEM] * 3,
+        out_specs=VMEM,
+        out_shape=pltpu.VMEM((2, 8, 1152), jnp.bfloat16),
+        compiler_params=pltpu.CompilerParams(vmem_limit_bytes=2 * MIB),
+        cost_estimate=pl.CostEstimate(flops=0, bytes_accessed=1 << 16, transcendentals=0),
+    )(coeffs, mine, theirs)
+
+
+def unpack_kernel(*refs):
+    pieces, slab_ref, table_ref = refs[:4], refs[-2], refs[-1]
+    for k, piece in enumerate(pieces):
+        slab_ref[:, k * 16 : k * 16 + 16, :] = piece[:, :, :1024]
+        table_ref[k * 16 : k * 16 + 16, :] = piece[0, :, 1024:].astype(jnp.float32)
+
+
+def unpack(pieces, after):
+    return pl.pallas_call(
+        unpack_kernel,
+        in_specs=[VMEM] * 4 + [ANY],
+        out_specs=[VMEM] * 2,
+        out_shape=[pltpu.VMEM((2, 64, 1024), jnp.bfloat16), pltpu.VMEM((64, 128), jnp.float32)],
+        compiler_params=pltpu.CompilerParams(vmem_limit_bytes=2 * MIB),
+        cost_estimate=pl.CostEstimate(flops=0, bytes_accessed=MIB, transcendentals=0),
+    )(*[near(piece) for piece in pieces], after)
+
+
+def pick_kernel(mine_ref, theirs_ref, out_ref):
+    out_ref[...] = choose(mine_ref[...], theirs_ref[...])
+
+
+def pick(mine, theirs):
+    return pl.pallas_call(
+        pick_kernel,
         in_specs=[VMEM] * 2,
         out_specs=VMEM,
-        out_shape=jax.ShapeDtypeStruct((64, 8, 128), jnp.float32),
-        cost_estimate=pl.CostEstimate(flops=10**6, bytes_accessed=MIB, transcendentals=0),
-    )(row, near(after))
+        out_shape=pltpu.VMEM((64, 128), jnp.float32),
+        compiler_params=pltpu.CompilerParams(vmem_limit_bytes=2 * MIB),
+        cost_estimate=pl.CostEstimate(flops=0, bytes_accessed=1 << 16, transcendentals=0),
+    )(near(mine), near(theirs))
+
+
+def gather_tables(table):
+    table = pick(table, swap(table))
+    side = lax.ppermute(table, AXES, along_x(1, -1))
+    return [table, side, swap(side), lax.ppermute(table, AXES, along_x(2, 2))]
 
 
 def on_device(coeffs, coupling, one_body, target_orb, source_orb, excite, live_rows):
     signs, token = split_cores(coupling, source_orb[None, :], excite)
-    slab = join([coeffs] + fetch(coeffs, 0), [(0, 1)], [token])[0]
-
-    table = lax.all_to_all(spread(one_body.reshape(8, 64), slab), "blk", 0, 0, tiled=True)
-
-    slab = join([slab] + fetch(slab, 1), [(0, 1, 2, 3)], [table])[0]
+    row = one_body.reshape(8, 64)
+    packed = pack(coeffs, row, swap(row))
+    packed = join([packed] + fetch(packed, 0), [(0, 1)], [token])[0]
     arranged, token = arrange(ORDER, signs)
-    halves = list(join([slab] + fetch(slab, 2), [(0, 1), (2, 3)], [token]))
-    left = lookup(target_orb[None, :], table, arranged)
-
-    got = [fetch(half, 3) for half in halves]
+    slab, table = unpack([packed] + fetch(packed, 1), token)
+    tables = gather_tables(table)
+    halves = list(
+        join([slab] + fetch(slab, 2), [(0, 1), (2, 3), (2, 3)], [near(tables[1]), near(tables[3])])
+    )
+    spare = halves.pop()
+    left, token = lookup(target_orb[None, :], tables, arranged, halves[0])
+    late = relay(spare, token)
+
+    got = [fetch(halves[0], 3)]
+    got.append([lax.ppermute(h, AXES, route(o)) for h, o in zip((halves[1], halves[1], late), STAGES[3])])
     own = halves + [swap(half) for half in halves]
     total, token = product(live_rows, left, ((0, 512), (2048, 512)), own, None, False)
     first = join(got[0], [(0, 1, 2)], [token])[0]

time: 80.7 us -> 72.3 us (0.90)
  waiting for transfers between devices: 14.7 us -> 10.8 us
  starting transfers between devices: 38.6 us -> 36 us
  Pallas kernels: 24.9 us -> 23.1 us
    ppermute x13 -> x10, waiting for transfers between devices: 13.6 us -> 0.18 us  [fetch(): return [lax.ppermute(block, AXES, route(o)) for o in STAGES[stage]]]
    all_to_all x1 -> x0, starting transfers between devices: 7.89 us -> none  [on_device(): lax.all_to_all(spread(one_body.reshape(8, 64), slab), 'blk', 0, 0, tiled=...]
    ppermute x0 -> x5, waiting for transfers between devices: none -> 7.87 us  [the longest x1 3.76 us: gather_tables(): return [table, side, swap(side), lax.ppermute(table, AXES, along_x(2, 2))]]
    ppermute x4 -> x7, starting transfers between devices: 4.62 us -> 11.1 us  [swap(): return lax.ppermute(block, AXES, SWAP)]
    ppermute x13 -> x10, starting transfers between devices: 26.1 us -> 20.3 us  [fetch(): return [lax.ppermute(block, AXES, route(o)) for o in STAGES[stage]]]
    ppermute x0 -> x5, starting transfers between devices: none -> 4.55 us  [the longest x3 2.38 us: on_device(): lax.ppermute(h, AXES, route(o))]
    ppermute x4 -> x7, waiting for transfers between devices: 0.49 us -> 2.76 us  [swap(): return lax.ppermute(block, AXES, SWAP)]
    pallas_call x3 -> x6, Pallas kernels: 9.08 us -> 7.21 us  [the longest x1 3.66 us: lookup(): pl.pallas_call(lookup_kernel, in_specs=[VMEM] * 7, out_specs=[VMEM] * 2,...]
  transfers between devices with their start and end apart: 18 -> 22, of which waited for: 5 -> 8; matrix products, arithmetic and copies ran while one was open for 0% -> 0% of each run, Pallas kernels for 25% -> 27%
where the time goes in v3:
time: 72.3 us; the launch traced here: 72.2 us
  starting transfers between devices  36 us (50%)
  Pallas kernels  23.1 us (32%)
  waiting for transfers between devices  10.8 us (15%)
  local copies, waits for them, and re-layouts  1.45 us (2%)
  between operations  0.81 us (1%)
    ppermute x10, starting transfers between devices, fetch(): return [lax.ppermute(block, AXES, route(o)) for o in STAGES[stage]]  20.3 us
    pallas_call x4, Pallas kernels, product(): pl.pallas_call(functools.partial(product_kernel, first, last, starts, cou...  11.9 us
    ppermute x7, starting transfers between devices, swap(): return lax.ppermute(block, AXES, SWAP)  11.1 us
    ppermute x1, waiting for transfers between devices, gather_tables(): return [table, side, swap(side), lax.ppermute(table, AXES, along_x(2, 2))]  3.76 us
    ppermute x3, waiting for transfers between devices, on_device(): lax.ppermute(h, AXES, route(o))  3.71 us
    pallas_call x1, Pallas kernels, arrange(): pl.pallas_call(arrange_kernel, in_specs=[VMEM] * 2, out_specs=[VMEM] * 2,...  3.7 us
    pallas_call x1, Pallas kernels, lookup(): pl.pallas_call(lookup_kernel, in_specs=[VMEM] * 7, out_specs=[VMEM] * 2,...  3.66 us
    pallas_call x1, Pallas kernels, split_cores(): pl.pallas_call(split_kernel, in_specs=[ANY] * 3, out_specs=[VMEM] * 2, ou...  3.44 us
  transfers between devices with their start and end apart: 22, of which 8 were waited for; matrix products, arithmetic and copies ran while one was open for 0% of the time, Pallas kernels for 27%

profile of v3, /device:TPU:1, one launch (start us, length us, event | category | flops | bytes accessed | tf_op | source)
XLA Modules:
  0.0 72.2 jit_solution(1299567657840185221)
XLA Ops:
  0.0 3.2 %collective-permute-start = (f32[8,64]{1,0:T(8,128)}, f32[8,64]{1,0:T(8,128)S(1)}, u32[]{:S(2)}, u32[]{:S(2)}) collective-permute-start(f32[8,64]{1,0:T(8,128)} %bitcast.3), channel_id=1, source_target_pairs={{0,1},{1,0},{2,3},{3,2},{4,5},{5,4},{6,7},{7,6},{8,9},{9,8},{10,11... | collective-permute-start | bytes 6152 | tf_op jit(solution)/shard_map/ppermute | solution.py:47
  3.2 1.0 %collective-permute-done.theirs_ref = f32[8,64]{1,0:T(8,128)S(1)} collective-permute-done((f32[8,64]{1,0:T(8,128)}, f32[8,64]{1,0:T(8,128)S(1)}, u32[]{:S(2)}, u32[]{:S(2)}) %collective-permute-start) | collective-permute-done | bytes 2080 | tf_op jit(solution)/shard_map/ppermute | solution.py:47
  4.3 0.0 copy-start
  4.3 0.8 %copy-done = bf16[2,8,1024]{2,1,0:T(8,128)(2,1)S(1)} copy-done((bf16[2,8,1024]{2,1,0:T(8,128)(2,1)S(1)}, bf16[2,8,1024]{2,1,0:T(8,128)(2,1)}, u32[]{:S(2)}) %copy-start) | copy-done | bytes 32792
  5.0 0.0 copy-start.1
  5.0 0.7 copy-done.1
  5.7 0.0 copy-start.3
  5.7 0.1 shard_map.84.refs_0_
  5.8 5.2 %collective-permute-start.1 = (bf16[2,8,1152]{2,1,0:T(8,128)(2,1)S(1)}, bf16[2,8,1152]{2,1,0:T(8,128)(2,1)S(1)}, u32[]{:S(2)}, u32[]{:S(2)}) collective-permute-start(bf16[2,8,1152]{2,1,0:T(8,128)(2,1)S(1)} %shard_map.84.refs_0_), channel_id=1, source_target_pairs={{32,0},{33,1},{34,2},{35,3},{36,4},{37,5},{38,6},{39,7},{40,8},{41... | collective-permute-start | bytes 110600 | tf_op jit(solution)/shard_map/ppermute | solution.py:43
  11.0 3.4 %shard_map.82 = (bf16[2,528,1024]{2,1,0:T(8,128)(2,1)S(1)}, f32[8,128]{1,0:T(8,128)S(1)}) custom-call(s32[4,4]{1,0:T(4,128)} %coupling_ref.1, s32[1,2048]{1,0:T(1,128)} %bitcast.6, s32[512,2048]{1,0:T(8,128)} %excite_ref.1), custom_call_target="tpu_custom_call" | custom-call | flops 553648128 | bytes 7340032 | tf_op jit(solution)/shard_map/pallas_call | solution.py:119
  14.4 0.0 collective-permute-done.1.refs_1_
  14.5 3.4 %collective-permute-start.2 = (bf16[2,16,1152]{2,1,0:T(8,128)(2,1)S(1)}, bf16[2,16,1152]{2,1,0:T(8,128)(2,1)S(1)}, u32[]{:S(2)}, u32[]{:S(2)}) collective-permute-start(bf16[2,16,1152]{2,1,0:T(8,128)(2,1)S(1)} %shard_map.85.refs_0_), channel_id=1, source_target_pairs={{12,0},{185,1},{14,2},{187,3},{8,4},{189,5},{10,6},{191,7},{20,8},... | collective-permute-start | bytes 221192 | tf_op jit(solution)/shard_map/ppermute | solution.py:43
  17.9 1.2 %collective-permute-start.3 = (bf16[2,16,1152]{2,1,0:T(8,128)(2,1)S(1)}, bf16[2,16,1152]{2,1,0:T(8,128)(2,1)S(1)}, u32[]{:S(2)}, u32[]{:S(2)}) collective-permute-start(bf16[2,16,1152]{2,1,0:T(8,128)(2,1)S(1)} %shard_map.85.refs_0_), channel_id=1, source_target_pairs={{16,0},{49,1},{18,2},{51,3},{20,4},{53,5},{22,6},{55,7},{24,8},{57... | collective-permute-start | bytes 221192 | tf_op jit(solution)/shard_map/ppermute | solution.py:43
  19.1 1.7 %collective-permute-start.4 = (bf16[2,16,1152]{2,1,0:T(8,128)(2,1)S(1)}, bf16[2,16,1152]{2,1,0:T(8,128)(2,1)S(1)}, u32[]{:S(2)}, u32[]{:S(2)}) collective-permute-start(bf16[2,16,1152]{2,1,0:T(8,128)(2,1)S(1)} %shard_map.85.refs_0_), channel_id=1, source_target_pairs={{60,0},{137,1},{62,2},{139,3},{56,4},{141,5},{58,6},{143,7},{4,8},... | collective-permute-start | bytes 221192 | tf_op jit(solution)/shard_map/ppermute | solution.py:43
  20.8 0.0 copy-done.3
  20.8 0.0 copy-start.2
  20.8 3.7 %shard_map.83 = (bf16[8,528,256]{2,1,0:T(8,128)(2,1)S(1)}, f32[8,128]{1,0:T(8,128)S(1)}) custom-call(s32[2,4,8,1,256]{4,3,2,1,0:T(1,128)S(1)} %copy-done.3, bf16[2,528,1024]{2,1,0:T(8,128)(2,1)S(1)} %get-tuple-element.21.signs_ref), custom_call_target="tpu_custom_call" | custom-call | flops 2214592512 | bytes 4194304 | tf_op jit(solution)/shard_map/pallas_call | solution.py:152
  24.5 0.0 collective-permute-done.2.refs_1_
  24.6 0.0 collective-permute-done.3.refs_2_
  24.6 0.2 collective-permute-done.4.refs_3_
  24.8 5.2 %collective-permute-start.5 = (bf16[2,64,1024]{2,1,0:T(8,128)(2,1)S(1)}, bf16[2,64,1024]{2,1,0:T(8,128)(2,1)S(1)}, u32[]{:S(2)}, u32[]{:S(2)}) collective-permute-start(bf16[2,64,1024]{2,1,0:T(8,128)(2,1)S(1)} %get-tuple-element.25.refs_0_), channel_id=1, source_target_pairs={{72,0},{59,1},{74,2},{61,3},{76,4},{63,5},{78,6},{57,7},{80,8},{3,... | collective-permute-start | bytes 786440 | tf_op jit(solution)/shard_map/ppermute | solution.py:43
  29.9 0.0 collective-permute-start.6
  29.9 0.7 collective-permute-start.7
  30.6 3.3 %collective-permute-start.8 = (f32[64,128]{1,0:T(8,128)S(1)}, f32[64,128]{1,0:T(8,128)S(1)}, u32[]{:S(2)}, u32[]{:S(2)}) collective-permute-start(f32[64,128]{1,0:T(8,128)S(1)} %get-tuple-element.26.mine_ref), channel_id=1, source_target_pairs={{0,1},{1,0},{2,3},{3,2},{4,5},{5,4},{6,7},{7,6},{8,9},{9,8},{10,11... | collective-permute-start | bytes 98312 | tf_op jit(solution)/shard_map/ppermute | solution.py:47
  33.9 0.9 %collective-permute-done.8.theirs_ref = f32[64,128]{1,0:T(8,128)S(1)} collective-permute-done((f32[64,128]{1,0:T(8,128)S(1)}, f32[64,128]{1,0:T(8,128)S(1)}, u32[]{:S(2)}, u32[]{:S(2)}) %collective-permute-start.8) | collective-permute-done | bytes 32800 | tf_op jit(solution)/shard_map/ppermute | solution.py:47
  34.8 1.9 %collective-permute-start.10 = (f32[64,128]{1,0:T(8,128)S(1)}, f32[64,128]{1,0:T(8,128)S(1)}, u32[]{:S(2)}, u32[]{:S(2)}) collective-permute-start(f32[64,128]{1,0:T(8,128)S(1)} %shard_map.87.refs_0_), channel_id=1, source_target_pairs={{4,0},{5,1},{6,2},{7,3},{0,4},{1,5},{2,6},{3,7},{12,8},{13,9},{14,... | collective-permute-start | bytes 98312 | tf_op jit(solution)/shard_map/ppermute | solution.py:391
  36.6 0.3 collective-permute-start.9
  37.0 3.8 %collective-permute-done.10.refs_5_.refs_3_ = f32[64,128]{1,0:T(8,128)S(1)} collective-permute-done((f32[64,128]{1,0:T(8,128)S(1)}, f32[64,128]{1,0:T(8,128)S(1)}, u32[]{:S(2)}, u32[]{:S(2)}) %collective-permute-start.10) | collective-permute-done | bytes 32800 | tf_op jit(solution)/shard_map/ppermute | solution.py:391
  40.7 0.4 collective-permute-done.9.refs_4_.refs_1_
  41.1 0.0 collective-permute-done.5.refs_1_
  41.1 0.0 collective-permute-done.6.refs_2_
  41.1 0.0 collective-permute-done.7.refs_3_
  41.1 0.1 shard_map.88
  41.2 2.2 %collective-permute-start.18 = (bf16[2,128,1024]{2,1,0:T(8,128)(2,1)S(1)}, bf16[2,128,1024]{2,1,0:T(8,128)(2,1)S(1)}, u32[]{:S(2)}, u32[]{:S(2)}) collective-permute-start(bf16[2,128,1024]{2,1,0:T(8,128)(2,1)S(1)} %get-tuple-element.27.after_ref.refs_2_), channel_id=1, source_target_pairs={{0,1},{1,0},{2,3},{3,2},{4,5},{5,4},{6,7},{7,6},{8,9},{9,8},{10,11... | collective-permute-start | bytes 1572872 | tf_op jit(solution)/shard_map/ppermute | solution.py:47
  43.5 0.1 collective-permute-start.19
  43.6 1.3 %collective-permute-start.15 = (bf16[2,128,1024]{2,1,0:T(8,128)(2,1)S(1)}, bf16[2,128,1024]{2,1,0:T(8,128)(2,1)S(1)}, u32[]{:S(2)}, u32[]{:S(2)}) collective-permute-start(bf16[2,128,1024]{2,1,0:T(8,128)(2,1)S(1)} %get-tuple-element.27.after_ref.refs_2_), channel_id=1, source_target_pairs={{2,0},{65,1},{4,2},{67,3},{6,4},{69,5},{0,6},{71,7},{10,8},{73,9},... | collective-permute-start | bytes 1572872 | tf_op jit(solution)/shard_map/ppermute | solution.py:43
  44.9 1.5 %collective-permute-start.11 = (f32[64,128]{1,0:T(8,128)S(1)}, f32[64,128]{1,0:T(8,128)S(1)}, u32[]{:S(2)}, u32[]{:S(2)}) collective-permute-start(f32[64,128]{1,0:T(8,128)S(1)} %collective-permute-done.9.refs_4_.refs_1_), channel_id=1, source_target_pairs={{0,1},{1,0},{2,3},{3,2},{4,5},{5,4},{6,7},{7,6},{8,9},{9,8},{10,11... | collective-permute-start | bytes 98312 | tf_op jit(solution)/shard_map/ppermute | solution.py:47
  46.4 0.0 collective-permute-start.16
  46.4 0.9 %collective-permute-done.11.refs_2_ = f32[64,128]{1,0:T(8,128)S(1)} collective-permute-done((f32[64,128]{1,0:T(8,128)S(1)}, f32[64,128]{1,0:T(8,128)S(1)}, u32[]{:S(2)}, u32[]{:S(2)}) %collective-permute-start.11) | collective-permute-done | bytes 32800 | tf_op jit(solution)/shard_map/ppermute | solution.py:47
  47.3 1.5 %collective-permute-start.17 = (bf16[2,128,1024]{2,1,0:T(8,128)(2,1)S(1)}, bf16[2,128,1024]{2,1,0:T(8,128)(2,1)S(1)}, u32[]{:S(2)}, u32[]{:S(2)}) collective-permute-start(bf16[2,128,1024]{2,1,0:T(8,128)(2,1)S(1)} %get-tuple-element.27.after_ref.refs_2_), channel_id=1, source_target_pairs={{8,0},{57,1},{10,2},{59,3},{12,4},{61,5},{14,6},{63,7},{16,8},{1,9... | collective-permute-start | bytes 1572872 | tf_op jit(solution)/shard_map/ppermute | solution.py:43
  48.8 0.0 copy-done.2
  48.8 3.7 %shard_map.89 = (bf16[512,4096]{1,0:T(8,128)(2,1)S(1)}, f32[8,128]{1,0:T(8,128)S(1)}) custom-call(s32[1,512]{1,0:T(1,128)S(1)} %bitcast.5, bf16[8,528,256]{2,1,0:T(8,128)(2,1)S(1)} %get-tuple-element.22.signs_ref, bf16[2,128,1024]{2,1,0:T(8,128)(2,1)S(1)} %get-tuple-element.27.after_ref.refs_2_, f32[64,128]{1,0:T(8,128)S(1)} %shard_map.87.refs_0_, ...), custom_call_target="tpu_custom_call" | custom-call | flops 1000000 | bytes 1048576 | tf_op jit(solution)/shard_map/pallas_call | solution.py:207
  52.5 0.0 collective-permute-done.18.refs_4_
  52.5 1.9 %collective-permute-start.12 = (bf16[2,128,1024]{2,1,0:T(8,128)(2,1)S(1)}, bf16[2,128,1024]{2,1,0:T(8,128)(2,1)S(1)}, u32[]{:S(2)}, u32[]{:S(2)}) collective-permute-start(bf16[2,128,1024]{2,1,0:T(8,128)(2,1)S(1)} %get-tuple-element.29.refs_3_), channel_id=1, source_target_pairs={{2,0},{65,1},{4,2},{67,3},{6,4},{69,5},{0,6},{71,7},{10,8},{73,9},... | collective-permute-start | bytes 1572872 | tf_op jit(solution)/shard_map/ppermute | solution.py:410
  54.5 0.0 collective-permute-done.19.refs_5_
  54.5 0.2 collective-permute-start.14
  54.7 0.0 collective-permute-done.15.refs_0_
  54.7 0.2 collective-permute-start.13
  55.6 2.5 %shard_map.91 = (f32[2,512,1024]{2,1,0:T(8,128)S(1)}, f32[8,128]{1,0:T(8,128)S(1)}) custom-call(s32[1]{0:T(128)S(6)} %copy.15.refs_0_, bf16[512,4096]{1,0:T(8,128)(2,1)S(1)} %get-tuple-element.28.refs_1_, bf16[2,128,1024]{2,1,0:T(8,128)(2,1)S(1)} %get-tuple-element.27.after_ref.refs_2_, bf16[2,128,1024]{2,1,0:T(8,128)(2,1)S(1)} %get-tuple-element.29.refs_3_, ...), custom_call_target="tpu_custom_call" | custom-call | flops 1000000 | bytes 1048576 | tf_op jit(solution)/shard_map/pallas_call | solution.py:312
  58.1 0.0 collective-permute-done.16.refs_1_
  58.1 0.0 collective-permute-done.17.refs_2_
  58.1 0.1 shard_map.92.refs_2_
  58.2 0.1 collective-permute-start.21
  58.3 2.2 %shard_map.93 = (f32[2,512,1024]{2,1,0:T(8,128)S(1)}, f32[8,128]{1,0:T(8,128)S(1)}) custom-call(s32[1]{0:T(128)S(6)} %copy.15.refs_0_, bf16[512,4096]{1,0:T(8,128)(2,1)S(1)} %get-tuple-element.28.refs_1_, bf16[2,384,1024]{2,1,0:T(8,128)(2,1)S(1)} %shard_map.92.refs_2_, f32[2,512,1024]{2,1,0:T(8,128)S(1)} %get-tuple-element.33.refs_3_), custom_call_target="tpu_custom_call", output_to_operand_aliasing={{0}: (3, {})} | custom-call | flops 1000000 | bytes 1048576 | tf_op jit(solution)/shard_map/pallas_call | solution.py:312
  60.5 3.5 %collective-permute-done.14.refs_2_ = bf16[2,128,1024]{2,1,0:T(8,128)(2,1)S(1)} collective-permute-done((bf16[2,128,1024]{2,1,0:T(8,128)(2,1)S(1)}, bf16[2,128,1024]{2,1,0:T(8,128)(2,1)S(1)}, u32[]{:S(2)}, u32[]{:S(2)}) %collective-permute-start.14) | collective-permute-done | bytes 524320 | tf_op jit(solution)/shard_map/ppermute | solution.py:410
  64.0 0.0 collective-permute-done.12.refs_0_
  64.0 0.2 collective-permute-done.13.refs_1_
  64.2 0.1 shard_map.94.refs_3_
  64.3 0.6 collective-permute-start.20
  65.0 0.0 collective-permute-done.21.refs_2_
  65.0 3.8 %shard_map.95 = (f32[2,512,1024]{2,1,0:T(8,128)S(1)}, f32[8,128]{1,0:T(8,128)}) custom-call(s32[1]{0:T(128)S(6)} %copy.15.refs_0_, bf16[512,4096]{1,0:T(8,128)(2,1)S(1)} %get-tuple-element.28.refs_1_, bf16[2,384,1024]{2,1,0:T(8,128)(2,1)S(1)} %collective-permute-done.21.refs_2_, ...), custom_call_target="tpu_custom_call", output_to_operand_aliasing={{0}: (4, {})} | custom-call | flops 1000000 | bytes 1048576 | tf_op jit(solution)/shard_map/pallas_call | solution.py:312
  68.8 0.0 collective-permute-done.20.refs_2_
  68.8 3.4 %shard_map.96 = f32[2,512,1024]{2,1,0:T(8,128)} custom-call(s32[1]{0:T(128)S(6)} %copy.15.refs_0_, bf16[512,4096]{1,0:T(8,128)(2,1)S(1)} %get-tuple-element.28.refs_1_, bf16[2,384,1024]{2,1,0:T(8,128)(2,1)S(1)} %collective-permute-done.20.refs_2_, f32[2,512,1024]{2,1,0:T(8,128)S(1)} %get-tuple-element.36.refs_3_), custom_call_target="tpu_custom_call" | custom-call | flops 1000000 | bytes 1048576 | tf_op jit(solution)/shard_map/pallas_call | solution.py:312
  (4 shorter events, 0.0 us)
Async XLA Ops:
  0.0 4.3 %collective-permute-start = (f32[8,64]{1,0:T(8,128)}, f32[8,64]{1,0:T(8,128)S(1)}, u32[]{:S(2)}, u32[]{:S(2)}) collective-permute-start(f32[8,64]{1,0:T(8,128)} %bitcast.3), channel_id=1, source_target_pairs={{0,1},{1,0},{2,3},{3,2},{4,5},{5,4},{6,7},{7,6},{8,9},{9,8},{10,11... | collective-permute-start | bytes 6152 | tf_op jit(solution)/shard_map/ppermute | solution.py:47
  4.3 0.8 %copy-start = (bf16[2,8,1024]{2,1,0:T(8,128)(2,1)S(1)}, bf16[2,8,1024]{2,1,0:T(8,128)(2,1)}, u32[]{:S(2)}) copy-start(bf16[2,8,1024]{2,1,0:T(8,128)(2,1)} %coeffs_ref.1) | copy-start | bytes 98308
  5.0 0.7 copy-start.1
  5.7 15.1 %copy-start.3 = (s32[2,4,8,1,256]{4,3,2,1,0:T(1,128)S(1)}, s32[2,4,8,1,256]{4,3,2,1,0:T(1,128)}, u32[]{:S(2)}) copy-start(s32[2,4,8,1,256]{4,3,2,1,0:T(1,128)} %constant.2.clone.order_ref) | copy-start | bytes 196612
  5.8 8.7 %collective-permute-start.1 = (bf16[2,8,1152]{2,1,0:T(8,128)(2,1)S(1)}, bf16[2,8,1152]{2,1,0:T(8,128)(2,1)S(1)}, u32[]{:S(2)}, u32[]{:S(2)}) collective-permute-start(bf16[2,8,1152]{2,1,0:T(8,128)(2,1)S(1)} %shard_map.84.refs_0_), channel_id=1, source_target_pairs={{32,0},{33,1},{34,2},{35,3},{36,4},{37,5},{38,6},{39,7},{40,8},{41... | collective-permute-start | bytes 110600 | tf_op jit(solution)/shard_map/ppermute | solution.py:43
  14.5 10.1 %collective-permute-start.2 = (bf16[2,16,1152]{2,1,0:T(8,128)(2,1)S(1)}, bf16[2,16,1152]{2,1,0:T(8,128)(2,1)S(1)}, u32[]{:S(2)}, u32[]{:S(2)}) collective-permute-start(bf16[2,16,1152]{2,1,0:T(8,128)(2,1)S(1)} %shard_map.85.refs_0_), channel_id=1, source_target_pairs={{12,0},{185,1},{14,2},{187,3},{8,4},{189,5},{10,6},{191,7},{20,8},... | collective-permute-start | bytes 221192 | tf_op jit(solution)/shard_map/ppermute | solution.py:43
  17.9 6.6 %collective-permute-start.3 = (bf16[2,16,1152]{2,1,0:T(8,128)(2,1)S(1)}, bf16[2,16,1152]{2,1,0:T(8,128)(2,1)S(1)}, u32[]{:S(2)}, u32[]{:S(2)}) collective-permute-start(bf16[2,16,1152]{2,1,0:T(8,128)(2,1)S(1)} %shard_map.85.refs_0_), channel_id=1, source_target_pairs={{16,0},{49,1},{18,2},{51,3},{20,4},{53,5},{22,6},{55,7},{24,8},{57... | collective-permute-start | bytes 221192 | tf_op jit(solution)/shard_map/ppermute | solution.py:43
  19.1 5.6 %collective-permute-start.4 = (bf16[2,16,1152]{2,1,0:T(8,128)(2,1)S(1)}, bf16[2,16,1152]{2,1,0:T(8,128)(2,1)S(1)}, u32[]{:S(2)}, u32[]{:S(2)}) collective-permute-start(bf16[2,16,1152]{2,1,0:T(8,128)(2,1)S(1)} %shard_map.85.refs_0_), channel_id=1, source_target_pairs={{60,0},{137,1},{62,2},{139,3},{56,4},{141,5},{58,6},{143,7},{4,8},... | collective-permute-start | bytes 221192 | tf_op jit(solution)/shard_map/ppermute | solution.py:43
  20.8 28.0 %copy-start.2 = (s32[512]{0:T(512)S(1)}, s32[512]{0:T(512)}, u32[]{:S(2)}) copy-start(s32[512]{0:T(512)} %param.11) | copy-start | bytes 6148
  24.8 16.4 %collective-permute-start.5 = (bf16[2,64,1024]{2,1,0:T(8,128)(2,1)S(1)}, bf16[2,64,1024]{2,1,0:T(8,128)(2,1)S(1)}, u32[]{:S(2)}, u32[]{:S(2)}) collective-permute-start(bf16[2,64,1024]{2,1,0:T(8,128)(2,1)S(1)} %get-tuple-element.25.refs_0_), channel_id=1, source_target_pairs={{72,0},{59,1},{74,2},{61,3},{76,4},{63,5},{78,6},{57,7},{80,8},{3,... | collective-permute-start | bytes 786440 | tf_op jit(solution)/shard_map/ppermute | solution.py:43
  29.9 11.2 %collective-permute-start.6 = (bf16[2,64,1024]{2,1,0:T(8,128)(2,1)S(1)}, bf16[2,64,1024]{2,1,0:T(8,128)(2,1)S(1)}, u32[]{:S(2)}, u32[]{:S(2)}) collective-permute-start(bf16[2,64,1024]{2,1,0:T(8,128)(2,1)S(1)} %get-tuple-element.25.refs_0_), channel_id=1, source_target_pairs={{128,0},{5,1},{130,2},{7,3},{132,4},{1,5},{134,6},{3,7},{136,8},{1... | collective-permute-start | bytes 786440 | tf_op jit(solution)/shard_map/ppermute | solution.py:43
  29.9 11.2 %collective-permute-start.7 = (bf16[2,64,1024]{2,1,0:T(8,128)(2,1)S(1)}, bf16[2,64,1024]{2,1,0:T(8,128)(2,1)S(1)}, u32[]{:S(2)}, u32[]{:S(2)}) collective-permute-start(bf16[2,64,1024]{2,1,0:T(8,128)(2,1)S(1)} %get-tuple-element.25.refs_0_), channel_id=1, source_target_pairs={{200,0},{63,1},{202,2},{57,3},{204,4},{59,5},{206,6},{61,7},{208,8... | collective-permute-start | bytes 786440 | tf_op jit(solution)/shard_map/ppermute | solution.py:43
  30.6 4.2 %collective-permute-start.8 = (f32[64,128]{1,0:T(8,128)S(1)}, f32[64,128]{1,0:T(8,128)S(1)}, u32[]{:S(2)}, u32[]{:S(2)}) collective-permute-start(f32[64,128]{1,0:T(8,128)S(1)} %get-tuple-element.26.mine_ref), channel_id=1, source_target_pairs={{0,1},{1,0},{2,3},{3,2},{4,5},{5,4},{6,7},{7,6},{8,9},{9,8},{10,11... | collective-permute-start | bytes 98312 | tf_op jit(solution)/shard_map/ppermute | solution.py:47
  34.8 5.9 %collective-permute-start.10 = (f32[64,128]{1,0:T(8,128)S(1)}, f32[64,128]{1,0:T(8,128)S(1)}, u32[]{:S(2)}, u32[]{:S(2)}) collective-permute-start(f32[64,128]{1,0:T(8,128)S(1)} %shard_map.87.refs_0_), channel_id=1, source_target_pairs={{4,0},{5,1},{6,2},{7,3},{0,4},{1,5},{2,6},{3,7},{12,8},{13,9},{14,... | collective-permute-start | bytes 98312 | tf_op jit(solution)/shard_map/ppermute | solution.py:391
  36.6 4.5 %collective-permute-start.9 = (f32[64,128]{1,0:T(8,128)S(1)}, f32[64,128]{1,0:T(8,128)S(1)}, u32[]{:S(2)}, u32[]{:S(2)}) collective-permute-start(f32[64,128]{1,0:T(8,128)S(1)} %shard_map.87.refs_0_), channel_id=1, source_target_pairs={{2,0},{7,1},{4,2},{1,3},{6,4},{3,5},{0,6},{5,7},{10,8},{15,9},{12,... | collective-permute-start | bytes 98312 | tf_op jit(solution)/shard_map/ppermute | solution.py:390
  41.2 11.3 %collective-permute-start.18 = (bf16[2,128,1024]{2,1,0:T(8,128)(2,1)S(1)}, bf16[2,128,1024]{2,1,0:T(8,128)(2,1)S(1)}, u32[]{:S(2)}, u32[]{:S(2)}) collective-permute-start(bf16[2,128,1024]{2,1,0:T(8,128)(2,1)S(1)} %get-tuple-element.27.after_ref.refs_2_), channel_id=1, source_target_pairs={{0,1},{1,0},{2,3},{3,2},{4,5},{5,4},{6,7},{7,6},{8,9},{9,8},{10,11... | collective-permute-start | bytes 1572872 | tf_op jit(solution)/shard_map/ppermute | solution.py:47
  43.5 11.0 %collective-permute-start.19 = (bf16[2,128,1024]{2,1,0:T(8,128)(2,1)S(1)}, bf16[2,128,1024]{2,1,0:T(8,128)(2,1)S(1)}, u32[]{:S(2)}, u32[]{:S(2)}) collective-permute-start(bf16[2,128,1024]{2,1,0:T(8,128)(2,1)S(1)} %get-tuple-element.29.refs_3_), channel_id=1, source_target_pairs={{0,1},{1,0},{2,3},{3,2},{4,5},{5,4},{6,7},{7,6},{8,9},{9,8},{10,11... | collective-permute-start | bytes 1572872 | tf_op jit(solution)/shard_map/ppermute | solution.py:47
  43.6 11.1 %collective-permute-start.15 = (bf16[2,128,1024]{2,1,0:T(8,128)(2,1)S(1)}, bf16[2,128,1024]{2,1,0:T(8,128)(2,1)S(1)}, u32[]{:S(2)}, u32[]{:S(2)}) collective-permute-start(bf16[2,128,1024]{2,1,0:T(8,128)(2,1)S(1)} %get-tuple-element.27.after_ref.refs_2_), channel_id=1, source_target_pairs={{2,0},{65,1},{4,2},{67,3},{6,4},{69,5},{0,6},{71,7},{10,8},{73,9},... | collective-permute-start | bytes 1572872 | tf_op jit(solution)/shard_map/ppermute | solution.py:43
  44.9 2.4 %collective-permute-start.11 = (f32[64,128]{1,0:T(8,128)S(1)}, f32[64,128]{1,0:T(8,128)S(1)}, u32[]{:S(2)}, u32[]{:S(2)}) collective-permute-start(f32[64,128]{1,0:T(8,128)S(1)} %collective-permute-done.9.refs_4_.refs_1_), channel_id=1, source_target_pairs={{0,1},{1,0},{2,3},{3,2},{4,5},{5,4},{6,7},{7,6},{8,9},{9,8},{10,11... | collective-permute-start | bytes 98312 | tf_op jit(solution)/shard_map/ppermute | solution.py:47
  46.4 11.7 %collective-permute-start.16 = (bf16[2,128,1024]{2,1,0:T(8,128)(2,1)S(1)}, bf16[2,128,1024]{2,1,0:T(8,128)(2,1)S(1)}, u32[]{:S(2)}, u32[]{:S(2)}) collective-permute-start(bf16[2,128,1024]{2,1,0:T(8,128)(2,1)S(1)} %get-tuple-element.27.after_ref.refs_2_), channel_id=1, source_target_pairs={{6,0},{193,1},{0,2},{195,3},{2,4},{197,5},{4,6},{199,7},{14,8},{20... | collective-permute-start | bytes 1572872 | tf_op jit(solution)/shard_map/ppermute | solution.py:43
  47.3 10.8 %collective-permute-start.17 = (bf16[2,128,1024]{2,1,0:T(8,128)(2,1)S(1)}, bf16[2,128,1024]{2,1,0:T(8,128)(2,1)S(1)}, u32[]{:S(2)}, u32[]{:S(2)}) collective-permute-start(bf16[2,128,1024]{2,1,0:T(8,128)(2,1)S(1)} %get-tuple-element.27.after_ref.refs_2_), channel_id=1, source_target_pairs={{8,0},{57,1},{10,2},{59,3},{12,4},{61,5},{14,6},{63,7},{16,8},{1,9... | collective-permute-start | bytes 1572872 | tf_op jit(solution)/shard_map/ppermute | solution.py:43
  52.5 11.5 %collective-permute-start.12 = (bf16[2,128,1024]{2,1,0:T(8,128)(2,1)S(1)}, bf16[2,128,1024]{2,1,0:T(8,128)(2,1)S(1)}, u32[]{:S(2)}, u32[]{:S(2)}) collective-permute-start(bf16[2,128,1024]{2,1,0:T(8,128)(2,1)S(1)} %get-tuple-element.29.refs_3_), channel_id=1, source_target_pairs={{2,0},{65,1},{4,2},{67,3},{6,4},{69,5},{0,6},{71,7},{10,8},{73,9},... | collective-permute-start | bytes 1572872 | tf_op jit(solution)/shard_map/ppermute | solution.py:410
  54.5 9.5 %collective-permute-start.14 = (bf16[2,128,1024]{2,1,0:T(8,128)(2,1)S(1)}, bf16[2,128,1024]{2,1,0:T(8,128)(2,1)S(1)}, u32[]{:S(2)}, u32[]{:S(2)}) collective-permute-start(bf16[2,128,1024]{2,1,0:T(8,128)(2,1)S(1)} %shard_map.90), channel_id=1, source_target_pairs={{8,0},{57,1},{10,2},{59,3},{12,4},{61,5},{14,6},{63,7},{16,8},{1,9... | collective-permute-start | bytes 1572872 | tf_op jit(solution)/shard_map/ppermute | solution.py:410
  54.7 9.5 %collective-permute-start.13 = (bf16[2,128,1024]{2,1,0:T(8,128)(2,1)S(1)}, bf16[2,128,1024]{2,1,0:T(8,128)(2,1)S(1)}, u32[]{:S(2)}, u32[]{:S(2)}) collective-permute-start(bf16[2,128,1024]{2,1,0:T(8,128)(2,1)S(1)} %get-tuple-element.29.refs_3_), channel_id=1, source_target_pairs={{6,0},{193,1},{0,2},{195,3},{2,4},{197,5},{4,6},{199,7},{14,8},{20... | collective-permute-start | bytes 1572872 | tf_op jit(solution)/shard_map/ppermute | solution.py:410
  58.2 6.8 %collective-permute-start.21 = (bf16[2,384,1024]{2,1,0:T(8,128)(2,1)S(1)}, bf16[2,384,1024]{2,1,0:T(8,128)(2,1)S(1)}, u32[]{:S(2)}, u32[]{:S(2)}) collective-permute-start(bf16[2,384,1024]{2,1,0:T(8,128)(2,1)S(1)} %shard_map.92.refs_2_), channel_id=1, source_target_pairs={{0,1},{1,0},{2,3},{3,2},{4,5},{5,4},{6,7},{7,6},{8,9},{9,8},{10,11... | collective-permute-start | bytes 4718600 | tf_op jit(solution)/shard_map/ppermute | solution.py:47
  64.3 4.5 %collective-permute-start.20 = (bf16[2,384,1024]{2,1,0:T(8,128)(2,1)S(1)}, bf16[2,384,1024]{2,1,0:T(8,128)(2,1)S(1)}, u32[]{:S(2)}, u32[]{:S(2)}) collective-permute-start(bf16[2,384,1024]{2,1,0:T(8,128)(2,1)S(1)} %shard_map.94.refs_3_), channel_id=1, source_target_pairs={{0,1},{1,0},{2,3},{3,2},{4,5},{5,4},{6,7},{7,6},{8,9},{9,8},{10,11... | collective-permute-start | bytes 4718600 | tf_op jit(solution)/shard_map/ppermute | solution.py:47

commit v4 on v3

--- a/solution.py
+++ b/solution.py
@@ -188,19 +188,29 @@
         row = lax.dot_general(hot, table, (((0,), (0,)), ((), ())), preferred_element_type=jnp.float32)
         rows[part * 512 : part * 512 + 512, :] = row.astype(jnp.bfloat16)
 
-    @pl.loop(0, 8)
-    def _(pair):
+    for pair in range(8):
         lines = lax.broadcasted_iota(jnp.int32, (256, 256), 0)
         extra = signs_ref[pair, 512:528, :].astype(jnp.float32)
         label = extra[0:1, :].astype(jnp.int32)
-        pick = jnp.where(lines == label, extra[1:2, :], 0.0).astype(jnp.bfloat16)
-        look = jnp.dot(rows[...], pick, preferred_element_type=jnp.float32)
-        sign = signs_ref[pair, 0:512, :].astype(jnp.float32)
-        for part in range(2):
-            value = (look[part * 512 : part * 512 + 512] * sign).astype(jnp.bfloat16)
-            for chunk in range(2):
-                at = pl.multiple_of(pair * 512 + chunk * 256 + part * 128, 128)
-                out_ref[:, pl.ds(at, 128)] = value[:, chunk * 128 : chunk * 128 + 128]
+        choice = jnp.where(lines == label, extra[1:2, :], 0.0).astype(jnp.bfloat16)
+        look = jnp.dot(rows[...], choice, preferred_element_type=jnp.float32).astype(jnp.bfloat16)
+        sign = signs_ref[pair, 0:512, :]
+        real, imag = look[:512] * sign, look[512:] * sign
+        for half in range(2):
+            at, step = column(2 * pair + half)
+            piece = slice(half * 128, half * 128 + 128)
+            out_ref[:512, at : at + 128] = real[:, piece]
+            out_ref[:512, at + step : at + step + 128] = -imag[:, piece]
+            out_ref[512:, at : at + 128] = imag[:, piece]
+            out_ref[512:, at + step : at + step + 128] = real[:, piece]
+
+
+def column(chunk):
+    sibling, chunk = divmod(chunk, 8)
+    if chunk < 2:
+        return sibling * 2048 + chunk * 256, 128
+    group, place = divmod(chunk - 2, 3)
+    return sibling * 2048 + 512 + group * 768 + place * 128, 384
 
 
 def lookup(target, tables, signs, after):
@@ -208,7 +218,7 @@
         lookup_kernel,
         in_specs=[VMEM] * 7,
         out_specs=[VMEM] * 2,
-        out_shape=[pltpu.VMEM((512, 4096), jnp.bfloat16), TOKEN],
+        out_shape=[pltpu.VMEM((1024, 4096), jnp.bfloat16), TOKEN],
         scratch_shapes=[pltpu.VMEM((1024, 256), jnp.bfloat16)],
         compiler_params=pltpu.CompilerParams(vmem_limit_bytes=16 * MIB),
         cost_estimate=pl.CostEstimate(flops=10**6, bytes_accessed=MIB, transcendentals=0),
@@ -255,34 +265,28 @@
     )(near(block), after)
 
 
-def product_kernel(first, last, starts, count, width, *refs):
+def product_kernel(first, last, starts, width, *refs):
     live_ref, left_ref = refs[:2]
-    blocks = refs[2 : 2 + count]
-    total_ref = None if first else refs[2 + count]
-    out_ref, right = refs[-2 - (not last)], refs[-1]
-    pieces = [(block, row) for block in blocks for row in range(0, block.shape[1], 128)]
+    blocks = refs[2 : 2 + len(starts)]
+    total_ref = None if first else refs[2 + len(starts)]
+    out_ref = refs[-1 - (not last)]
     if not last:
-        refs[-2][...] = jnp.zeros_like(refs[-2])
+        refs[-1][...] = jnp.zeros_like(refs[-1])
 
     def columns(n):
         at = pl.ds(pl.multiple_of(n * width, width), width)
-        for part in range(2):
-            for k, (block, row) in enumerate(pieces):
-                right[k * 256 : k * 256 + 128, :] = block[part, row : row + 128, at]
-                other = block[1 - part, row : row + 128, at]
-                right[k * 256 + 128 : k * 256 + 256, :] = other if part else -other
-            acc = None if first else total_ref[part, :, at]
-            row = 0
-            for start, deep in starts:
-                left = left_ref[:, start : start + deep]
-                more = jnp.dot(left, right[row : row + deep, :], preferred_element_type=jnp.float32)
-                acc = more if acc is None else acc + more
-                row += deep
-            if last:
-                line = lax.broadcasted_iota(jnp.int32, acc.shape, 0)
-                out_ref[part] = jnp.where(line < live_ref[0], acc, 0.0)
-            else:
-                out_ref[part, :, at] = acc
+        acc = None if first else total_ref[:, :, at].reshape(1024, width)
+        for start, block in zip(starts, blocks):
+            deep = 2 * block.shape[1]
+            right = block[:, :, at].reshape(deep, width)
+            more = jnp.dot(left_ref[:, start : start + deep], right, preferred_element_type=jnp.float32)
+            acc = more if acc is None else acc + more
+        acc = acc.reshape(2, 512, width)
+        if last:
+            line = lax.broadcasted_iota(jnp.int32, acc.shape, 1)
+            out_ref[...] = jnp.where(line < live_ref[0], acc, 0.0)
+        else:
+            out_ref[:, :, at] = acc
 
     if last:
         columns(pl.program_id(0))
@@ -308,11 +312,9 @@
         )
         if not first:
             out["input_output_aliases"] = {2 + count: 0}
-    deep = sum(2 * b.shape[1] for b in blocks)
-    return pl.pallas_call(
-        functools.partial(product_kernel, first, last, starts, count, width),
+    return pl.pallas_call(
+        functools.partial(product_kernel, first, last, starts, width),
         in_specs=[SMEM] + [VMEM] * len(arrays),
-        scratch_shapes=[pltpu.VMEM((deep, width), jnp.bfloat16)],
         compiler_params=pltpu.CompilerParams(vmem_limit_bytes=16 * MIB),
         cost_estimate=pl.CostEstimate(flops=flops, bytes_accessed=MIB, transcendentals=0),
         **out,
@@ -409,14 +411,14 @@
     got = [fetch(halves[0], 3)]
     got.append([lax.ppermute(h, AXES, route(o)) for h, o in zip((halves[1], halves[1], late), STAGES[3])])
     own = halves + [swap(half) for half in halves]
-    total, token = product(live_rows, left, ((0, 512), (2048, 512)), own, None, False)
+    total, token = product(live_rows, left, (0, 256, 2048, 2304), own, None, False)
     first = join(got[0], [(0, 1, 2)], [token])[0]
     their_first = swap(first)
-    total, token = product(live_rows, left, ((512, 768),), [first], total, False)
+    total, token = product(live_rows, left, (512,), [first], total, False)
     second = join(got[1], [(0, 1, 2)], [token])[0]
     their_second = swap(second)
-    total, _ = product(live_rows, left, ((2560, 768), (1280, 768)), [their_first, second], total, False)
-    return product(live_rows, left, ((3328, 768),), [their_second], total, True)
+    total, _ = product(live_rows, left, (2560, 1280), [their_first, second], total, False)
+    return product(live_rows, left, (3328,), [their_second], total, True)
 
 
 def solution(mesh):

time: 72.3 us -> 71.6 us (level)
  Pallas kernels: 23.1 us -> 21.3 us
  starting transfers between devices: 36 us -> 37.7 us
    pallas_call x1, Pallas kernels: 3.66 us -> 1.74 us  [lookup(): pl.pallas_call(lookup_kernel, in_specs=[VMEM] * 7, out_specs=[VMEM] * 2,...]
    ppermute x7, starting transfers between devices: 11.1 us -> 12.9 us  [swap(): return lax.ppermute(block, AXES, SWAP)]
    ppermute x3, waiting for transfers between devices: 3.71 us -> 2.6 us  [on_device(): lax.ppermute(h, AXES, route(o))]
  transfers between devices with their start and end apart: 22 -> 22, of which waited for: 8 -> 8; matrix products, arithmetic and copies ran while one was open for 0% -> 0% of each run, Pallas kernels for 27% -> 25%
where the time goes in v4:
time: 71.6 us; the launch traced here: 71.4 us
  starting transfers between devices  37.7 us (53%)
  Pallas kernels  21.3 us (30%)
  waiting for transfers between devices  10.1 us (14%)
  local copies, waits for them, and re-layouts  1.45 us (2%)
  between operations  0.81 us (1%)
    ppermute x10, starting transfers between devices, fetch(): return [lax.ppermute(block, AXES, route(o)) for o in STAGES[stage]]  20.3 us
    ppermute x7, starting transfers between devices, swap(): return lax.ppermute(block, AXES, SWAP)  12.9 us
    pallas_call x4, Pallas kernels, product(): pl.pallas_call(functools.partial(product_kernel, first, last, starts, wid...  12 us
    ppermute x1, waiting for transfers between devices, gather_tables(): return [table, side, swap(side), lax.ppermute(table, AXES, along_x(2, 2))]  3.76 us
    pallas_call x1, Pallas kernels, arrange(): pl.pallas_call(arrange_kernel, in_specs=[VMEM] * 2, out_specs=[VMEM] * 2,...  3.7 us
    pallas_call x1, Pallas kernels, split_cores(): pl.pallas_call(split_kernel, in_specs=[ANY] * 3, out_specs=[VMEM] * 2, ou...  3.44 us
    ppermute x7, waiting for transfers between devices, swap(): return lax.ppermute(block, AXES, SWAP)  2.76 us
    ppermute x3, waiting for transfers between devices, on_device(): lax.ppermute(h, AXES, route(o))  2.6 us
  transfers between devices with their start and end apart: 22, of which 8 were waited for; matrix products, arithmetic and copies ran while one was open for 0% of the time, Pallas kernels for 25%

profile of v4, /device:TPU:1, one launch (start us, length us, event | category | flops | bytes accessed | tf_op | source)
XLA Modules:
  0.0 71.4 jit_solution(8735980917337715434)
XLA Ops:
  0.0 3.2 %collective-permute-start = (f32[8,64]{1,0:T(8,128)}, f32[8,64]{1,0:T(8,128)S(1)}, u32[]{:S(2)}, u32[]{:S(2)}) collective-permute-start(f32[8,64]{1,0:T(8,128)} %bitcast.3), channel_id=1, source_target_pairs={{0,1},{1,0},{2,3},{3,2},{4,5},{5,4},{6,7},{7,6},{8,9},{9,8},{10,11... | collective-permute-start | bytes 6152 | tf_op jit(solution)/shard_map/ppermute | solution.py:47
  3.2 1.0 %collective-permute-done.theirs_ref = f32[8,64]{1,0:T(8,128)S(1)} collective-permute-done((f32[8,64]{1,0:T(8,128)}, f32[8,64]{1,0:T(8,128)S(1)}, u32[]{:S(2)}, u32[]{:S(2)}) %collective-permute-start) | collective-permute-done | bytes 2080 | tf_op jit(solution)/shard_map/ppermute | solution.py:47
  4.3 0.0 copy-start
  4.3 0.8 %copy-done = bf16[2,8,1024]{2,1,0:T(8,128)(2,1)S(1)} copy-done((bf16[2,8,1024]{2,1,0:T(8,128)(2,1)S(1)}, bf16[2,8,1024]{2,1,0:T(8,128)(2,1)}, u32[]{:S(2)}) %copy-start) | copy-done | bytes 32792
  5.0 0.0 copy-start.1
  5.0 0.7 copy-done.1
  5.7 0.0 copy-start.3
  5.7 0.1 shard_map.84.refs_0_
  5.8 5.2 %collective-permute-start.1 = (bf16[2,8,1152]{2,1,0:T(8,128)(2,1)S(1)}, bf16[2,8,1152]{2,1,0:T(8,128)(2,1)S(1)}, u32[]{:S(2)}, u32[]{:S(2)}) collective-permute-start(bf16[2,8,1152]{2,1,0:T(8,128)(2,1)S(1)} %shard_map.84.refs_0_), channel_id=1, source_target_pairs={{32,0},{33,1},{34,2},{35,3},{36,4},{37,5},{38,6},{39,7},{40,8},{41... | collective-permute-start | bytes 110600 | tf_op jit(solution)/shard_map/ppermute | solution.py:43
  11.0 3.4 %shard_map.82 = (bf16[2,528,1024]{2,1,0:T(8,128)(2,1)S(1)}, f32[8,128]{1,0:T(8,128)S(1)}) custom-call(s32[4,4]{1,0:T(4,128)} %coupling_ref.1, s32[1,2048]{1,0:T(1,128)} %bitcast.6, s32[512,2048]{1,0:T(8,128)} %excite_ref.1), custom_call_target="tpu_custom_call" | custom-call | flops 553648128 | bytes 7340032 | tf_op jit(solution)/shard_map/pallas_call | solution.py:119
  14.4 0.0 collective-permute-done.1.refs_1_
  14.5 3.4 %collective-permute-start.2 = (bf16[2,16,1152]{2,1,0:T(8,128)(2,1)S(1)}, bf16[2,16,1152]{2,1,0:T(8,128)(2,1)S(1)}, u32[]{:S(2)}, u32[]{:S(2)}) collective-permute-start(bf16[2,16,1152]{2,1,0:T(8,128)(2,1)S(1)} %shard_map.85.refs_0_), channel_id=1, source_target_pairs={{12,0},{185,1},{14,2},{187,3},{8,4},{189,5},{10,6},{191,7},{20,8},... | collective-permute-start | bytes 221192 | tf_op jit(solution)/shard_map/ppermute | solution.py:43
  17.9 1.2 %collective-permute-start.3 = (bf16[2,16,1152]{2,1,0:T(8,128)(2,1)S(1)}, bf16[2,16,1152]{2,1,0:T(8,128)(2,1)S(1)}, u32[]{:S(2)}, u32[]{:S(2)}) collective-permute-start(bf16[2,16,1152]{2,1,0:T(8,128)(2,1)S(1)} %shard_map.85.refs_0_), channel_id=1, source_target_pairs={{16,0},{49,1},{18,2},{51,3},{20,4},{53,5},{22,6},{55,7},{24,8},{57... | collective-permute-start | bytes 221192 | tf_op jit(solution)/shard_map/ppermute | solution.py:43
  19.1 1.7 %collective-permute-start.4 = (bf16[2,16,1152]{2,1,0:T(8,128)(2,1)S(1)}, bf16[2,16,1152]{2,1,0:T(8,128)(2,1)S(1)}, u32[]{:S(2)}, u32[]{:S(2)}) collective-permute-start(bf16[2,16,1152]{2,1,0:T(8,128)(2,1)S(1)} %shard_map.85.refs_0_), channel_id=1, source_target_pairs={{60,0},{137,1},{62,2},{139,3},{56,4},{141,5},{58,6},{143,7},{4,8},... | collective-permute-start | bytes 221192 | tf_op jit(solution)/shard_map/ppermute | solution.py:43
  20.8 0.0 copy-done.3
  20.8 0.0 copy-start.2
  20.8 3.7 %shard_map.83 = (bf16[8,528,256]{2,1,0:T(8,128)(2,1)S(1)}, f32[8,128]{1,0:T(8,128)S(1)}) custom-call(s32[2,4,8,1,256]{4,3,2,1,0:T(1,128)S(1)} %copy-done.3, bf16[2,528,1024]{2,1,0:T(8,128)(2,1)S(1)} %get-tuple-element.21.signs_ref), custom_call_target="tpu_custom_call" | custom-call | flops 2214592512 | bytes 4194304 | tf_op jit(solution)/shard_map/pallas_call | solution.py:152
  24.5 0.0 collective-permute-done.2.refs_1_
  24.6 0.0 collective-permute-done.3.refs_2_
  24.6 0.2 collective-permute-done.4.refs_3_
  24.8 5.2 %collective-permute-start.5 = (bf16[2,64,1024]{2,1,0:T(8,128)(2,1)S(1)}, bf16[2,64,1024]{2,1,0:T(8,128)(2,1)S(1)}, u32[]{:S(2)}, u32[]{:S(2)}) collective-permute-start(bf16[2,64,1024]{2,1,0:T(8,128)(2,1)S(1)} %get-tuple-element.25.refs_0_), channel_id=1, source_target_pairs={{72,0},{59,1},{74,2},{61,3},{76,4},{63,5},{78,6},{57,7},{80,8},{3,... | collective-permute-start | bytes 786440 | tf_op jit(solution)/shard_map/ppermute | solution.py:43
  29.9 0.0 collective-permute-start.6
  29.9 0.7 collective-permute-start.7
  30.6 3.3 %collective-permute-start.8 = (f32[64,128]{1,0:T(8,128)S(1)}, f32[64,128]{1,0:T(8,128)S(1)}, u32[]{:S(2)}, u32[]{:S(2)}) collective-permute-start(f32[64,128]{1,0:T(8,128)S(1)} %get-tuple-element.26.mine_ref), channel_id=1, source_target_pairs={{0,1},{1,0},{2,3},{3,2},{4,5},{5,4},{6,7},{7,6},{8,9},{9,8},{10,11... | collective-permute-start | bytes 98312 | tf_op jit(solution)/shard_map/ppermute | solution.py:47
  33.9 0.9 %collective-permute-done.8.theirs_ref = f32[64,128]{1,0:T(8,128)S(1)} collective-permute-done((f32[64,128]{1,0:T(8,128)S(1)}, f32[64,128]{1,0:T(8,128)S(1)}, u32[]{:S(2)}, u32[]{:S(2)}) %collective-permute-start.8) | collective-permute-done | bytes 32800 | tf_op jit(solution)/shard_map/ppermute | solution.py:47
  34.8 1.9 %collective-permute-start.10 = (f32[64,128]{1,0:T(8,128)S(1)}, f32[64,128]{1,0:T(8,128)S(1)}, u32[]{:S(2)}, u32[]{:S(2)}) collective-permute-start(f32[64,128]{1,0:T(8,128)S(1)} %shard_map.87.refs_0_), channel_id=1, source_target_pairs={{4,0},{5,1},{6,2},{7,3},{0,4},{1,5},{2,6},{3,7},{12,8},{13,9},{14,... | collective-permute-start | bytes 98312 | tf_op jit(solution)/shard_map/ppermute | solution.py:393
  36.6 0.3 collective-permute-start.9
  37.0 3.8 %collective-permute-done.10.refs_5_.refs_3_ = f32[64,128]{1,0:T(8,128)S(1)} collective-permute-done((f32[64,128]{1,0:T(8,128)S(1)}, f32[64,128]{1,0:T(8,128)S(1)}, u32[]{:S(2)}, u32[]{:S(2)}) %collective-permute-start.10) | collective-permute-done | bytes 32800 | tf_op jit(solution)/shard_map/ppermute | solution.py:393
  40.7 0.4 collective-permute-done.9.refs_4_.refs_1_
  41.1 0.0 collective-permute-done.5.refs_1_
  41.1 0.0 collective-permute-done.6.refs_2_
  41.1 0.0 collective-permute-done.7.refs_3_
  41.1 0.1 shard_map.88
  41.2 2.2 %collective-permute-start.18 = (bf16[2,128,1024]{2,1,0:T(8,128)(2,1)S(1)}, bf16[2,128,1024]{2,1,0:T(8,128)(2,1)S(1)}, u32[]{:S(2)}, u32[]{:S(2)}) collective-permute-start(bf16[2,128,1024]{2,1,0:T(8,128)(2,1)S(1)} %get-tuple-element.27.after_ref.refs_2_), channel_id=1, source_target_pairs={{0,1},{1,0},{2,3},{3,2},{4,5},{5,4},{6,7},{7,6},{8,9},{9,8},{10,11... | collective-permute-start | bytes 1572872 | tf_op jit(solution)/shard_map/ppermute | solution.py:47
  43.5 0.1 collective-permute-start.19
  43.6 1.3 %collective-permute-start.15 = (bf16[2,128,1024]{2,1,0:T(8,128)(2,1)S(1)}, bf16[2,128,1024]{2,1,0:T(8,128)(2,1)S(1)}, u32[]{:S(2)}, u32[]{:S(2)}) collective-permute-start(bf16[2,128,1024]{2,1,0:T(8,128)(2,1)S(1)} %get-tuple-element.27.after_ref.refs_2_), channel_id=1, source_target_pairs={{2,0},{65,1},{4,2},{67,3},{6,4},{69,5},{0,6},{71,7},{10,8},{73,9},... | collective-permute-start | bytes 1572872 | tf_op jit(solution)/shard_map/ppermute | solution.py:43
  44.9 1.5 %collective-permute-start.11 = (f32[64,128]{1,0:T(8,128)S(1)}, f32[64,128]{1,0:T(8,128)S(1)}, u32[]{:S(2)}, u32[]{:S(2)}) collective-permute-start(f32[64,128]{1,0:T(8,128)S(1)} %collective-permute-done.9.refs_4_.refs_1_), channel_id=1, source_target_pairs={{0,1},{1,0},{2,3},{3,2},{4,5},{5,4},{6,7},{7,6},{8,9},{9,8},{10,11... | collective-permute-start | bytes 98312 | tf_op jit(solution)/shard_map/ppermute | solution.py:47
  46.4 0.0 collective-permute-start.16
  46.4 0.9 %collective-permute-done.11.refs_2_ = f32[64,128]{1,0:T(8,128)S(1)} collective-permute-done((f32[64,128]{1,0:T(8,128)S(1)}, f32[64,128]{1,0:T(8,128)S(1)}, u32[]{:S(2)}, u32[]{:S(2)}) %collective-permute-start.11) | collective-permute-done | bytes 32800 | tf_op jit(solution)/shard_map/ppermute | solution.py:47
  47.3 1.5 %collective-permute-start.17 = (bf16[2,128,1024]{2,1,0:T(8,128)(2,1)S(1)}, bf16[2,128,1024]{2,1,0:T(8,128)(2,1)S(1)}, u32[]{:S(2)}, u32[]{:S(2)}) collective-permute-start(bf16[2,128,1024]{2,1,0:T(8,128)(2,1)S(1)} %get-tuple-element.27.after_ref.refs_2_), channel_id=1, source_target_pairs={{8,0},{57,1},{10,2},{59,3},{12,4},{61,5},{14,6},{63,7},{16,8},{1,9... | collective-permute-start | bytes 1572872 | tf_op jit(solution)/shard_map/ppermute | solution.py:43
  48.8 0.0 copy-done.2
  48.8 1.7 %shard_map.89 = (bf16[1024,4096]{1,0:T(8,128)(2,1)S(1)}, f32[8,128]{1,0:T(8,128)S(1)}) custom-call(s32[1,512]{1,0:T(1,128)S(1)} %bitcast.5, bf16[8,528,256]{2,1,0:T(8,128)(2,1)S(1)} %get-tuple-element.22.signs_ref, bf16[2,128,1024]{2,1,0:T(8,128)(2,1)S(1)} %get-tuple-element.27.after_ref.refs_2_, f32[64,128]{1,0:T(8,128)S(1)} %shard_map.87.refs_0_, ...), custom_call_target="tpu_custom_call" | custom-call | flops 1000000 | bytes 1048576 | tf_op jit(solution)/shard_map/pallas_call | solution.py:217
  50.6 0.0 collective-permute-done.18.refs_4_
  50.6 1.9 %collective-permute-start.12 = (bf16[2,128,1024]{2,1,0:T(8,128)(2,1)S(1)}, bf16[2,128,1024]{2,1,0:T(8,128)(2,1)S(1)}, u32[]{:S(2)}, u32[]{:S(2)}) collective-permute-start(bf16[2,128,1024]{2,1,0:T(8,128)(2,1)S(1)} %get-tuple-element.29.refs_3_), channel_id=1, source_target_pairs={{2,0},{65,1},{4,2},{67,3},{6,4},{69,5},{0,6},{71,7},{10,8},{73,9},... | collective-permute-start | bytes 1572872 | tf_op jit(solution)/shard_map/ppermute | solution.py:412
  52.5 0.0 collective-permute-done.19.refs_5_
  52.5 0.2 collective-permute-start.14
  52.7 0.0 collective-permute-done.15.refs_0_
  52.7 0.2 collective-permute-start.13
  53.6 2.5 %shard_map.91 = (f32[2,512,1024]{2,1,0:T(8,128)S(1)}, f32[8,128]{1,0:T(8,128)S(1)}) custom-call(s32[1]{0:T(128)S(6)} %copy.15.refs_0_, bf16[1024,4096]{1,0:T(8,128)(2,1)S(1)} %get-tuple-element.28.refs_1_, bf16[2,128,1024]{2,1,0:T(8,128)(2,1)S(1)} %get-tuple-element.27.after_ref.refs_2_, bf16[2,128,1024]{2,1,0:T(8,128)(2,1)S(1)} %get-tuple-element.29.refs_3_, ...), custom_call_target="tpu_custom_call" | custom-call | flops 1000000 | bytes 1048576 | tf_op jit(solution)/shard_map/pallas_call | solution.py:315
  56.1 0.0 collective-permute-done.16.refs_1_
  56.1 0.4 collective-permute-done.17.refs_2_
  56.5 0.1 shard_map.92.refs_2_
  56.6 0.9 %collective-permute-start.21 = (bf16[2,384,1024]{2,1,0:T(8,128)(2,1)S(1)}, bf16[2,384,1024]{2,1,0:T(8,128)(2,1)S(1)}, u32[]{:S(2)}, u32[]{:S(2)}) collective-permute-start(bf16[2,384,1024]{2,1,0:T(8,128)(2,1)S(1)} %shard_map.92.refs_2_), channel_id=1, source_target_pairs={{0,1},{1,0},{2,3},{3,2},{4,5},{5,4},{6,7},{7,6},{8,9},{9,8},{10,11... | collective-permute-start | bytes 4718600 | tf_op jit(solution)/shard_map/ppermute | solution.py:47
  57.6 2.3 %shard_map.93 = (f32[2,512,1024]{2,1,0:T(8,128)S(1)}, f32[8,128]{1,0:T(8,128)S(1)}) custom-call(s32[1]{0:T(128)S(6)} %copy.15.refs_0_, bf16[1024,4096]{1,0:T(8,128)(2,1)S(1)} %get-tuple-element.28.refs_1_, bf16[2,384,1024]{2,1,0:T(8,128)(2,1)S(1)} %shard_map.92.refs_2_, f32[2,512,1024]{2,1,0:T(8,128)S(1)} %get-tuple-element.33.refs_3_), custom_call_target="tpu_custom_call", output_to_operand_aliasing={{0}: (3, {})} | custom-call | flops 1000000 | bytes 1048576 | tf_op jit(solution)/shard_map/pallas_call | solution.py:315
  59.9 2.6 %collective-permute-done.14.refs_2_ = bf16[2,128,1024]{2,1,0:T(8,128)(2,1)S(1)} collective-permute-done((bf16[2,128,1024]{2,1,0:T(8,128)(2,1)S(1)}, bf16[2,128,1024]{2,1,0:T(8,128)(2,1)S(1)}, u32[]{:S(2)}, u32[]{:S(2)}) %collective-permute-start.14) | collective-permute-done | bytes 524320 | tf_op jit(solution)/shard_map/ppermute | solution.py:412
  62.5 0.0 collective-permute-done.12.refs_0_
  62.5 0.0 collective-permute-done.13.refs_1_
  62.5 0.1 shard_map.94.refs_3_
  62.6 1.6 %collective-permute-start.20 = (bf16[2,384,1024]{2,1,0:T(8,128)(2,1)S(1)}, bf16[2,384,1024]{2,1,0:T(8,128)(2,1)S(1)}, u32[]{:S(2)}, u32[]{:S(2)}) collective-permute-start(bf16[2,384,1024]{2,1,0:T(8,128)(2,1)S(1)} %shard_map.94.refs_3_), channel_id=1, source_target_pairs={{0,1},{1,0},{2,3},{3,2},{4,5},{5,4},{6,7},{7,6},{8,9},{9,8},{10,11... | collective-permute-start | bytes 4718600 | tf_op jit(solution)/shard_map/ppermute | solution.py:47
  64.2 0.0 collective-permute-done.21.refs_2_
  64.2 3.9 %shard_map.95 = (f32[2,512,1024]{2,1,0:T(8,128)S(1)}, f32[8,128]{1,0:T(8,128)}) custom-call(s32[1]{0:T(128)S(6)} %copy.15.refs_0_, bf16[1024,4096]{1,0:T(8,128)(2,1)S(1)} %get-tuple-element.28.refs_1_, bf16[2,384,1024]{2,1,0:T(8,128)(2,1)S(1)} %collective-permute-done.21.refs_2_, ...), custom_call_target="tpu_custom_call", output_to_operand_aliasing={{0}: (4, {})} | custom-call | flops 1000000 | bytes 1048576 | tf_op jit(solution)/shard_map/pallas_call | solution.py:315
  68.1 0.0 collective-permute-done.20.refs_2_
  68.1 3.3 %shard_map.96 = f32[2,512,1024]{2,1,0:T(8,128)} custom-call(s32[1]{0:T(128)S(6)} %copy.15.refs_0_, bf16[1024,4096]{1,0:T(8,128)(2,1)S(1)} %get-tuple-element.28.refs_1_, bf16[2,384,1024]{2,1,0:T(8,128)(2,1)S(1)} %collective-permute-done.20.refs_2_, f32[2,512,1024]{2,1,0:T(8,128)S(1)} %get-tuple-element.36.refs_3_), custom_call_target="tpu_custom_call" | custom-call | flops 1000000 | bytes 1048576 | tf_op jit(solution)/shard_map/pallas_call | solution.py:315
  (4 shorter events, 0.0 us)
Async XLA Ops:
  0.0 4.3 %collective-permute-start = (f32[8,64]{1,0:T(8,128)}, f32[8,64]{1,0:T(8,128)S(1)}, u32[]{:S(2)}, u32[]{:S(2)}) collective-permute-start(f32[8,64]{1,0:T(8,128)} %bitcast.3), channel_id=1, source_target_pairs={{0,1},{1,0},{2,3},{3,2},{4,5},{5,4},{6,7},{7,6},{8,9},{9,8},{10,11... | collective-permute-start | bytes 6152 | tf_op jit(solution)/shard_map/ppermute | solution.py:47
  4.3 0.8 %copy-start = (bf16[2,8,1024]{2,1,0:T(8,128)(2,1)S(1)}, bf16[2,8,1024]{2,1,0:T(8,128)(2,1)}, u32[]{:S(2)}) copy-start(bf16[2,8,1024]{2,1,0:T(8,128)(2,1)} %coeffs_ref.1) | copy-start | bytes 98308
  5.0 0.7 copy-start.1
  5.7 15.1 %copy-start.3 = (s32[2,4,8,1,256]{4,3,2,1,0:T(1,128)S(1)}, s32[2,4,8,1,256]{4,3,2,1,0:T(1,128)}, u32[]{:S(2)}) copy-start(s32[2,4,8,1,256]{4,3,2,1,0:T(1,128)} %constant.2.clone.order_ref) | copy-start | bytes 196612
  5.8 8.7 %collective-permute-start.1 = (bf16[2,8,1152]{2,1,0:T(8,128)(2,1)S(1)}, bf16[2,8,1152]{2,1,0:T(8,128)(2,1)S(1)}, u32[]{:S(2)}, u32[]{:S(2)}) collective-permute-start(bf16[2,8,1152]{2,1,0:T(8,128)(2,1)S(1)} %shard_map.84.refs_0_), channel_id=1, source_target_pairs={{32,0},{33,1},{34,2},{35,3},{36,4},{37,5},{38,6},{39,7},{40,8},{41... | collective-permute-start | bytes 110600 | tf_op jit(solution)/shard_map/ppermute | solution.py:43
  14.5 10.1 %collective-permute-start.2 = (bf16[2,16,1152]{2,1,0:T(8,128)(2,1)S(1)}, bf16[2,16,1152]{2,1,0:T(8,128)(2,1)S(1)}, u32[]{:S(2)}, u32[]{:S(2)}) collective-permute-start(bf16[2,16,1152]{2,1,0:T(8,128)(2,1)S(1)} %shard_map.85.refs_0_), channel_id=1, source_target_pairs={{12,0},{185,1},{14,2},{187,3},{8,4},{189,5},{10,6},{191,7},{20,8},... | collective-permute-start | bytes 221192 | tf_op jit(solution)/shard_map/ppermute | solution.py:43
  17.9 6.6 %collective-permute-start.3 = (bf16[2,16,1152]{2,1,0:T(8,128)(2,1)S(1)}, bf16[2,16,1152]{2,1,0:T(8,128)(2,1)S(1)}, u32[]{:S(2)}, u32[]{:S(2)}) collective-permute-start(bf16[2,16,1152]{2,1,0:T(8,128)(2,1)S(1)} %shard_map.85.refs_0_), channel_id=1, source_target_pairs={{16,0},{49,1},{18,2},{51,3},{20,4},{53,5},{22,6},{55,7},{24,8},{57... | collective-permute-start | bytes 221192 | tf_op jit(solution)/shard_map/ppermute | solution.py:43
  19.1 5.6 %collective-permute-start.4 = (bf16[2,16,1152]{2,1,0:T(8,128)(2,1)S(1)}, bf16[2,16,1152]{2,1,0:T(8,128)(2,1)S(1)}, u32[]{:S(2)}, u32[]{:S(2)}) collective-permute-start(bf16[2,16,1152]{2,1,0:T(8,128)(2,1)S(1)} %shard_map.85.refs_0_), channel_id=1, source_target_pairs={{60,0},{137,1},{62,2},{139,3},{56,4},{141,5},{58,6},{143,7},{4,8},... | collective-permute-start | bytes 221192 | tf_op jit(solution)/shard_map/ppermute | solution.py:43
  20.8 28.0 %copy-start.2 = (s32[512]{0:T(512)S(1)}, s32[512]{0:T(512)}, u32[]{:S(2)}) copy-start(s32[512]{0:T(512)} %param.11) | copy-start | bytes 6148
  24.8 16.4 %collective-permute-start.5 = (bf16[2,64,1024]{2,1,0:T(8,128)(2,1)S(1)}, bf16[2,64,1024]{2,1,0:T(8,128)(2,1)S(1)}, u32[]{:S(2)}, u32[]{:S(2)}) collective-permute-start(bf16[2,64,1024]{2,1,0:T(8,128)(2,1)S(1)} %get-tuple-element.25.refs_0_), channel_id=1, source_target_pairs={{72,0},{59,1},{74,2},{61,3},{76,4},{63,5},{78,6},{57,7},{80,8},{3,... | collective-permute-start | bytes 786440 | tf_op jit(solution)/shard_map/ppermute | solution.py:43
  29.9 11.2 %collective-permute-start.6 = (bf16[2,64,1024]{2,1,0:T(8,128)(2,1)S(1)}, bf16[2,64,1024]{2,1,0:T(8,128)(2,1)S(1)}, u32[]{:S(2)}, u32[]{:S(2)}) collective-permute-start(bf16[2,64,1024]{2,1,0:T(8,128)(2,1)S(1)} %get-tuple-element.25.refs_0_), channel_id=1, source_target_pairs={{128,0},{5,1},{130,2},{7,3},{132,4},{1,5},{134,6},{3,7},{136,8},{1... | collective-permute-start | bytes 786440 | tf_op jit(solution)/shard_map/ppermute | solution.py:43
  29.9 11.2 %collective-permute-start.7 = (bf16[2,64,1024]{2,1,0:T(8,128)(2,1)S(1)}, bf16[2,64,1024]{2,1,0:T(8,128)(2,1)S(1)}, u32[]{:S(2)}, u32[]{:S(2)}) collective-permute-start(bf16[2,64,1024]{2,1,0:T(8,128)(2,1)S(1)} %get-tuple-element.25.refs_0_), channel_id=1, source_target_pairs={{200,0},{63,1},{202,2},{57,3},{204,4},{59,5},{206,6},{61,7},{208,8... | collective-permute-start | bytes 786440 | tf_op jit(solution)/shard_map/ppermute | solution.py:43
  30.6 4.2 %collective-permute-start.8 = (f32[64,128]{1,0:T(8,128)S(1)}, f32[64,128]{1,0:T(8,128)S(1)}, u32[]{:S(2)}, u32[]{:S(2)}) collective-permute-start(f32[64,128]{1,0:T(8,128)S(1)} %get-tuple-element.26.mine_ref), channel_id=1, source_target_pairs={{0,1},{1,0},{2,3},{3,2},{4,5},{5,4},{6,7},{7,6},{8,9},{9,8},{10,11... | collective-permute-start | bytes 98312 | tf_op jit(solution)/shard_map/ppermute | solution.py:47
  34.8 5.9 %collective-permute-start.10 = (f32[64,128]{1,0:T(8,128)S(1)}, f32[64,128]{1,0:T(8,128)S(1)}, u32[]{:S(2)}, u32[]{:S(2)}) collective-permute-start(f32[64,128]{1,0:T(8,128)S(1)} %shard_map.87.refs_0_), channel_id=1, source_target_pairs={{4,0},{5,1},{6,2},{7,3},{0,4},{1,5},{2,6},{3,7},{12,8},{13,9},{14,... | collective-permute-start | bytes 98312 | tf_op jit(solution)/shard_map/ppermute | solution.py:393
  36.6 4.5 %collective-permute-start.9 = (f32[64,128]{1,0:T(8,128)S(1)}, f32[64,128]{1,0:T(8,128)S(1)}, u32[]{:S(2)}, u32[]{:S(2)}) collective-permute-start(f32[64,128]{1,0:T(8,128)S(1)} %shard_map.87.refs_0_), channel_id=1, source_target_pairs={{2,0},{7,1},{4,2},{1,3},{6,4},{3,5},{0,6},{5,7},{10,8},{15,9},{12,... | collective-permute-start | bytes 98312 | tf_op jit(solution)/shard_map/ppermute | solution.py:392
  41.2 9.3 %collective-permute-start.18 = (bf16[2,128,1024]{2,1,0:T(8,128)(2,1)S(1)}, bf16[2,128,1024]{2,1,0:T(8,128)(2,1)S(1)}, u32[]{:S(2)}, u32[]{:S(2)}) collective-permute-start(bf16[2,128,1024]{2,1,0:T(8,128)(2,1)S(1)} %get-tuple-element.27.after_ref.refs_2_), channel_id=1, source_target_pairs={{0,1},{1,0},{2,3},{3,2},{4,5},{5,4},{6,7},{7,6},{8,9},{9,8},{10,11... | collective-permute-start | bytes 1572872 | tf_op jit(solution)/shard_map/ppermute | solution.py:47
  43.5 9.0 %collective-permute-start.19 = (bf16[2,128,1024]{2,1,0:T(8,128)(2,1)S(1)}, bf16[2,128,1024]{2,1,0:T(8,128)(2,1)S(1)}, u32[]{:S(2)}, u32[]{:S(2)}) collective-permute-start(bf16[2,128,1024]{2,1,0:T(8,128)(2,1)S(1)} %get-tuple-element.29.refs_3_), channel_id=1, source_target_pairs={{0,1},{1,0},{2,3},{3,2},{4,5},{5,4},{6,7},{7,6},{8,9},{9,8},{10,11... | collective-permute-start | bytes 1572872 | tf_op jit(solution)/shard_map/ppermute | solution.py:47
  43.6 9.2 %collective-permute-start.15 = (bf16[2,128,1024]{2,1,0:T(8,128)(2,1)S(1)}, bf16[2,128,1024]{2,1,0:T(8,128)(2,1)S(1)}, u32[]{:S(2)}, u32[]{:S(2)}) collective-permute-start(bf16[2,128,1024]{2,1,0:T(8,128)(2,1)S(1)} %get-tuple-element.27.after_ref.refs_2_), channel_id=1, source_target_pairs={{2,0},{65,1},{4,2},{67,3},{6,4},{69,5},{0,6},{71,7},{10,8},{73,9},... | collective-permute-start | bytes 1572872 | tf_op jit(solution)/shard_map/ppermute | solution.py:43
  44.9 2.4 %collective-permute-start.11 = (f32[64,128]{1,0:T(8,128)S(1)}, f32[64,128]{1,0:T(8,128)S(1)}, u32[]{:S(2)}, u32[]{:S(2)}) collective-permute-start(f32[64,128]{1,0:T(8,128)S(1)} %collective-permute-done.9.refs_4_.refs_1_), channel_id=1, source_target_pairs={{0,1},{1,0},{2,3},{3,2},{4,5},{5,4},{6,7},{7,6},{8,9},{9,8},{10,11... | collective-permute-start | bytes 98312 | tf_op jit(solution)/shard_map/ppermute | solution.py:47
  46.4 9.7 %collective-permute-start.16 = (bf16[2,128,1024]{2,1,0:T(8,128)(2,1)S(1)}, bf16[2,128,1024]{2,1,0:T(8,128)(2,1)S(1)}, u32[]{:S(2)}, u32[]{:S(2)}) collective-permute-start(bf16[2,128,1024]{2,1,0:T(8,128)(2,1)S(1)} %get-tuple-element.27.after_ref.refs_2_), channel_id=1, source_target_pairs={{6,0},{193,1},{0,2},{195,3},{2,4},{197,5},{4,6},{199,7},{14,8},{20... | collective-permute-start | bytes 1572872 | tf_op jit(solution)/shard_map/ppermute | solution.py:43
  47.3 9.2 %collective-permute-start.17 = (bf16[2,128,1024]{2,1,0:T(8,128)(2,1)S(1)}, bf16[2,128,1024]{2,1,0:T(8,128)(2,1)S(1)}, u32[]{:S(2)}, u32[]{:S(2)}) collective-permute-start(bf16[2,128,1024]{2,1,0:T(8,128)(2,1)S(1)} %get-tuple-element.27.after_ref.refs_2_), channel_id=1, source_target_pairs={{8,0},{57,1},{10,2},{59,3},{12,4},{61,5},{14,6},{63,7},{16,8},{1,9... | collective-permute-start | bytes 1572872 | tf_op jit(solution)/shard_map/ppermute | solution.py:43
  50.6 11.8 %collective-permute-start.12 = (bf16[2,128,1024]{2,1,0:T(8,128)(2,1)S(1)}, bf16[2,128,1024]{2,1,0:T(8,128)(2,1)S(1)}, u32[]{:S(2)}, u32[]{:S(2)}) collective-permute-start(bf16[2,128,1024]{2,1,0:T(8,128)(2,1)S(1)} %get-tuple-element.29.refs_3_), channel_id=1, source_target_pairs={{2,0},{65,1},{4,2},{67,3},{6,4},{69,5},{0,6},{71,7},{10,8},{73,9},... | collective-permute-start | bytes 1572872 | tf_op jit(solution)/shard_map/ppermute | solution.py:412
  52.5 9.9 %collective-permute-start.14 = (bf16[2,128,1024]{2,1,0:T(8,128)(2,1)S(1)}, bf16[2,128,1024]{2,1,0:T(8,128)(2,1)S(1)}, u32[]{:S(2)}, u32[]{:S(2)}) collective-permute-start(bf16[2,128,1024]{2,1,0:T(8,128)(2,1)S(1)} %shard_map.90), channel_id=1, source_target_pairs={{8,0},{57,1},{10,2},{59,3},{12,4},{61,5},{14,6},{63,7},{16,8},{1,9... | collective-permute-start | bytes 1572872 | tf_op jit(solution)/shard_map/ppermute | solution.py:412
  52.7 9.7 %collective-permute-start.13 = (bf16[2,128,1024]{2,1,0:T(8,128)(2,1)S(1)}, bf16[2,128,1024]{2,1,0:T(8,128)(2,1)S(1)}, u32[]{:S(2)}, u32[]{:S(2)}) collective-permute-start(bf16[2,128,1024]{2,1,0:T(8,128)(2,1)S(1)} %get-tuple-element.29.refs_3_), channel_id=1, source_target_pairs={{6,0},{193,1},{0,2},{195,3},{2,4},{197,5},{4,6},{199,7},{14,8},{20... | collective-permute-start | bytes 1572872 | tf_op jit(solution)/shard_map/ppermute | solution.py:412
  56.6 7.5 %collective-permute-start.21 = (bf16[2,384,1024]{2,1,0:T(8,128)(2,1)S(1)}, bf16[2,384,1024]{2,1,0:T(8,128)(2,1)S(1)}, u32[]{:S(2)}, u32[]{:S(2)}) collective-permute-start(bf16[2,384,1024]{2,1,0:T(8,128)(2,1)S(1)} %shard_map.92.refs_2_), channel_id=1, source_target_pairs={{0,1},{1,0},{2,3},{3,2},{4,5},{5,4},{6,7},{7,6},{8,9},{9,8},{10,11... | collective-permute-start | bytes 4718600 | tf_op jit(solution)/shard_map/ppermute | solution.py:47
  62.6 5.5 %collective-permute-start.20 = (bf16[2,384,1024]{2,1,0:T(8,128)(2,1)S(1)}, bf16[2,384,1024]{2,1,0:T(8,128)(2,1)S(1)}, u32[]{:S(2)}, u32[]{:S(2)}) collective-permute-start(bf16[2,384,1024]{2,1,0:T(8,128)(2,1)S(1)} %shard_map.94.refs_3_), channel_id=1, source_target_pairs={{0,1},{1,0},{2,3},{3,2},{4,5},{5,4},{6,7},{7,6},{8,9},{9,8},{10,11... | collective-permute-start | bytes 4718600 | tf_op jit(solution)/shard_map/ppermute | solution.py:47

commit v5 on v4

--- a/solution.py
+++ b/solution.py
@@ -59,7 +59,7 @@
 
 def order_constants():
     lasts = HERE + STAGES[3]
-    own = [(lasts[0], 0), (lasts[0], 1)] + [(o, h) for h in (0, 1) for o in lasts[1:]]
+    own = [(o, h) for o in lasts for h in (0, 1)]
     table = np.zeros((2, 4, 8, 1, 256), np.int32)
     for core in (0, 1):
         for pair in range(8):
@@ -206,11 +206,7 @@
 
 
 def column(chunk):
-    sibling, chunk = divmod(chunk, 8)
-    if chunk < 2:
-        return sibling * 2048 + chunk * 256, 128
-    group, place = divmod(chunk - 2, 3)
-    return sibling * 2048 + 512 + group * 768 + place * 128, 384
+    return chunk // 2 * 512 + chunk % 2 * 128, 256
 
 
 def lookup(target, tables, signs, after):
@@ -249,20 +245,20 @@
     )(*[near(p) for p in pieces], *after)
 
 
-def relay_kernel(block_ref, after_ref, out_ref):
-    del block_ref, after_ref, out_ref
-
-
-def relay(block, after):
+def relay_kernel(*refs):
+    del refs
+
+
+def relay(blocks, after):
     return pl.pallas_call(
         relay_kernel,
-        in_specs=[VMEM] * 2,
-        out_specs=VMEM,
-        out_shape=pltpu.VMEM(block.shape, block.dtype),
-        input_output_aliases={0: 0},
+        in_specs=[VMEM] * (len(blocks) + 1),
+        out_specs=[VMEM] * len(blocks),
+        out_shape=[pltpu.VMEM(block.shape, block.dtype) for block in blocks],
+        input_output_aliases={k: k for k in range(len(blocks))},
         compiler_params=pltpu.CompilerParams(vmem_limit_bytes=2 * MIB),
         cost_estimate=pl.CostEstimate(flops=0, bytes_accessed=0, transcendentals=0),
-    )(near(block), after)
+    )(*[near(block) for block in blocks], after)
 
 
 def product_kernel(first, last, starts, width, *refs):
@@ -351,7 +347,7 @@
         out_shape=pltpu.VMEM((2, 8, 1152), jnp.bfloat16),
         compiler_params=pltpu.CompilerParams(vmem_limit_bytes=2 * MIB),
         cost_estimate=pl.CostEstimate(flops=0, bytes_accessed=1 << 16, transcendentals=0),
-    )(coeffs, mine, theirs)
+    )(*[pltpu.with_memory_space_constraint(a, pltpu.HBM) for a in (coeffs, mine)], theirs)
 
 
 def unpack_kernel(*refs):
@@ -401,24 +397,19 @@
     arranged, token = arrange(ORDER, signs)
     slab, table = unpack([packed] + fetch(packed, 1), token)
     tables = gather_tables(table)
-    halves = list(
-        join([slab] + fetch(slab, 2), [(0, 1), (2, 3), (2, 3)], [near(tables[1]), near(tables[3])])
-    )
-    spare = halves.pop()
-    left, token = lookup(target_orb[None, :], tables, arranged, halves[0])
-    late = relay(spare, token)
-
-    got = [fetch(halves[0], 3)]
-    got.append([lax.ppermute(h, AXES, route(o)) for h, o in zip((halves[1], halves[1], late), STAGES[3])])
-    own = halves + [swap(half) for half in halves]
-    total, token = product(live_rows, left, (0, 256, 2048, 2304), own, None, False)
-    first = join(got[0], [(0, 1, 2)], [token])[0]
-    their_first = swap(first)
-    total, token = product(live_rows, left, (512,), [first], total, False)
-    second = join(got[1], [(0, 1, 2)], [token])[0]
-    their_second = swap(second)
-    total, _ = product(live_rows, left, (2560, 1280), [their_first, second], total, False)
-    return product(live_rows, left, (3328,), [their_second], total, True)
+    slab = join([slab] + fetch(slab, 2), [(0, 1, 2, 3)], [near(tables[1]), near(tables[3])])[0]
+    left, _ = lookup(target_orb[None, :], tables, arranged, slab)
+
+    got = fetch(slab, 3)
+    total, token = product(live_rows, left, (0, 2048), [slab, swap(slab)], None, False)
+    third = relay(got[2:], token)[0]
+    their_third = swap(third)
+    total, token = product(live_rows, left, (1536,), [third], total, False)
+    got = [relay([block], token)[0] for block in got[:2]]
+    swapped = [swap(block) for block in got]
+    total, _ = product(live_rows, left, (512, 1024), got, total, False)
+    total, _ = product(live_rows, left, (3584, 3072), [their_third, swapped[1]], total, False)
+    return product(live_rows, left, (2560,), swapped[:1], total, True)
 
 
 def solution(mesh):

time: 71.6 us -> 70.3 us (0.982)
  starting transfers between devices: 37.7 us -> 32.9 us
  waiting for transfers between devices: 10.1 us -> 13.9 us
  local copies, waits for them, and re-layouts: 1.45 us -> 0.01 us
  Pallas kernels: 21.3 us -> 22.5 us
    ppermute x10, waiting for transfers between devices: 0.57 us -> 7.77 us  [fetch(): return [lax.ppermute(block, AXES, route(o)) for o in STAGES[stage]]]
    ppermute x7, starting transfers between devices: 12.9 us -> 10.3 us  [swap(): return lax.ppermute(block, AXES, SWAP)]
    ppermute x3 -> x0, waiting for transfers between devices: 2.6 us -> none  [on_device(): lax.ppermute(h, AXES, route(o))]
    ppermute x3 -> x0, starting transfers between devices: 2.36 us -> none  [on_device(): lax.ppermute(h, AXES, route(o))]
    ppermute x1, waiting for transfers between devices: 3.76 us -> 2.19 us  [gather_tables(): return [table, side, swap(side), lax.ppermute(table, AXES, along_x(2, 2))]]
    unnamed x8 -> x4, local copies, waits for them, and re-layouts: 1.45 us -> 0.01 us
    ppermute x1, waiting for transfers between devices: 0.41 us -> 1.43 us  [gather_tables(): side = lax.ppermute(table, AXES, along_x(1, -1))]
    pallas_call x1, Pallas kernels: 0.08 us -> 0.83 us  [pack(): pl.pallas_call(pack_kernel, in_specs=[VMEM] * 3, out_specs=VMEM, out_shap...]
  transfers between devices with their start and end apart: 22 -> 19, of which waited for: 8 -> 10; matrix products, arithmetic and copies ran while one was open for 0% -> 0% of each run, Pallas kernels for 25% -> 27%
where the time goes in v5:
time: 70.3 us; the launch traced here: 70.1 us
  starting transfers between devices  32.9 us (47%)
  Pallas kernels  22.5 us (32%)
  waiting for transfers between devices  13.9 us (20%)
  between operations  0.79 us (1%)
    ppermute x10, starting transfers between devices, fetch(): return [lax.ppermute(block, AXES, route(o)) for o in STAGES[stage]]  20.5 us
    pallas_call x5, Pallas kernels, product(): pl.pallas_call(functools.partial(product_kernel, first, last, starts, wid...  12.7 us
    ppermute x7, starting transfers between devices, swap(): return lax.ppermute(block, AXES, SWAP)  10.3 us
    ppermute x10, waiting for transfers between devices, fetch(): return [lax.ppermute(block, AXES, route(o)) for o in STAGES[stage]]  7.77 us
    pallas_call x1, Pallas kernels, arrange(): pl.pallas_call(arrange_kernel, in_specs=[VMEM] * 2, out_specs=[VMEM] * 2,...  3.7 us
    pallas_call x1, Pallas kernels, split_cores(): pl.pallas_call(split_kernel, in_specs=[ANY] * 3, out_specs=[VMEM] * 2, ou...  3.44 us
    ppermute x7, waiting for transfers between devices, swap(): return lax.ppermute(block, AXES, SWAP)  2.55 us
    ppermute x1, waiting for transfers between devices, gather_tables(): return [table, side, swap(side), lax.ppermute(table, AXES, along_x(2, 2))]  2.19 us
  transfers between devices with their start and end apart: 19, of which 10 were waited for; matrix products, arithmetic and copies ran while one was open for 0% of the time, Pallas kernels for 27%

profile of v5, /device:TPU:1, one launch (start us, length us, event | category | flops | bytes accessed | tf_op | source)
XLA Modules:
  0.0 70.1 jit_solution(10333810303885876333)
XLA Ops:
  0.0 0.0 copy-start.1
  0.0 3.2 %collective-permute-start = (f32[8,64]{1,0:T(8,128)}, f32[8,64]{1,0:T(8,128)S(1)}, u32[]{:S(2)}, u32[]{:S(2)}) collective-permute-start(f32[8,64]{1,0:T(8,128)} %bitcast.5), channel_id=1, source_target_pairs={{0,1},{1,0},{2,3},{3,2},{4,5},{5,4},{6,7},{7,6},{8,9},{9,8},{10,11... | collective-permute-start | bytes 6152 | tf_op jit(solution)/shard_map/ppermute | solution.py:47
  3.2 1.0 %collective-permute-done.theirs_ref = f32[8,64]{1,0:T(8,128)S(1)} collective-permute-done((f32[8,64]{1,0:T(8,128)}, f32[8,64]{1,0:T(8,128)S(1)}, u32[]{:S(2)}, u32[]{:S(2)}) %collective-permute-start) | collective-permute-done | bytes 2080 | tf_op jit(solution)/shard_map/ppermute | solution.py:47
  4.3 0.8 %shard_map.84.refs_0_ = bf16[2,8,1152]{2,1,0:T(8,128)(2,1)S(1)} custom-call(bf16[2,8,1024]{2,1,0:T(8,128)(2,1)} %coeffs_ref.1, f32[8,64]{1,0:T(8,128)} %bitcast.6, f32[8,64]{1,0:T(8,128)S(1)} %collective-permute-done.theirs_ref), custom_call_target="tpu_custom_call" | custom-call | bytes 65536 | tf_op jit(solution)/shard_map/pallas_call | solution.py:343
  5.1 5.2 %collective-permute-start.1 = (bf16[2,8,1152]{2,1,0:T(8,128)(2,1)S(1)}, bf16[2,8,1152]{2,1,0:T(8,128)(2,1)S(1)}, u32[]{:S(2)}, u32[]{:S(2)}) collective-permute-start(bf16[2,8,1152]{2,1,0:T(8,128)(2,1)S(1)} %shard_map.84.refs_0_), channel_id=1, source_target_pairs={{32,0},{33,1},{34,2},{35,3},{36,4},{37,5},{38,6},{39,7},{40,8},{41... | collective-permute-start | bytes 110600 | tf_op jit(solution)/shard_map/ppermute | solution.py:43
  10.3 3.4 %shard_map.82 = (bf16[2,528,1024]{2,1,0:T(8,128)(2,1)S(1)}, f32[8,128]{1,0:T(8,128)S(1)}) custom-call(s32[4,4]{1,0:T(4,128)} %coupling_ref.1, s32[1,2048]{1,0:T(1,128)} %bitcast.4, s32[512,2048]{1,0:T(8,128)} %excite_ref.1), custom_call_target="tpu_custom_call" | custom-call | flops 553648128 | bytes 7340032 | tf_op jit(solution)/shard_map/pallas_call | solution.py:119
  13.8 0.0 collective-permute-done.1.refs_1_
  13.8 4.7 %collective-permute-start.4 = (bf16[2,16,1152]{2,1,0:T(8,128)(2,1)S(1)}, bf16[2,16,1152]{2,1,0:T(8,128)(2,1)S(1)}, u32[]{:S(2)}, u32[]{:S(2)}) collective-permute-start(bf16[2,16,1152]{2,1,0:T(8,128)(2,1)S(1)} %shard_map.85.refs_0_), channel_id=1, source_target_pairs={{60,0},{137,1},{62,2},{139,3},{56,4},{141,5},{58,6},{143,7},{4,8},... | collective-permute-start | bytes 221192 | tf_op jit(solution)/shard_map/ppermute | solution.py:43
  18.5 0.0 collective-permute-start.3
  18.5 0.4 collective-permute-start.2
  18.9 0.0 copy-done.1
  18.9 0.0 copy-start
  18.9 3.7 %shard_map.83 = (bf16[8,528,256]{2,1,0:T(8,128)(2,1)S(1)}, f32[8,128]{1,0:T(8,128)S(1)}) custom-call(s32[2,4,8,1,256]{4,3,2,1,0:T(1,128)S(1)} %copy-done.1, bf16[2,528,1024]{2,1,0:T(8,128)(2,1)S(1)} %get-tuple-element.18.signs_ref), custom_call_target="tpu_custom_call" | custom-call | flops 2214592512 | bytes 4194304 | tf_op jit(solution)/shard_map/pallas_call | solution.py:152
  22.6 0.0 collective-permute-done.4.refs_3_
  22.7 1.9 %collective-permute-done.3.refs_2_ = bf16[2,16,1152]{2,1,0:T(8,128)(2,1)S(1)} collective-permute-done((bf16[2,16,1152]{2,1,0:T(8,128)(2,1)S(1)}, bf16[2,16,1152]{2,1,0:T(8,128)(2,1)S(1)}, u32[]{:S(2)}, u32[]{:S(2)}) %collective-permute-start.3) | collective-permute-done | bytes 73760 | tf_op jit(solution)/shard_map/ppermute | solution.py:43
  24.5 0.9 %collective-permute-done.2.refs_1_ = bf16[2,16,1152]{2,1,0:T(8,128)(2,1)S(1)} collective-permute-done((bf16[2,16,1152]{2,1,0:T(8,128)(2,1)S(1)}, bf16[2,16,1152]{2,1,0:T(8,128)(2,1)S(1)}, u32[]{:S(2)}, u32[]{:S(2)}) %collective-permute-start.2) | collective-permute-done | bytes 73760 | tf_op jit(solution)/shard_map/ppermute | solution.py:43
  25.5 0.3 collective-permute-start.7
  25.8 2.5 %collective-permute-start.6 = (bf16[2,64,1024]{2,1,0:T(8,128)(2,1)S(1)}, bf16[2,64,1024]{2,1,0:T(8,128)(2,1)S(1)}, u32[]{:S(2)}, u32[]{:S(2)}) collective-permute-start(bf16[2,64,1024]{2,1,0:T(8,128)(2,1)S(1)} %get-tuple-element.22.refs_0_), channel_id=1, source_target_pairs={{128,0},{5,1},{130,2},{7,3},{132,4},{1,5},{134,6},{3,7},{136,8},{1... | collective-permute-start | bytes 786440 | tf_op jit(solution)/shard_map/ppermute | solution.py:43
  28.3 2.8 %collective-permute-start.5 = (bf16[2,64,1024]{2,1,0:T(8,128)(2,1)S(1)}, bf16[2,64,1024]{2,1,0:T(8,128)(2,1)S(1)}, u32[]{:S(2)}, u32[]{:S(2)}) collective-permute-start(bf16[2,64,1024]{2,1,0:T(8,128)(2,1)S(1)} %get-tuple-element.22.refs_0_), channel_id=1, source_target_pairs={{72,0},{59,1},{74,2},{61,3},{76,4},{63,5},{78,6},{57,7},{80,8},{3,... | collective-permute-start | bytes 786440 | tf_op jit(solution)/shard_map/ppermute | solution.py:43
  31.1 4.4 %collective-permute-start.8 = (f32[64,128]{1,0:T(8,128)S(1)}, f32[64,128]{1,0:T(8,128)S(1)}, u32[]{:S(2)}, u32[]{:S(2)}) collective-permute-start(f32[64,128]{1,0:T(8,128)S(1)} %get-tuple-element.23.mine_ref), channel_id=1, source_target_pairs={{0,1},{1,0},{2,3},{3,2},{4,5},{5,4},{6,7},{7,6},{8,9},{9,8},{10,11... | collective-permute-start | bytes 98312 | tf_op jit(solution)/shard_map/ppermute | solution.py:47
  35.4 0.9 %collective-permute-done.8.theirs_ref = f32[64,128]{1,0:T(8,128)S(1)} collective-permute-done((f32[64,128]{1,0:T(8,128)S(1)}, f32[64,128]{1,0:T(8,128)S(1)}, u32[]{:S(2)}, u32[]{:S(2)}) %collective-permute-start.8) | collective-permute-done | bytes 32800 | tf_op jit(solution)/shard_map/ppermute | solution.py:47
  36.3 1.6 %collective-permute-start.10 = (f32[64,128]{1,0:T(8,128)S(1)}, f32[64,128]{1,0:T(8,128)S(1)}, u32[]{:S(2)}, u32[]{:S(2)}) collective-permute-start(f32[64,128]{1,0:T(8,128)S(1)} %shard_map.87.refs_0_), channel_id=1, source_target_pairs={{4,0},{5,1},{6,2},{7,3},{0,4},{1,5},{2,6},{3,7},{12,8},{13,9},{14,... | collective-permute-start | bytes 98312 | tf_op jit(solution)/shard_map/ppermute | solution.py:389
  38.0 0.5 collective-permute-start.9
  38.4 2.2 %collective-permute-done.10.refs_5_.refs_3_ = f32[64,128]{1,0:T(8,128)S(1)} collective-permute-done((f32[64,128]{1,0:T(8,128)S(1)}, f32[64,128]{1,0:T(8,128)S(1)}, u32[]{:S(2)}, u32[]{:S(2)}) %collective-permute-start.10) | collective-permute-done | bytes 32800 | tf_op jit(solution)/shard_map/ppermute | solution.py:389
  40.6 1.4 %collective-permute-done.9.refs_4_.refs_1_ = f32[64,128]{1,0:T(8,128)S(1)} collective-permute-done((f32[64,128]{1,0:T(8,128)S(1)}, f32[64,128]{1,0:T(8,128)S(1)}, u32[]{:S(2)}, u32[]{:S(2)}) %collective-permute-start.9) | collective-permute-done | bytes 32800 | tf_op jit(solution)/shard_map/ppermute | solution.py:388
  42.1 0.0 collective-permute-done.7.refs_3_
  42.1 0.0 collective-permute-done.6.refs_2_
  42.1 0.0 collective-permute-done.5.refs_1_
  42.1 0.1 shard_map.88.after_ref.refs_2_
  42.2 0.6 collective-permute-start.14
  42.7 1.9 %collective-permute-start.13 = (bf16[2,256,1024]{2,1,0:T(8,128)(2,1)S(1)}, bf16[2,256,1024]{2,1,0:T(8,128)(2,1)S(1)}, u32[]{:S(2)}, u32[]{:S(2)}) collective-permute-start(bf16[2,256,1024]{2,1,0:T(8,128)(2,1)S(1)} %shard_map.88.after_ref.refs_2_), channel_id=1, source_target_pairs={{8,0},{57,1},{10,2},{59,3},{12,4},{61,5},{14,6},{63,7},{16,8},{1,9... | collective-permute-start | bytes 3145736 | tf_op jit(solution)/shard_map/ppermute | solution.py:43
  44.6 0.4 collective-permute-start.17
  45.0 2.3 %collective-permute-start.12 = (bf16[2,256,1024]{2,1,0:T(8,128)(2,1)S(1)}, bf16[2,256,1024]{2,1,0:T(8,128)(2,1)S(1)}, u32[]{:S(2)}, u32[]{:S(2)}) collective-permute-start(bf16[2,256,1024]{2,1,0:T(8,128)(2,1)S(1)} %shard_map.88.after_ref.refs_2_), channel_id=1, source_target_pairs={{2,0},{65,1},{4,2},{67,3},{6,4},{69,5},{0,6},{71,7},{10,8},{73,9},... | collective-permute-start | bytes 3145736 | tf_op jit(solution)/shard_map/ppermute | solution.py:43
  47.3 0.6 collective-permute-start.11
  48.6 0.2 collective-permute-done.11.refs_2_
  48.8 0.0 copy-done
  48.8 1.8 %shard_map.89 = (bf16[1024,4096]{1,0:T(8,128)(2,1)S(1)}, f32[8,128]{1,0:T(8,128)}) custom-call(s32[1,512]{1,0:T(1,128)S(1)} %bitcast.3, bf16[8,528,256]{2,1,0:T(8,128)(2,1)S(1)} %get-tuple-element.19.signs_ref, bf16[2,256,1024]{2,1,0:T(8,128)(2,1)S(1)} %shard_map.88.after_ref.refs_2_, f32[64,128]{1,0:T(8,128)S(1)} %shard_map.87.refs_0_, ...), custom_call_target="tpu_custom_call" | custom-call | flops 1000000 | bytes 1048576 | tf_op jit(solution)/shard_map/pallas_call | solution.py:213
  50.5 0.0 collective-permute-done.14.refs_3_
  50.5 2.5 %shard_map.90 = (f32[2,512,1024]{2,1,0:T(8,128)S(1)}, f32[8,128]{1,0:T(8,128)S(1)}) custom-call(s32[1]{0:T(128)S(6)} %copy.21.refs_0_, bf16[1024,4096]{1,0:T(8,128)(2,1)S(1)} %get-tuple-element.24.refs_1_, bf16[2,256,1024]{2,1,0:T(8,128)(2,1)S(1)} %shard_map.88.after_ref.refs_2_, bf16[2,256,1024]{2,1,0:T(8,128)(2,1)S(1)} %collective-permute-done.14.refs_3_), custom_call_target="tpu_custom_call" | custom-call | flops 1000000 | bytes 1048576 | tf_op jit(solution)/shard_map/pallas_call | solution.py:311
  53.1 4.8 %collective-permute-done.13.refs_0_ = bf16[2,256,1024]{2,1,0:T(8,128)(2,1)S(1)} collective-permute-done((bf16[2,256,1024]{2,1,0:T(8,128)(2,1)S(1)}, bf16[2,256,1024]{2,1,0:T(8,128)(2,1)S(1)}, u32[]{:S(2)}, u32[]{:S(2)}) %collective-permute-start.13) | collective-permute-done | bytes 1048608 | tf_op jit(solution)/shard_map/ppermute | solution.py:43
  57.9 1.7 %shard_map.92 = (f32[2,512,1024]{2,1,0:T(8,128)S(1)}, f32[8,128]{1,0:T(8,128)S(1)}) custom-call(s32[1]{0:T(128)S(6)} %copy.21.refs_0_, bf16[1024,4096]{1,0:T(8,128)(2,1)S(1)} %get-tuple-element.24.refs_1_, bf16[2,256,1024]{2,1,0:T(8,128)(2,1)S(1)} %shard_map.91.refs_2_, f32[2,512,1024]{2,1,0:T(8,128)S(1)} %get-tuple-element.26.refs_3_), custom_call_target="tpu_custom_call", output_to_operand_aliasing={{0}: (3, {})} | custom-call | flops 1000000 | bytes 1048576 | tf_op jit(solution)/shard_map/pallas_call | solution.py:311
  59.6 0.1 collective-permute-done.17.refs_0_
  59.8 0.9 %collective-permute-start.18 = (bf16[2,256,1024]{2,1,0:T(8,128)(2,1)S(1)}, bf16[2,256,1024]{2,1,0:T(8,128)(2,1)S(1)}, u32[]{:S(2)}, u32[]{:S(2)}) collective-permute-start(bf16[2,256,1024]{2,1,0:T(8,128)(2,1)S(1)} %shard_map.94.refs_3_), channel_id=1, source_target_pairs={{0,1},{1,0},{2,3},{3,2},{4,5},{5,4},{6,7},{7,6},{8,9},{9,8},{10,11... | collective-permute-start | bytes 3145736 | tf_op jit(solution)/shard_map/ppermute | solution.py:47
  60.7 0.0 collective-permute-start.16
  60.7 0.0 collective-permute-done.12.refs_0_
  60.7 0.5 collective-permute-start.15
  61.2 2.8 %shard_map.95 = (f32[2,512,1024]{2,1,0:T(8,128)S(1)}, f32[8,128]{1,0:T(8,128)}) custom-call(s32[1]{0:T(128)S(6)} %copy.21.refs_0_, bf16[1024,4096]{1,0:T(8,128)(2,1)S(1)} %get-tuple-element.24.refs_1_, bf16[2,256,1024]{2,1,0:T(8,128)(2,1)S(1)} %shard_map.93.refs_2_, bf16[2,256,1024]{2,1,0:T(8,128)(2,1)S(1)} %shard_map.94.refs_3_, ...), custom_call_target="tpu_custom_call", output_to_operand_aliasing={{0}: (4, {})} | custom-call | flops 1000000 | bytes 1048576 | tf_op jit(solution)/shard_map/pallas_call | solution.py:311
  64.0 0.0 collective-permute-done.18.refs_3_
  64.0 0.4 collective-permute-done.16.refs_2_
  64.5 2.8 %shard_map.96 = (f32[2,512,1024]{2,1,0:T(8,128)S(1)}, f32[8,128]{1,0:T(8,128)}) custom-call(s32[1]{0:T(128)S(6)} %copy.21.refs_0_, bf16[1024,4096]{1,0:T(8,128)(2,1)S(1)} %get-tuple-element.24.refs_1_, bf16[2,256,1024]{2,1,0:T(8,128)(2,1)S(1)} %collective-permute-done.16.refs_2_, ...), custom_call_target="tpu_custom_call", output_to_operand_aliasing={{0}: (4, {})} | custom-call | flops 1000000 | bytes 1048576 | tf_op jit(solution)/shard_map/pallas_call | solution.py:311
  67.3 0.0 collective-permute-done.15.refs_2_
  67.3 2.8 %shard_map.97 = f32[2,512,1024]{2,1,0:T(8,128)} custom-call(s32[1]{0:T(128)S(6)} %copy.21.refs_0_, bf16[1024,4096]{1,0:T(8,128)(2,1)S(1)} %get-tuple-element.24.refs_1_, bf16[2,256,1024]{2,1,0:T(8,128)(2,1)S(1)} %collective-permute-done.15.refs_2_, f32[2,512,1024]{2,1,0:T(8,128)S(1)} %get-tuple-element.30.refs_3_), custom_call_target="tpu_custom_call" | custom-call | flops 1000000 | bytes 1048576 | tf_op jit(solution)/shard_map/pallas_call | solution.py:311
  (6 shorter events, 0.0 us)
Async XLA Ops:
  0.0 18.9 %copy-start.1 = (s32[2,4,8,1,256]{4,3,2,1,0:T(1,128)S(1)}, s32[2,4,8,1,256]{4,3,2,1,0:T(1,128)}, u32[]{:S(2)}) copy-start(s32[2,4,8,1,256]{4,3,2,1,0:T(1,128)} %constant.2.clone.order_ref) | copy-start | bytes 196612
  0.0 4.3 %collective-permute-start = (f32[8,64]{1,0:T(8,128)}, f32[8,64]{1,0:T(8,128)S(1)}, u32[]{:S(2)}, u32[]{:S(2)}) collective-permute-start(f32[8,64]{1,0:T(8,128)} %bitcast.5), channel_id=1, source_target_pairs={{0,1},{1,0},{2,3},{3,2},{4,5},{5,4},{6,7},{7,6},{8,9},{9,8},{10,11... | collective-permute-start | bytes 6152 | tf_op jit(solution)/shard_map/ppermute | solution.py:47
  5.1 8.7 %collective-permute-start.1 = (bf16[2,8,1152]{2,1,0:T(8,128)(2,1)S(1)}, bf16[2,8,1152]{2,1,0:T(8,128)(2,1)S(1)}, u32[]{:S(2)}, u32[]{:S(2)}) collective-permute-start(bf16[2,8,1152]{2,1,0:T(8,128)(2,1)S(1)} %shard_map.84.refs_0_), channel_id=1, source_target_pairs={{32,0},{33,1},{34,2},{35,3},{36,4},{37,5},{38,6},{39,7},{40,8},{41... | collective-permute-start | bytes 110600 | tf_op jit(solution)/shard_map/ppermute | solution.py:43
  13.8 8.9 %collective-permute-start.4 = (bf16[2,16,1152]{2,1,0:T(8,128)(2,1)S(1)}, bf16[2,16,1152]{2,1,0:T(8,128)(2,1)S(1)}, u32[]{:S(2)}, u32[]{:S(2)}) collective-permute-start(bf16[2,16,1152]{2,1,0:T(8,128)(2,1)S(1)} %shard_map.85.refs_0_), channel_id=1, source_target_pairs={{60,0},{137,1},{62,2},{139,3},{56,4},{141,5},{58,6},{143,7},{4,8},... | collective-permute-start | bytes 221192 | tf_op jit(solution)/shard_map/ppermute | solution.py:43
  18.5 6.0 %collective-permute-start.3 = (bf16[2,16,1152]{2,1,0:T(8,128)(2,1)S(1)}, bf16[2,16,1152]{2,1,0:T(8,128)(2,1)S(1)}, u32[]{:S(2)}, u32[]{:S(2)}) collective-permute-start(bf16[2,16,1152]{2,1,0:T(8,128)(2,1)S(1)} %shard_map.85.refs_0_), channel_id=1, source_target_pairs={{16,0},{49,1},{18,2},{51,3},{20,4},{53,5},{22,6},{55,7},{24,8},{57... | collective-permute-start | bytes 221192 | tf_op jit(solution)/shard_map/ppermute | solution.py:43
  18.5 6.9 %collective-permute-start.2 = (bf16[2,16,1152]{2,1,0:T(8,128)(2,1)S(1)}, bf16[2,16,1152]{2,1,0:T(8,128)(2,1)S(1)}, u32[]{:S(2)}, u32[]{:S(2)}) collective-permute-start(bf16[2,16,1152]{2,1,0:T(8,128)(2,1)S(1)} %shard_map.85.refs_0_), channel_id=1, source_target_pairs={{12,0},{185,1},{14,2},{187,3},{8,4},{189,5},{10,6},{191,7},{20,8},... | collective-permute-start | bytes 221192 | tf_op jit(solution)/shard_map/ppermute | solution.py:43
  18.9 29.8 %copy-start = (s32[512]{0:T(512)S(1)}, s32[512]{0:T(512)}, u32[]{:S(2)}) copy-start(s32[512]{0:T(512)} %param.11) | copy-start | bytes 6148
  25.5 16.6 %collective-permute-start.7 = (bf16[2,64,1024]{2,1,0:T(8,128)(2,1)S(1)}, bf16[2,64,1024]{2,1,0:T(8,128)(2,1)S(1)}, u32[]{:S(2)}, u32[]{:S(2)}) collective-permute-start(bf16[2,64,1024]{2,1,0:T(8,128)(2,1)S(1)} %get-tuple-element.22.refs_0_), channel_id=1, source_target_pairs={{200,0},{63,1},{202,2},{57,3},{204,4},{59,5},{206,6},{61,7},{208,8... | collective-permute-start | bytes 786440 | tf_op jit(solution)/shard_map/ppermute | solution.py:43
  25.8 16.3 %collective-permute-start.6 = (bf16[2,64,1024]{2,1,0:T(8,128)(2,1)S(1)}, bf16[2,64,1024]{2,1,0:T(8,128)(2,1)S(1)}, u32[]{:S(2)}, u32[]{:S(2)}) collective-permute-start(bf16[2,64,1024]{2,1,0:T(8,128)(2,1)S(1)} %get-tuple-element.22.refs_0_), channel_id=1, source_target_pairs={{128,0},{5,1},{130,2},{7,3},{132,4},{1,5},{134,6},{3,7},{136,8},{1... | collective-permute-start | bytes 786440 | tf_op jit(solution)/shard_map/ppermute | solution.py:43
  28.3 13.8 %collective-permute-start.5 = (bf16[2,64,1024]{2,1,0:T(8,128)(2,1)S(1)}, bf16[2,64,1024]{2,1,0:T(8,128)(2,1)S(1)}, u32[]{:S(2)}, u32[]{:S(2)}) collective-permute-start(bf16[2,64,1024]{2,1,0:T(8,128)(2,1)S(1)} %get-tuple-element.22.refs_0_), channel_id=1, source_target_pairs={{72,0},{59,1},{74,2},{61,3},{76,4},{63,5},{78,6},{57,7},{80,8},{3,... | collective-permute-start | bytes 786440 | tf_op jit(solution)/shard_map/ppermute | solution.py:43
  31.1 5.2 %collective-permute-start.8 = (f32[64,128]{1,0:T(8,128)S(1)}, f32[64,128]{1,0:T(8,128)S(1)}, u32[]{:S(2)}, u32[]{:S(2)}) collective-permute-start(f32[64,128]{1,0:T(8,128)S(1)} %get-tuple-element.23.mine_ref), channel_id=1, source_target_pairs={{0,1},{1,0},{2,3},{3,2},{4,5},{5,4},{6,7},{7,6},{8,9},{9,8},{10,11... | collective-permute-start | bytes 98312 | tf_op jit(solution)/shard_map/ppermute | solution.py:47
  36.3 4.3 %collective-permute-start.10 = (f32[64,128]{1,0:T(8,128)S(1)}, f32[64,128]{1,0:T(8,128)S(1)}, u32[]{:S(2)}, u32[]{:S(2)}) collective-permute-start(f32[64,128]{1,0:T(8,128)S(1)} %shard_map.87.refs_0_), channel_id=1, source_target_pairs={{4,0},{5,1},{6,2},{7,3},{0,4},{1,5},{2,6},{3,7},{12,8},{13,9},{14,... | collective-permute-start | bytes 98312 | tf_op jit(solution)/shard_map/ppermute | solution.py:389
  38.0 4.1 %collective-permute-start.9 = (f32[64,128]{1,0:T(8,128)S(1)}, f32[64,128]{1,0:T(8,128)S(1)}, u32[]{:S(2)}, u32[]{:S(2)}) collective-permute-start(f32[64,128]{1,0:T(8,128)S(1)} %shard_map.87.refs_0_), channel_id=1, source_target_pairs={{2,0},{7,1},{4,2},{1,3},{6,4},{3,5},{0,6},{5,7},{10,8},{15,9},{12,... | collective-permute-start | bytes 98312 | tf_op jit(solution)/shard_map/ppermute | solution.py:388
  42.2 8.4 %collective-permute-start.14 = (bf16[2,256,1024]{2,1,0:T(8,128)(2,1)S(1)}, bf16[2,256,1024]{2,1,0:T(8,128)(2,1)S(1)}, u32[]{:S(2)}, u32[]{:S(2)}) collective-permute-start(bf16[2,256,1024]{2,1,0:T(8,128)(2,1)S(1)} %shard_map.88.after_ref.refs_2_), channel_id=1, source_target_pairs={{0,1},{1,0},{2,3},{3,2},{4,5},{5,4},{6,7},{7,6},{8,9},{9,8},{10,11... | collective-permute-start | bytes 3145736 | tf_op jit(solution)/shard_map/ppermute | solution.py:47
  42.7 15.2 %collective-permute-start.13 = (bf16[2,256,1024]{2,1,0:T(8,128)(2,1)S(1)}, bf16[2,256,1024]{2,1,0:T(8,128)(2,1)S(1)}, u32[]{:S(2)}, u32[]{:S(2)}) collective-permute-start(bf16[2,256,1024]{2,1,0:T(8,128)(2,1)S(1)} %shard_map.88.after_ref.refs_2_), channel_id=1, source_target_pairs={{8,0},{57,1},{10,2},{59,3},{12,4},{61,5},{14,6},{63,7},{16,8},{1,9... | collective-permute-start | bytes 3145736 | tf_op jit(solution)/shard_map/ppermute | solution.py:43
  44.6 15.2 %collective-permute-start.17 = (bf16[2,256,1024]{2,1,0:T(8,128)(2,1)S(1)}, bf16[2,256,1024]{2,1,0:T(8,128)(2,1)S(1)}, u32[]{:S(2)}, u32[]{:S(2)}) collective-permute-start(bf16[2,256,1024]{2,1,0:T(8,128)(2,1)S(1)} %shard_map.88.after_ref.refs_2_), channel_id=1, source_target_pairs={{6,0},{193,1},{0,2},{195,3},{2,4},{197,5},{4,6},{199,7},{14,8},{20... | collective-permute-start | bytes 3145736 | tf_op jit(solution)/shard_map/ppermute | solution.py:43
  45.0 15.7 %collective-permute-start.12 = (bf16[2,256,1024]{2,1,0:T(8,128)(2,1)S(1)}, bf16[2,256,1024]{2,1,0:T(8,128)(2,1)S(1)}, u32[]{:S(2)}, u32[]{:S(2)}) collective-permute-start(bf16[2,256,1024]{2,1,0:T(8,128)(2,1)S(1)} %shard_map.88.after_ref.refs_2_), channel_id=1, source_target_pairs={{2,0},{65,1},{4,2},{67,3},{6,4},{69,5},{0,6},{71,7},{10,8},{73,9},... | collective-permute-start | bytes 3145736 | tf_op jit(solution)/shard_map/ppermute | solution.py:43
  47.3 1.5 %collective-permute-start.11 = (f32[64,128]{1,0:T(8,128)S(1)}, f32[64,128]{1,0:T(8,128)S(1)}, u32[]{:S(2)}, u32[]{:S(2)}) collective-permute-start(f32[64,128]{1,0:T(8,128)S(1)} %collective-permute-done.9.refs_4_.refs_1_), channel_id=1, source_target_pairs={{0,1},{1,0},{2,3},{3,2},{4,5},{5,4},{6,7},{7,6},{8,9},{9,8},{10,11... | collective-permute-start | bytes 98312 | tf_op jit(solution)/shard_map/ppermute | solution.py:47
  59.8 4.3 %collective-permute-start.18 = (bf16[2,256,1024]{2,1,0:T(8,128)(2,1)S(1)}, bf16[2,256,1024]{2,1,0:T(8,128)(2,1)S(1)}, u32[]{:S(2)}, u32[]{:S(2)}) collective-permute-start(bf16[2,256,1024]{2,1,0:T(8,128)(2,1)S(1)} %shard_map.94.refs_3_), channel_id=1, source_target_pairs={{0,1},{1,0},{2,3},{3,2},{4,5},{5,4},{6,7},{7,6},{8,9},{9,8},{10,11... | collective-permute-start | bytes 3145736 | tf_op jit(solution)/shard_map/ppermute | solution.py:47
  60.7 3.8 %collective-permute-start.16 = (bf16[2,256,1024]{2,1,0:T(8,128)(2,1)S(1)}, bf16[2,256,1024]{2,1,0:T(8,128)(2,1)S(1)}, u32[]{:S(2)}, u32[]{:S(2)}) collective-permute-start(bf16[2,256,1024]{2,1,0:T(8,128)(2,1)S(1)} %shard_map.91.refs_2_), channel_id=1, source_target_pairs={{0,1},{1,0},{2,3},{3,2},{4,5},{5,4},{6,7},{7,6},{8,9},{9,8},{10,11... | collective-permute-start | bytes 3145736 | tf_op jit(solution)/shard_map/ppermute | solution.py:47
  60.7 6.6 %collective-permute-start.15 = (bf16[2,256,1024]{2,1,0:T(8,128)(2,1)S(1)}, bf16[2,256,1024]{2,1,0:T(8,128)(2,1)S(1)}, u32[]{:S(2)}, u32[]{:S(2)}) collective-permute-start(bf16[2,256,1024]{2,1,0:T(8,128)(2,1)S(1)} %shard_map.93.refs_2_), channel_id=1, source_target_pairs={{0,1},{1,0},{2,3},{3,2},{4,5},{5,4},{6,7},{7,6},{8,9},{9,8},{10,11... | collective-permute-start | bytes 3145736 | tf_op jit(solution)/shard_map/ppermute | solution.py:47

commit v6 on v5

--- a/solution.py
+++ b/solution.py
@@ -408,8 +408,7 @@
     got = [relay([block], token)[0] for block in got[:2]]
     swapped = [swap(block) for block in got]
     total, _ = product(live_rows, left, (512, 1024), got, total, False)
-    total, _ = product(live_rows, left, (3584, 3072), [their_third, swapped[1]], total, False)
-    return product(live_rows, left, (2560,), swapped[:1], total, True)
+    return product(live_rows, left, (3584, 3072, 2560), [their_third, swapped[1], swapped[0]], total, True)
 
 
 def solution(mesh):

time: 70.3 us -> 71 us (level)
  waiting for transfers between devices: 13.9 us -> 15.5 us
    ppermute x7, waiting for transfers between devices: 2.55 us -> 4.06 us  [swap(): return lax.ppermute(block, AXES, SWAP)]
    pallas_call x5 -> x4, Pallas kernels: 12.7 us -> 11.9 us  [product(): pl.pallas_call(functools.partial(product_kernel, first, last, starts, wid...]
  transfers between devices with their start and end apart: 19 -> 19, of which waited for: 10 -> 11; matrix products, arithmetic and copies ran while one was open for 0% -> 0% of each run, Pallas kernels for 27% -> 22%
where the time goes in v6:
time: 71 us; the launch traced here: 70.9 us
  starting transfers between devices  32.9 us (46%)
  Pallas kernels  21.8 us (31%)
  waiting for transfers between devices  15.5 us (22%)
  between operations  0.77 us (1%)
    ppermute x10, starting transfers between devices, fetch(): return [lax.ppermute(block, AXES, route(o)) for o in STAGES[stage]]  20.5 us
    pallas_call x4, Pallas kernels, product(): pl.pallas_call(functools.partial(product_kernel, first, last, starts, wid...  11.9 us
    ppermute x7, starting transfers between devices, swap(): return lax.ppermute(block, AXES, SWAP)  10.3 us
    ppermute x10, waiting for transfers between devices, fetch(): return [lax.ppermute(block, AXES, route(o)) for o in STAGES[stage]]  7.78 us
    ppermute x7, waiting for transfers between devices, swap(): return lax.ppermute(block, AXES, SWAP)  4.06 us
    pallas_call x1, Pallas kernels, arrange(): pl.pallas_call(arrange_kernel, in_specs=[VMEM] * 2, out_specs=[VMEM] * 2,...  3.7 us
    pallas_call x1, Pallas kernels, split_cores(): pl.pallas_call(split_kernel, in_specs=[ANY] * 3, out_specs=[VMEM] * 2, ou...  3.44 us
    ppermute x1, waiting for transfers between devices, gather_tables(): return [table, side, swap(side), lax.ppermute(table, AXES, along_x(2, 2))]  2.19 us
  transfers between devices with their start and end apart: 19, of which 11 were waited for; matrix products, arithmetic and copies ran while one was open for 0% of the time, Pallas kernels for 22%

profile of v6, /device:TPU:1, one launch (start us, length us, event | category | flops | bytes accessed | tf_op | source)
XLA Modules:
  0.0 70.9 jit_solution(1583440798338981003)
XLA Ops:
  0.0 0.0 copy-start.1
  0.0 3.2 %collective-permute-start = (f32[8,64]{1,0:T(8,128)}, f32[8,64]{1,0:T(8,128)S(1)}, u32[]{:S(2)}, u32[]{:S(2)}) collective-permute-start(f32[8,64]{1,0:T(8,128)} %bitcast.5), channel_id=1, source_target_pairs={{0,1},{1,0},{2,3},{3,2},{4,5},{5,4},{6,7},{7,6},{8,9},{9,8},{10,11... | collective-permute-start | bytes 6152 | tf_op jit(solution)/shard_map/ppermute | solution.py:47
  3.2 1.0 %collective-permute-done.theirs_ref = f32[8,64]{1,0:T(8,128)S(1)} collective-permute-done((f32[8,64]{1,0:T(8,128)}, f32[8,64]{1,0:T(8,128)S(1)}, u32[]{:S(2)}, u32[]{:S(2)}) %collective-permute-start) | collective-permute-done | bytes 2080 | tf_op jit(solution)/shard_map/ppermute | solution.py:47
  4.3 0.8 %shard_map.84.refs_0_ = bf16[2,8,1152]{2,1,0:T(8,128)(2,1)S(1)} custom-call(bf16[2,8,1024]{2,1,0:T(8,128)(2,1)} %coeffs_ref.1, f32[8,64]{1,0:T(8,128)} %bitcast.6, f32[8,64]{1,0:T(8,128)S(1)} %collective-permute-done.theirs_ref), custom_call_target="tpu_custom_call" | custom-call | bytes 65536 | tf_op jit(solution)/shard_map/pallas_call | solution.py:343
  5.1 5.2 %collective-permute-start.1 = (bf16[2,8,1152]{2,1,0:T(8,128)(2,1)S(1)}, bf16[2,8,1152]{2,1,0:T(8,128)(2,1)S(1)}, u32[]{:S(2)}, u32[]{:S(2)}) collective-permute-start(bf16[2,8,1152]{2,1,0:T(8,128)(2,1)S(1)} %shard_map.84.refs_0_), channel_id=1, source_target_pairs={{32,0},{33,1},{34,2},{35,3},{36,4},{37,5},{38,6},{39,7},{40,8},{41... | collective-permute-start | bytes 110600 | tf_op jit(solution)/shard_map/ppermute | solution.py:43
  10.3 3.4 %shard_map.82 = (bf16[2,528,1024]{2,1,0:T(8,128)(2,1)S(1)}, f32[8,128]{1,0:T(8,128)S(1)}) custom-call(s32[4,4]{1,0:T(4,128)} %coupling_ref.1, s32[1,2048]{1,0:T(1,128)} %bitcast.4, s32[512,2048]{1,0:T(8,128)} %excite_ref.1), custom_call_target="tpu_custom_call" | custom-call | flops 553648128 | bytes 7340032 | tf_op jit(solution)/shard_map/pallas_call | solution.py:119
  13.8 0.0 collective-permute-done.1.refs_1_
  13.8 4.7 %collective-permute-start.4 = (bf16[2,16,1152]{2,1,0:T(8,128)(2,1)S(1)}, bf16[2,16,1152]{2,1,0:T(8,128)(2,1)S(1)}, u32[]{:S(2)}, u32[]{:S(2)}) collective-permute-start(bf16[2,16,1152]{2,1,0:T(8,128)(2,1)S(1)} %shard_map.85.refs_0_), channel_id=1, source_target_pairs={{60,0},{137,1},{62,2},{139,3},{56,4},{141,5},{58,6},{143,7},{4,8},... | collective-permute-start | bytes 221192 | tf_op jit(solution)/shard_map/ppermute | solution.py:43
  18.5 0.0 collective-permute-start.3
  18.5 0.4 collective-permute-start.2
  18.9 0.0 copy-done.1
  18.9 0.0 copy-start
  18.9 3.7 %shard_map.83 = (bf16[8,528,256]{2,1,0:T(8,128)(2,1)S(1)}, f32[8,128]{1,0:T(8,128)S(1)}) custom-call(s32[2,4,8,1,256]{4,3,2,1,0:T(1,128)S(1)} %copy-done.1, bf16[2,528,1024]{2,1,0:T(8,128)(2,1)S(1)} %get-tuple-element.17.signs_ref), custom_call_target="tpu_custom_call" | custom-call | flops 2214592512 | bytes 4194304 | tf_op jit(solution)/shard_map/pallas_call | solution.py:152
  22.6 0.0 collective-permute-done.4.refs_3_
  22.7 1.9 %collective-permute-done.3.refs_2_ = bf16[2,16,1152]{2,1,0:T(8,128)(2,1)S(1)} collective-permute-done((bf16[2,16,1152]{2,1,0:T(8,128)(2,1)S(1)}, bf16[2,16,1152]{2,1,0:T(8,128)(2,1)S(1)}, u32[]{:S(2)}, u32[]{:S(2)}) %collective-permute-start.3) | collective-permute-done | bytes 73760 | tf_op jit(solution)/shard_map/ppermute | solution.py:43
  24.5 0.9 %collective-permute-done.2.refs_1_ = bf16[2,16,1152]{2,1,0:T(8,128)(2,1)S(1)} collective-permute-done((bf16[2,16,1152]{2,1,0:T(8,128)(2,1)S(1)}, bf16[2,16,1152]{2,1,0:T(8,128)(2,1)S(1)}, u32[]{:S(2)}, u32[]{:S(2)}) %collective-permute-start.2) | collective-permute-done | bytes 73760 | tf_op jit(solution)/shard_map/ppermute | solution.py:43
  25.5 0.3 collective-permute-start.7
  25.8 2.5 %collective-permute-start.6 = (bf16[2,64,1024]{2,1,0:T(8,128)(2,1)S(1)}, bf16[2,64,1024]{2,1,0:T(8,128)(2,1)S(1)}, u32[]{:S(2)}, u32[]{:S(2)}) collective-permute-start(bf16[2,64,1024]{2,1,0:T(8,128)(2,1)S(1)} %get-tuple-element.21.refs_0_), channel_id=1, source_target_pairs={{128,0},{5,1},{130,2},{7,3},{132,4},{1,5},{134,6},{3,7},{136,8},{1... | collective-permute-start | bytes 786440 | tf_op jit(solution)/shard_map/ppermute | solution.py:43
  28.3 2.8 %collective-permute-start.5 = (bf16[2,64,1024]{2,1,0:T(8,128)(2,1)S(1)}, bf16[2,64,1024]{2,1,0:T(8,128)(2,1)S(1)}, u32[]{:S(2)}, u32[]{:S(2)}) collective-permute-start(bf16[2,64,1024]{2,1,0:T(8,128)(2,1)S(1)} %get-tuple-element.21.refs_0_), channel_id=1, source_target_pairs={{72,0},{59,1},{74,2},{61,3},{76,4},{63,5},{78,6},{57,7},{80,8},{3,... | collective-permute-start | bytes 786440 | tf_op jit(solution)/shard_map/ppermute | solution.py:43
  31.1 4.4 %collective-permute-start.8 = (f32[64,128]{1,0:T(8,128)S(1)}, f32[64,128]{1,0:T(8,128)S(1)}, u32[]{:S(2)}, u32[]{:S(2)}) collective-permute-start(f32[64,128]{1,0:T(8,128)S(1)} %get-tuple-element.22.mine_ref), channel_id=1, source_target_pairs={{0,1},{1,0},{2,3},{3,2},{4,5},{5,4},{6,7},{7,6},{8,9},{9,8},{10,11... | collective-permute-start | bytes 98312 | tf_op jit(solution)/shard_map/ppermute | solution.py:47
  35.4 0.9 %collective-permute-done.8.theirs_ref = f32[64,128]{1,0:T(8,128)S(1)} collective-permute-done((f32[64,128]{1,0:T(8,128)S(1)}, f32[64,128]{1,0:T(8,128)S(1)}, u32[]{:S(2)}, u32[]{:S(2)}) %collective-permute-start.8) | collective-permute-done | bytes 32800 | tf_op jit(solution)/shard_map/ppermute | solution.py:47
  36.3 1.6 %collective-permute-start.10 = (f32[64,128]{1,0:T(8,128)S(1)}, f32[64,128]{1,0:T(8,128)S(1)}, u32[]{:S(2)}, u32[]{:S(2)}) collective-permute-start(f32[64,128]{1,0:T(8,128)S(1)} %shard_map.87.refs_0_), channel_id=1, source_target_pairs={{4,0},{5,1},{6,2},{7,3},{0,4},{1,5},{2,6},{3,7},{12,8},{13,9},{14,... | collective-permute-start | bytes 98312 | tf_op jit(solution)/shard_map/ppermute | solution.py:389
  38.0 0.5 collective-permute-start.9
  38.4 2.2 %collective-permute-done.10.refs_5_.refs_3_ = f32[64,128]{1,0:T(8,128)S(1)} collective-permute-done((f32[64,128]{1,0:T(8,128)S(1)}, f32[64,128]{1,0:T(8,128)S(1)}, u32[]{:S(2)}, u32[]{:S(2)}) %collective-permute-start.10) | collective-permute-done | bytes 32800 | tf_op jit(solution)/shard_map/ppermute | solution.py:389
  40.6 1.4 %collective-permute-done.9.refs_4_.refs_1_ = f32[64,128]{1,0:T(8,128)S(1)} collective-permute-done((f32[64,128]{1,0:T(8,128)S(1)}, f32[64,128]{1,0:T(8,128)S(1)}, u32[]{:S(2)}, u32[]{:S(2)}) %collective-permute-start.9) | collective-permute-done | bytes 32800 | tf_op jit(solution)/shard_map/ppermute | solution.py:388
  42.1 0.0 collective-permute-done.7.refs_3_
  42.1 0.0 collective-permute-done.6.refs_2_
  42.1 0.0 collective-permute-done.5.refs_1_
  42.1 0.1 shard_map.88.after_ref.refs_2_
  42.2 0.6 collective-permute-start.13
  42.7 1.9 %collective-permute-start.12 = (bf16[2,256,1024]{2,1,0:T(8,128)(2,1)S(1)}, bf16[2,256,1024]{2,1,0:T(8,128)(2,1)S(1)}, u32[]{:S(2)}, u32[]{:S(2)}) collective-permute-start(bf16[2,256,1024]{2,1,0:T(8,128)(2,1)S(1)} %shard_map.88.after_ref.refs_2_), channel_id=1, source_target_pairs={{8,0},{57,1},{10,2},{59,3},{12,4},{61,5},{14,6},{63,7},{16,8},{1,9... | collective-permute-start | bytes 3145736 | tf_op jit(solution)/shard_map/ppermute | solution.py:43
  44.6 0.4 collective-permute-start.15
  45.0 2.3 %collective-permute-start.17 = (bf16[2,256,1024]{2,1,0:T(8,128)(2,1)S(1)}, bf16[2,256,1024]{2,1,0:T(8,128)(2,1)S(1)}, u32[]{:S(2)}, u32[]{:S(2)}) collective-permute-start(bf16[2,256,1024]{2,1,0:T(8,128)(2,1)S(1)} %shard_map.88.after_ref.refs_2_), channel_id=1, source_target_pairs={{2,0},{65,1},{4,2},{67,3},{6,4},{69,5},{0,6},{71,7},{10,8},{73,9},... | collective-permute-start | bytes 3145736 | tf_op jit(solution)/shard_map/ppermute | solution.py:43
  47.3 0.6 collective-permute-start.11
  48.6 0.2 collective-permute-done.11.refs_2_
  48.8 0.0 copy-done
  48.8 1.8 %shard_map.89 = (bf16[1024,4096]{1,0:T(8,128)(2,1)S(1)}, f32[8,128]{1,0:T(8,128)}) custom-call(s32[1,512]{1,0:T(1,128)S(1)} %bitcast.3, bf16[8,528,256]{2,1,0:T(8,128)(2,1)S(1)} %get-tuple-element.18.signs_ref, bf16[2,256,1024]{2,1,0:T(8,128)(2,1)S(1)} %shard_map.88.after_ref.refs_2_, f32[64,128]{1,0:T(8,128)S(1)} %shard_map.87.refs_0_, ...), custom_call_target="tpu_custom_call" | custom-call | flops 1000000 | bytes 1048576 | tf_op jit(solution)/shard_map/pallas_call | solution.py:213
  50.5 0.0 collective-permute-done.13.refs_3_
  50.5 2.5 %shard_map.90 = (f32[2,512,1024]{2,1,0:T(8,128)S(1)}, f32[8,128]{1,0:T(8,128)S(1)}) custom-call(s32[1]{0:T(128)S(6)} %copy.19.refs_0_, bf16[1024,4096]{1,0:T(8,128)(2,1)S(1)} %get-tuple-element.23.refs_1_, bf16[2,256,1024]{2,1,0:T(8,128)(2,1)S(1)} %shard_map.88.after_ref.refs_2_, bf16[2,256,1024]{2,1,0:T(8,128)(2,1)S(1)} %collective-permute-done.13.refs_3_), custom_call_target="tpu_custom_call" | custom-call | flops 1000000 | bytes 1048576 | tf_op jit(solution)/shard_map/pallas_call | solution.py:311
  53.0 4.8 %collective-permute-done.12.refs_0_ = bf16[2,256,1024]{2,1,0:T(8,128)(2,1)S(1)} collective-permute-done((bf16[2,256,1024]{2,1,0:T(8,128)(2,1)S(1)}, bf16[2,256,1024]{2,1,0:T(8,128)(2,1)S(1)}, u32[]{:S(2)}, u32[]{:S(2)}) %collective-permute-start.12) | collective-permute-done | bytes 1048608 | tf_op jit(solution)/shard_map/ppermute | solution.py:43
  57.9 1.7 %shard_map.92 = (f32[2,512,1024]{2,1,0:T(8,128)S(1)}, f32[8,128]{1,0:T(8,128)S(1)}) custom-call(s32[1]{0:T(128)S(6)} %copy.19.refs_0_, bf16[1024,4096]{1,0:T(8,128)(2,1)S(1)} %get-tuple-element.23.refs_1_, bf16[2,256,1024]{2,1,0:T(8,128)(2,1)S(1)} %shard_map.91.refs_2_, f32[2,512,1024]{2,1,0:T(8,128)S(1)} %get-tuple-element.25.refs_3_), custom_call_target="tpu_custom_call", output_to_operand_aliasing={{0}: (3, {})} | custom-call | flops 1000000 | bytes 1048576 | tf_op jit(solution)/shard_map/pallas_call | solution.py:311
  59.6 0.1 collective-permute-done.15.refs_0_
  59.8 0.9 %collective-permute-start.16 = (bf16[2,256,1024]{2,1,0:T(8,128)(2,1)S(1)}, bf16[2,256,1024]{2,1,0:T(8,128)(2,1)S(1)}, u32[]{:S(2)}, u32[]{:S(2)}) collective-permute-start(bf16[2,256,1024]{2,1,0:T(8,128)(2,1)S(1)} %shard_map.93.refs_3_), channel_id=1, source_target_pairs={{0,1},{1,0},{2,3},{3,2},{4,5},{5,4},{6,7},{7,6},{8,9},{9,8},{10,11... | collective-permute-start | bytes 3145736 | tf_op jit(solution)/shard_map/ppermute | solution.py:47
  60.7 0.0 collective-permute-done.17.refs_0_
  60.7 0.1 collective-permute-start.18
  60.8 0.4 collective-permute-start.14
  61.2 2.8 %shard_map.95 = (f32[2,512,1024]{2,1,0:T(8,128)S(1)}, f32[8,128]{1,0:T(8,128)}) custom-call(s32[1]{0:T(128)S(6)} %copy.19.refs_0_, bf16[1024,4096]{1,0:T(8,128)(2,1)S(1)} %get-tuple-element.23.refs_1_, bf16[2,256,1024]{2,1,0:T(8,128)(2,1)S(1)} %shard_map.94.refs_2_, bf16[2,256,1024]{2,1,0:T(8,128)(2,1)S(1)} %shard_map.93.refs_3_, ...), custom_call_target="tpu_custom_call", output_to_operand_aliasing={{0}: (4, {})} | custom-call | flops 1000000 | bytes 1048576 | tf_op jit(solution)/shard_map/pallas_call | solution.py:311
  64.0 0.0 collective-permute-done.16.refs_3_
  64.0 0.5 collective-permute-done.18.refs_4_
  64.5 1.5 %collective-permute-done.14.refs_2_ = bf16[2,256,1024]{2,1,0:T(8,128)(2,1)S(1)} collective-permute-done((bf16[2,256,1024]{2,1,0:T(8,128)(2,1)S(1)}, bf16[2,256,1024]{2,1,0:T(8,128)(2,1)S(1)}, u32[]{:S(2)}, u32[]{:S(2)}) %collective-permute-start.14) | collective-permute-done | bytes 1048608 | tf_op jit(solution)/shard_map/ppermute | solution.py:47
  66.0 4.9 %shard_map.96 = f32[2,512,1024]{2,1,0:T(8,128)} custom-call(s32[1]{0:T(128)S(6)} %copy.19.refs_0_, bf16[1024,4096]{1,0:T(8,128)(2,1)S(1)} %get-tuple-element.23.refs_1_, bf16[2,256,1024]{2,1,0:T(8,128)(2,1)S(1)} %collective-permute-done.14.refs_2_, bf16[2,256,1024]{2,1,0:T(8,128)(2,1)S(1)} %collective-permute-done.16.refs_3_, ...), custom_call_target="tpu_custom_call" | custom-call | flops 1000000 | bytes 1048576 | tf_op jit(solution)/shard_map/pallas_call | solution.py:311
  (6 shorter events, 0.0 us)
Async XLA Ops:
  0.0 18.9 %copy-start.1 = (s32[2,4,8,1,256]{4,3,2,1,0:T(1,128)S(1)}, s32[2,4,8,1,256]{4,3,2,1,0:T(1,128)}, u32[]{:S(2)}) copy-start(s32[2,4,8,1,256]{4,3,2,1,0:T(1,128)} %constant.2.clone.order_ref) | copy-start | bytes 196612
  0.0 4.3 %collective-permute-start = (f32[8,64]{1,0:T(8,128)}, f32[8,64]{1,0:T(8,128)S(1)}, u32[]{:S(2)}, u32[]{:S(2)}) collective-permute-start(f32[8,64]{1,0:T(8,128)} %bitcast.5), channel_id=1, source_target_pairs={{0,1},{1,0},{2,3},{3,2},{4,5},{5,4},{6,7},{7,6},{8,9},{9,8},{10,11... | collective-permute-start | bytes 6152 | tf_op jit(solution)/shard_map/ppermute | solution.py:47
  5.1 8.7 %collective-permute-start.1 = (bf16[2,8,1152]{2,1,0:T(8,128)(2,1)S(1)}, bf16[2,8,1152]{2,1,0:T(8,128)(2,1)S(1)}, u32[]{:S(2)}, u32[]{:S(2)}) collective-permute-start(bf16[2,8,1152]{2,1,0:T(8,128)(2,1)S(1)} %shard_map.84.refs_0_), channel_id=1, source_target_pairs={{32,0},{33,1},{34,2},{35,3},{36,4},{37,5},{38,6},{39,7},{40,8},{41... | collective-permute-start | bytes 110600 | tf_op jit(solution)/shard_map/ppermute | solution.py:43
  13.8 8.9 %collective-permute-start.4 = (bf16[2,16,1152]{2,1,0:T(8,128)(2,1)S(1)}, bf16[2,16,1152]{2,1,0:T(8,128)(2,1)S(1)}, u32[]{:S(2)}, u32[]{:S(2)}) collective-permute-start(bf16[2,16,1152]{2,1,0:T(8,128)(2,1)S(1)} %shard_map.85.refs_0_), channel_id=1, source_target_pairs={{60,0},{137,1},{62,2},{139,3},{56,4},{141,5},{58,6},{143,7},{4,8},... | collective-permute-start | bytes 221192 | tf_op jit(solution)/shard_map/ppermute | solution.py:43
  18.5 6.0 %collective-permute-start.3 = (bf16[2,16,1152]{2,1,0:T(8,128)(2,1)S(1)}, bf16[2,16,1152]{2,1,0:T(8,128)(2,1)S(1)}, u32[]{:S(2)}, u32[]{:S(2)}) collective-permute-start(bf16[2,16,1152]{2,1,0:T(8,128)(2,1)S(1)} %shard_map.85.refs_0_), channel_id=1, source_target_pairs={{16,0},{49,1},{18,2},{51,3},{20,4},{53,5},{22,6},{55,7},{24,8},{57... | collective-permute-start | bytes 221192 | tf_op jit(solution)/shard_map/ppermute | solution.py:43
  18.5 6.9 %collective-permute-start.2 = (bf16[2,16,1152]{2,1,0:T(8,128)(2,1)S(1)}, bf16[2,16,1152]{2,1,0:T(8,128)(2,1)S(1)}, u32[]{:S(2)}, u32[]{:S(2)}) collective-permute-start(bf16[2,16,1152]{2,1,0:T(8,128)(2,1)S(1)} %shard_map.85.refs_0_), channel_id=1, source_target_pairs={{12,0},{185,1},{14,2},{187,3},{8,4},{189,5},{10,6},{191,7},{20,8},... | collective-permute-start | bytes 221192 | tf_op jit(solution)/shard_map/ppermute | solution.py:43
  18.9 29.8 %copy-start = (s32[512]{0:T(512)S(1)}, s32[512]{0:T(512)}, u32[]{:S(2)}) copy-start(s32[512]{0:T(512)} %param.11) | copy-start | bytes 6148
  25.5 16.6 %collective-permute-start.7 = (bf16[2,64,1024]{2,1,0:T(8,128)(2,1)S(1)}, bf16[2,64,1024]{2,1,0:T(8,128)(2,1)S(1)}, u32[]{:S(2)}, u32[]{:S(2)}) collective-permute-start(bf16[2,64,1024]{2,1,0:T(8,128)(2,1)S(1)} %get-tuple-element.21.refs_0_), channel_id=1, source_target_pairs={{200,0},{63,1},{202,2},{57,3},{204,4},{59,5},{206,6},{61,7},{208,8... | collective-permute-start | bytes 786440 | tf_op jit(solution)/shard_map/ppermute | solution.py:43
  25.8 16.3 %collective-permute-start.6 = (bf16[2,64,1024]{2,1,0:T(8,128)(2,1)S(1)}, bf16[2,64,1024]{2,1,0:T(8,128)(2,1)S(1)}, u32[]{:S(2)}, u32[]{:S(2)}) collective-permute-start(bf16[2,64,1024]{2,1,0:T(8,128)(2,1)S(1)} %get-tuple-element.21.refs_0_), channel_id=1, source_target_pairs={{128,0},{5,1},{130,2},{7,3},{132,4},{1,5},{134,6},{3,7},{136,8},{1... | collective-permute-start | bytes 786440 | tf_op jit(solution)/shard_map/ppermute | solution.py:43
  28.3 13.8 %collective-permute-start.5 = (bf16[2,64,1024]{2,1,0:T(8,128)(2,1)S(1)}, bf16[2,64,1024]{2,1,0:T(8,128)(2,1)S(1)}, u32[]{:S(2)}, u32[]{:S(2)}) collective-permute-start(bf16[2,64,1024]{2,1,0:T(8,128)(2,1)S(1)} %get-tuple-element.21.refs_0_), channel_id=1, source_target_pairs={{72,0},{59,1},{74,2},{61,3},{76,4},{63,5},{78,6},{57,7},{80,8},{3,... | collective-permute-start | bytes 786440 | tf_op jit(solution)/shard_map/ppermute | solution.py:43
  31.1 5.2 %collective-permute-start.8 = (f32[64,128]{1,0:T(8,128)S(1)}, f32[64,128]{1,0:T(8,128)S(1)}, u32[]{:S(2)}, u32[]{:S(2)}) collective-permute-start(f32[64,128]{1,0:T(8,128)S(1)} %get-tuple-element.22.mine_ref), channel_id=1, source_target_pairs={{0,1},{1,0},{2,3},{3,2},{4,5},{5,4},{6,7},{7,6},{8,9},{9,8},{10,11... | collective-permute-start | bytes 98312 | tf_op jit(solution)/shard_map/ppermute | solution.py:47
  36.3 4.3 %collective-permute-start.10 = (f32[64,128]{1,0:T(8,128)S(1)}, f32[64,128]{1,0:T(8,128)S(1)}, u32[]{:S(2)}, u32[]{:S(2)}) collective-permute-start(f32[64,128]{1,0:T(8,128)S(1)} %shard_map.87.refs_0_), channel_id=1, source_target_pairs={{4,0},{5,1},{6,2},{7,3},{0,4},{1,5},{2,6},{3,7},{12,8},{13,9},{14,... | collective-permute-start | bytes 98312 | tf_op jit(solution)/shard_map/ppermute | solution.py:389
  38.0 4.1 %collective-permute-start.9 = (f32[64,128]{1,0:T(8,128)S(1)}, f32[64,128]{1,0:T(8,128)S(1)}, u32[]{:S(2)}, u32[]{:S(2)}) collective-permute-start(f32[64,128]{1,0:T(8,128)S(1)} %shard_map.87.refs_0_), channel_id=1, source_target_pairs={{2,0},{7,1},{4,2},{1,3},{6,4},{3,5},{0,6},{5,7},{10,8},{15,9},{12,... | collective-permute-start | bytes 98312 | tf_op jit(solution)/shard_map/ppermute | solution.py:388
  42.2 8.4 %collective-permute-start.13 = (bf16[2,256,1024]{2,1,0:T(8,128)(2,1)S(1)}, bf16[2,256,1024]{2,1,0:T(8,128)(2,1)S(1)}, u32[]{:S(2)}, u32[]{:S(2)}) collective-permute-start(bf16[2,256,1024]{2,1,0:T(8,128)(2,1)S(1)} %shard_map.88.after_ref.refs_2_), channel_id=1, source_target_pairs={{0,1},{1,0},{2,3},{3,2},{4,5},{5,4},{6,7},{7,6},{8,9},{9,8},{10,11... | collective-permute-start | bytes 3145736 | tf_op jit(solution)/shard_map/ppermute | solution.py:47
  42.7 15.2 %collective-permute-start.12 = (bf16[2,256,1024]{2,1,0:T(8,128)(2,1)S(1)}, bf16[2,256,1024]{2,1,0:T(8,128)(2,1)S(1)}, u32[]{:S(2)}, u32[]{:S(2)}) collective-permute-start(bf16[2,256,1024]{2,1,0:T(8,128)(2,1)S(1)} %shard_map.88.after_ref.refs_2_), channel_id=1, source_target_pairs={{8,0},{57,1},{10,2},{59,3},{12,4},{61,5},{14,6},{63,7},{16,8},{1,9... | collective-permute-start | bytes 3145736 | tf_op jit(solution)/shard_map/ppermute | solution.py:43
  44.6 15.2 %collective-permute-start.15 = (bf16[2,256,1024]{2,1,0:T(8,128)(2,1)S(1)}, bf16[2,256,1024]{2,1,0:T(8,128)(2,1)S(1)}, u32[]{:S(2)}, u32[]{:S(2)}) collective-permute-start(bf16[2,256,1024]{2,1,0:T(8,128)(2,1)S(1)} %shard_map.88.after_ref.refs_2_), channel_id=1, source_target_pairs={{6,0},{193,1},{0,2},{195,3},{2,4},{197,5},{4,6},{199,7},{14,8},{20... | collective-permute-start | bytes 3145736 | tf_op jit(solution)/shard_map/ppermute | solution.py:43
  45.0 15.7 %collective-permute-start.17 = (bf16[2,256,1024]{2,1,0:T(8,128)(2,1)S(1)}, bf16[2,256,1024]{2,1,0:T(8,128)(2,1)S(1)}, u32[]{:S(2)}, u32[]{:S(2)}) collective-permute-start(bf16[2,256,1024]{2,1,0:T(8,128)(2,1)S(1)} %shard_map.88.after_ref.refs_2_), channel_id=1, source_target_pairs={{2,0},{65,1},{4,2},{67,3},{6,4},{69,5},{0,6},{71,7},{10,8},{73,9},... | collective-permute-start | bytes 3145736 | tf_op jit(solution)/shard_map/ppermute | solution.py:43
  47.3 1.5 %collective-permute-start.11 = (f32[64,128]{1,0:T(8,128)S(1)}, f32[64,128]{1,0:T(8,128)S(1)}, u32[]{:S(2)}, u32[]{:S(2)}) collective-permute-start(f32[64,128]{1,0:T(8,128)S(1)} %collective-permute-done.9.refs_4_.refs_1_), channel_id=1, source_target_pairs={{0,1},{1,0},{2,3},{3,2},{4,5},{5,4},{6,7},{7,6},{8,9},{9,8},{10,11... | collective-permute-start | bytes 98312 | tf_op jit(solution)/shard_map/ppermute | solution.py:47
  59.8 4.2 %collective-permute-start.16 = (bf16[2,256,1024]{2,1,0:T(8,128)(2,1)S(1)}, bf16[2,256,1024]{2,1,0:T(8,128)(2,1)S(1)}, u32[]{:S(2)}, u32[]{:S(2)}) collective-permute-start(bf16[2,256,1024]{2,1,0:T(8,128)(2,1)S(1)} %shard_map.93.refs_3_), channel_id=1, source_target_pairs={{0,1},{1,0},{2,3},{3,2},{4,5},{5,4},{6,7},{7,6},{8,9},{9,8},{10,11... | collective-permute-start | bytes 3145736 | tf_op jit(solution)/shard_map/ppermute | solution.py:47
  60.7 3.8 %collective-permute-start.18 = (bf16[2,256,1024]{2,1,0:T(8,128)(2,1)S(1)}, bf16[2,256,1024]{2,1,0:T(8,128)(2,1)S(1)}, u32[]{:S(2)}, u32[]{:S(2)}) collective-permute-start(bf16[2,256,1024]{2,1,0:T(8,128)(2,1)S(1)} %shard_map.94.refs_2_), channel_id=1, source_target_pairs={{0,1},{1,0},{2,3},{3,2},{4,5},{5,4},{6,7},{7,6},{8,9},{9,8},{10,11... | collective-permute-start | bytes 3145736 | tf_op jit(solution)/shard_map/ppermute | solution.py:47
  60.8 5.2 %collective-permute-start.14 = (bf16[2,256,1024]{2,1,0:T(8,128)(2,1)S(1)}, bf16[2,256,1024]{2,1,0:T(8,128)(2,1)S(1)}, u32[]{:S(2)}, u32[]{:S(2)}) collective-permute-start(bf16[2,256,1024]{2,1,0:T(8,128)(2,1)S(1)} %shard_map.91.refs_2_), channel_id=1, source_target_pairs={{0,1},{1,0},{2,3},{3,2},{4,5},{5,4},{6,7},{7,6},{8,9},{9,8},{10,11... | collective-permute-start | bytes 3145736 | tf_op jit(solution)/shard_map/ppermute | solution.py:47
